TPU v7x, 32 devices: a whole 2x2x4 slice. The times are simulated.
32 devices in a mesh: groups: 2 (over y), gz: 8 (over z, x), tile: 2 (over core).
Axes of the slice: x: 2, y: 2, z: 4, core: 2. Of those that a mesh axis runs over, the one named last changes fastest.
Arguments:
- volume: bfloat16 [16, 32, 12288], P(('groups', 'gz'), 'tile'), parts along dimension 0, may hold values from -6 to 6
- norm_gains: float32 [4, 96], replicated, may hold values from 0.1 to 1.9
- qkv_weight: bfloat16 [2, 96, 288], replicated, may hold values from -0.625 to 0.625
- out_weight: bfloat16 [2, 96, 96], replicated, may hold values from -0.625 to 0.625
- up_weight: bfloat16 [2, 96, 384], replicated, may hold values from -0.625 to 0.625
- down_weight: bfloat16 [2, 384, 96], replicated, may hold values from -0.3125 to 0.3125
- window_bias: float32 [3, 64, 64], replicated, may hold values from -4 to 4
Outputs:
- result: bfloat16 [16, 32, 12288], P(('groups', 'gz'), 'tile'), parts along dimension 0
There are 2 independent parts, one for each index of `groups`. A program takes and returns all parts, laid end to end along the dimension named above; an argument that names none is the same for every part. Nothing has to cross between parts.
All inputs are finite; a program needn't handle non-finite values.
Results may differ from a plain program's by a relative error of at most 0.02.
Values may be sent and summed in bfloat16 or wider, within the bound.
No kernel may reach another device: no remote copies, remote signals or barrier semaphores. Data moves between devices by JAX's collectives and lax.ppermute only.
A program may use at most 64 MiB of HBM per device.

v0:
```python
import jax
import jax.numpy as jnp
from jax import lax
from jax.sharding import PartitionSpec as P

epsilon = 1e-05


def shifted(array, axis, by):
    peers = lax.axis_size(axis)
    return lax.ppermute(array, axis, [(i, (i + by) % peers) for i in range(peers)])


def layer_norm(tokens, gain):
    values = tokens.astype(jnp.float32)
    average = jnp.mean(values, -1, keepdims=True)
    centered = values - average
    variance = jnp.mean(centered * centered, -1, keepdims=True)
    return (centered * lax.rsqrt(variance + epsilon) * gain).astype(jnp.bfloat16)


def feed_forward(tokens, gain, up_matrix, down_matrix):
    normed = layer_norm(tokens, gain)
    hidden = jax.nn.gelu(jnp.dot(normed, up_matrix, preferred_element_type=jnp.float32)).astype(
        jnp.bfloat16
    )
    total = tokens.astype(jnp.float32) + jnp.dot(
        hidden, down_matrix, preferred_element_type=jnp.float32
    )
    return total.astype(jnp.bfloat16)


def edge_label(index, extent):
    return jnp.where(index < 4, 2, jnp.where(index >= extent - 4, 1, 0)).astype(jnp.int32)


def head_masks(heads, channels):
    owner = jnp.arange(channels, dtype=jnp.int32) // (channels // heads)
    return (owner[None, :] == jnp.arange(heads, dtype=jnp.int32)[:, None]).astype(jnp.bfloat16)


def window_attention(
    row_block, first_row, height, channels, norm_gains, qkv_weight, out_weight, window_bias
):
    count = row_block.shape[0]
    columns = row_block.shape[1] // channels
    heads = window_bias.shape[0]
    head_size = channels // heads
    masks = head_masks(heads, channels)
    rolled = jnp.roll(row_block, -4 * channels, axis=1)
    windowed = rolled.reshape(count // 8, 8, columns // 8, 8 * channels).transpose(0, 2, 1, 3)
    normed = layer_norm(windowed.reshape(-1, channels), norm_gains[0])
    packed = jnp.dot(normed, qkv_weight[0], preferred_element_type=jnp.float32).astype(jnp.bfloat16)
    packed = packed.reshape(-1, 64, 3 * channels)
    queries = packed[:, :, :channels]
    keys = packed[:, :, channels : 2 * channels]
    values = packed[:, :, 2 * channels :]
    initial_rows = jnp.mod(first_row + jnp.arange(count, dtype=jnp.int32), height)
    initial_columns = jnp.mod(jnp.arange(columns, dtype=jnp.int32) + 4, columns)
    labels = (
        edge_label(initial_rows, height)[:, None] * 3
        + edge_label(initial_columns, columns)[None, :]
    )
    window_labels = (
        labels.reshape(count // 8, 8, columns // 8, 8).transpose(0, 2, 1, 3).reshape(-1, 64)
    )
    allowed = window_labels[:, :, None] == window_labels[:, None, :]
    head_queries = queries[:, None] * masks[None, :, None, :]
    scores = jnp.einsum("nhqc,nkc->nhqk", head_queries, keys, preferred_element_type=jnp.float32)
    scores = scores * head_size ** (-0.5) + window_bias[None]
    scores = jnp.where(allowed[:, None], scores, -jnp.inf)
    weights = jax.nn.softmax(scores, axis=-1).astype(jnp.bfloat16)
    head_values = values[:, None] * masks[None, :, None, :]
    attended = jnp.einsum(
        "nhqk,nhkc->nqc", weights, head_values, preferred_element_type=jnp.float32
    ).astype(jnp.bfloat16)
    lateral = jnp.dot(
        attended.reshape(-1, channels), out_weight[0], preferred_element_type=jnp.float32
    ).astype(jnp.bfloat16)
    lateral = lateral.reshape(count // 8, columns // 8, 8, 8 * channels).transpose(0, 2, 1, 3)
    return jnp.roll(lateral.reshape(count, columns * channels), 4 * channels, axis=1)


def axial_block(pencils, norm_gains, qkv_weight, out_weight, up_weight, down_weight, heads):
    planes, count, channels = pencils.shape
    head_size = channels // heads
    masks = head_masks(heads, channels)
    flat = jnp.transpose(pencils, (1, 0, 2)).reshape(-1, channels)
    normed = layer_norm(flat, norm_gains[2])
    packed = jnp.dot(normed, qkv_weight[1], preferred_element_type=jnp.float32).astype(jnp.bfloat16)
    packed = packed.reshape(count, planes, 3 * channels)
    queries = packed[:, :, :channels]
    keys = packed[:, :, channels : 2 * channels]
    values = packed[:, :, 2 * channels :]
    head_queries = queries[:, None] * masks[None, :, None, :]
    scores = jnp.einsum("phzc,pyc->phzy", head_queries, keys, preferred_element_type=jnp.float32)
    weights = jax.nn.softmax(scores * head_size ** (-0.5), axis=-1).astype(jnp.bfloat16)
    head_values = values[:, None] * masks[None, :, None, :]
    attended = jnp.einsum(
        "phzy,phyc->pzc", weights, head_values, preferred_element_type=jnp.float32
    ).astype(jnp.bfloat16)
    projected = jnp.dot(
        attended.reshape(-1, channels), out_weight[1], preferred_element_type=jnp.float32
    ).astype(jnp.bfloat16)
    after = (flat.astype(jnp.float32) + projected.astype(jnp.float32)).astype(jnp.bfloat16)
    mixed = feed_forward(after, norm_gains[3], up_weight[1], down_weight[1]).reshape(
        count, planes, channels
    )
    return jnp.transpose(mixed, (1, 0, 2))


def body(volume, norm_gains, qkv_weight, out_weight, up_weight, down_weight, window_bias):
    rows_here = volume.shape[1]
    row_width = volume.shape[2]
    channels = norm_gains.shape[1]
    heads = window_bias.shape[0]
    height = rows_here * lax.axis_size("tile")
    tile_start = lax.axis_index("tile") * rows_here
    plane = volume.reshape(rows_here, row_width)
    next_rows = shifted(plane[:4], "tile", -1)
    extended = jnp.concatenate([plane[4:], next_rows], 0)
    attended = window_attention(
        extended, tile_start + 4, height, channels, norm_gains, qkv_weight, out_weight, window_bias
    )
    tail_rows = shifted(attended[-4:], "tile", 1)
    lateral = jnp.concatenate([tail_rows, attended[:-4]], 0)
    middle = (
        (plane.astype(jnp.float32) + lateral.astype(jnp.float32))
        .astype(jnp.bfloat16)
        .reshape(-1, channels)
    )
    planes = lax.axis_size("gz")
    middle = feed_forward(middle, norm_gains[1], up_weight[0], down_weight[0])
    grouped = middle.reshape(planes, -1, channels)
    pencils = lax.all_to_all(grouped, "gz", split_axis=0, concat_axis=0, tiled=True)
    returned = lax.all_to_all(
        axial_block(pencils, norm_gains, qkv_weight, out_weight, up_weight, down_weight, heads),
        "gz",
        split_axis=0,
        concat_axis=0,
        tiled=True,
    )
    return returned.reshape(1, rows_here, row_width)


def solution(mesh):
    placed = (P(("groups", "gz"), "tile", None), P(), P(), P(), P(), P(), P())
    return jax.shard_map(
        body,
        mesh=mesh,
        in_specs=placed,
        out_specs=P(("groups", "gz"), "tile", None),
        check_vma=False,
    )
```

profile of v0, /device:TPU:0, one launch (start us, length us, event | category | flops | bytes accessed | tf_op | source)
XLA Modules:
  0.0 90.0 jit_solution(2044041924347802812)
XLA Ops:
  0.0 1.0 %slice_bitcast_fusion.9 = bf16[4,12288]{1,0:T(4,128)(2,1)S(1)} fusion(bf16[1,16,12288]{2,1,0:T(8,128)(2,1)} %param.7), kind=kLoop, calls=%fused_computation.99 | loop fusion | bytes 196608 | tf_op jit(solution)/shard_map/slice | solution.py:120
  1.0 0.5 collective-permute-start
  1.5 1.1 %slice_bitcast_fusion.4 = bf16[12,12288]{1,0:T(8,128)(2,1)S(1)} fusion(bf16[1,16,12288]{2,1,0:T(8,128)(2,1)} %param.7), kind=kLoop, calls=%fused_computation.96 | loop fusion | bytes 589824 | tf_op jit(solution)/shard_map/slice | solution.py:121
  2.6 1.4 %slice_bitcast_fusion.10 = (f32[96]{0:T(128)}, f32[96]{0:T(128)S(1)}, f32[96]{0:T(128)S(1)}, f32[96]{0:T(128)}) fusion(f32[4,96]{1,0:T(4,128)} %param.8), kind=kLoop, calls=%fused_computation.141 | loop fusion | bytes 3072 | tf_op jit(solution)/shard_map/mul | solution.py:19
  4.1 0.1 add.153
  4.3 1.1 %broadcast_compare_fusion = pred[32,64,64]{1,2,0:T(8,128)(4,1)} fusion(s32[32,64]{1,0:T(8,128)S(1)} %copy.33), kind=kLoop, calls=%fused_computation.85 | loop fusion | flops 131072 | bytes 139264 | tf_op jit(solution)/shard_map/eq | solution.py:67
  5.3 1.4 %reshape.314 = f32[2048,96]{1,0:T(8,128)S(1)} reshape(bf16[1,16,12288]{2,1,0:T(8,128)(2,1)} %param.7) | data formatting | bytes 1179648 | tf_op jit(solution)/shard_map/convert_element_type | solution.py:128
  6.9 1.6 %copy.36 = f32[3,64,64]{1,2,0:T(8,128)} copy(f32[3,64,64]{2,1,0:T(8,128)} %param.13) | data formatting | bytes 98304 | tf_op args[6]
  8.5 0.3 copy.39
  8.8 0.7 mul.230
  9.5 0.1 fusion.79
  9.7 0.5 reshape.315
  10.2 0.3 reduce_sum.90
  10.6 0.6 multiply_reduce_fusion.1
  11.2 0.1 div.61
  11.3 0.1 rsqrt.39
  11.4 0.3 mul.209
  11.8 0.3 mul.210
  12.1 0.3 sub.82
  12.5 1.2 %sub.83 = f32[2,16,8,768]{3,2,1,0:T(8,128)} reshape(f32[2,16,8,8,96]{4,3,2,1,0:T(8,128)S(1)} %sub.82) | data formatting | bytes 1572864 | tf_op jit(solution)/shard_map/sub | solution.py:17
  13.7 1.3 %multiply_convert_fusion.3 = bf16[2,16,8,768]{3,2,1,0:T(8,128)(2,1)S(1)} fusion(f32[2,16,8,768]{3,2,1,0:T(8,128)S(1)} %mul.210, f32[2,16,8,768]{3,2,1,0:T(8,128)} %sub.83, f32[768]{0:T(1024)S(1)} %mul.214, bf16[2,8,16,768]{3,1,2,0:T(8,128)(2,1)S(1)} %bitcast.137), kind=kLoop, calls=%fused_computation.80 | loop fusion | flops 983040 | bytes 2362368 | tf_op jit(solution)/shard_map/convert_element_type | solution.py:19
  14.9 0.6 convert_element_type.194
  15.5 1.4 %convolution_convert_fusion.1 = bf16[2048,288]{0,1:T(8,128)(2,1)S(1)} fusion(bf16[2048,96]{1,0:T(8,128)(2,1)S(1)} %convert_element_type.194, bf16[2,96,288]{2,1,0:T(8,128)(2,1)} %param.9), kind=kOutput, calls=%fused_computation.28 | convolution fusion | flops 113836032 | bytes 1646592 | tf_op jit(solution)/shard_map/dot_general | solution.py:53
  16.9 1.0 %copy.35 = bf16[2048,288]{1,0:T(8,128)(2,1)S(1)} copy(bf16[2048,288]{0,1:T(8,128)(2,1)S(1)} %convolution_convert_fusion.1) | data formatting | bytes 2359296 | tf_op jit(solution)/shard_map/convert_element_type | solution.py:53
  17.9 0.3 fusion.123
  18.2 4.3 %fusion.124 = (f32[32,3,64]{2,1,0:T(4,128)S(1)}, f32[32,3,64,64]{2,3,1,0:T(8,128)}) fusion(f32[3,64,64]{1,2,0:T(8,128)} %copy.36, pred[32,64,64]{1,2,0:T(8,128)(4,1)} %broadcast_compare_fusion, bf16[32,64,288]{2,1,0:T(8,128)(2,1)S(1)} %bitcast.134, bf16[3,96]{1,0:T(4,128)(2,1)S(1)} %fusion.106, bf16[32,64,96]{2,1,0:T(8,128)(2,1)S(1)} %get-tuple-element.10), kind=kOutput, calls=%fused_computation.160 | convolution fusion | flops 78053440 | bytes 2827264 | tf_op jit(solution)/shard_map/sub | solution.py:72
  22.6 2.6 %fusion.47 = bf16[32,64,96]{2,1,0:T(8,128)(2,1)S(1)} fusion(f32[32,3,64,64]{2,3,1,0:T(8,128)} %get-tuple-element.20, f32[32,3,64]{2,1,0:T(4,128)S(1)} %get-tuple-element.19, bf16[32,64,96]{2,1,0:T(8,128)(2,1)S(1)} %get-tuple-element.9, bf16[3,96]{1,0:T(4,128)(2,1)S(1)} %fusion.106), kind=kOutput, calls=%fused_computation.55 | convolution fusion | flops 77070336 | bytes 2384448 | tf_op jit(solution)/shard_map/nhqk,nhkc->nqc/dot_general | solution.py:74
  25.1 0.3 convolution_convert_fusion.3
  25.5 0.3 copy.38
  25.7 0.4 reshape.307
  26.3 0.1 collective-permute-start.1
  26.4 0.8 fusion.121
  27.2 0.4 collective-permute-done.1
  27.6 0.1 maximum_convert_fusion
  27.8 0.4 reshape.316
  28.2 0.3 copy.40
  28.7 0.6 fusion.120
  29.3 0.1 fusion.59
  29.4 0.3 mul.225
  29.7 0.6 mul.226
  30.4 1.0 %sub.90 = f32[16,128,96]{2,1,0:T(8,128)S(1)} broadcast(f32[16,128]{1,0:T(8,128)} %get-tuple-element.13), dimensions={0,1} | broadcast | bytes 794624 | tf_op jit(solution)/shard_map/sub | solution.py:17
  31.4 0.6 sub.91
  32.0 1.3 %multiply_convert_fusion.2 = bf16[1,16,12288]{2,1,0:T(8,128)(2,1)S(1)} fusion(f32[1,16,12288]{2,1,0:T(8,128)S(1)} %mul.226, f32[1,16,12288]{2,1,0:T(8,128)S(1)} %sub.91, bf16[1,12,12288]{2,1,0:T(8,128)(2,1)} %get-tuple-element.11, bf16[1,4,12288]{2,1,0:T(4,128)(2,1)S(1)} %bitcast.143, f32[12288]{0:T(1024)S(1)} %copy-done.1, bf16[1,16,12288]{2,1,0:T(8,128)(2,1)S(1)} %copy-done), kind=kLoop, calls=%fused_computation.73 | loop fusion | flops 2359296 | bytes 2801664 | tf_op jit(solution)/shard_map/convert_element_type | solution.py:19
  33.3 0.5 convert_element_type.209
  33.9 2.3 %fusion.21 = bf16[2048,96]{0,1:T(8,128)(2,1)S(1)} fusion(bf16[2048,96]{1,0:T(8,128)(2,1)S(1)} %convert_element_type.209, bf16[2048,96]{0,1:T(8,128)(2,1)S(1)} %get-tuple-element.6, bf16[2,384,96]{1,2,0:T(8,128)(2,1)} %param.12, bf16[2,96,384]{2,1,0:T(8,128)(2,1)} %param.11), kind=kOutput, calls=%fused_computation.31 | convolution fusion | flops 309657600 | bytes 1327104 | tf_op jit(solution)/shard_map/dot_general | solution.py:27
  36.2 19.5 %all_to_all.10 = bf16[8,256,96]{1,2,0:T(8,128)(2,1)S(1)} all-to-all(bf16[8,256,96]{1,2,0:T(8,128)(2,1)S(1)} %bitcast.141), channel_id=1, replica_groups=mesh['groups'=2,'gz'=8,'tile'=2] {'gz'}, dimensions={0} | all-to-all | bytes 786432 | tf_op jit(solution)/shard_map/all_to_all | solution.py:135
  55.7 0.1 multiply_reduce_fusion.3
  55.9 0.1 multiply_convert_fusion.1
  56.0 0.3 copy.43
  56.4 0.5 convolution_convert_fusion
  56.9 0.8 copy.44
  57.7 0.3 fusion.122
  58.0 5.0 %fusion.31 = f32[256,3,8,8]{2,3,1,0:T(8,128)S(1)} fusion(bf16[3,96]{1,0:T(4,128)(2,1)S(1)} %copy-done.7, bf16[256,8,96]{2,1,0:T(8,128)(2,1)S(1)} %get-tuple-element.8, bf16[256,8,288]{2,1,0:T(8,128)(2,1)S(1)} %bitcast.132), kind=kOutput, calls=%fused_computation.43 | convolution fusion | flops 10027008 | bytes 1246208 | tf_op jit(solution)/shard_map/phzc,pyc->phzy/dot_general | solution.py:96
  63.0 4.0 %fusion.127 = (f32[256,3,8]{2,1,0:T(4,128)}, f32[256,3,8,8]{2,3,1,0:T(8,128)}) fusion(f32[256,3,8,8]{2,3,1,0:T(8,128)S(1)} %fusion.31), kind=kOutput, calls=%fused_computation.161 | output fusion | flops 196615 | bytes 417792 | tf_op jit(solution)/shard_map/sub | solution.py:97
  67.1 0.4 copy.42
  67.6 0.3 copy.46
  67.9 2.9 %fusion.128 = (f32[2048]{0:T(1024)S(1)}, f32[2048,96]{0,1:T(8,128)S(1)}) fusion(f32[2048,96]{0,1:T(8,128)S(1)} %copy.46, bf16[2,96,96]{2,1,0:T(8,128)(2,1)S(1)} %copy-done.4, f32[256,3,8,8]{2,3,1,0:T(8,128)} %get-tuple-element.22, f32[256,3,8]{2,1,0:T(4,128)} %get-tuple-element.21, bf16[256,8,96]{2,1,0:T(8,128)(2,1)S(1)} %get-tuple-element.7, ...), kind=kOutput, calls=%fused_computation.162 | convolution fusion | flops 49248256 | bytes 2352128 | tf_op jit(solution)/shard_map/dot_general | solution.py:102
  70.9 0.1 multiply_reduce_fusion.2
  71.0 1.5 %fusion.22 = bf16[2048,96]{0,1:T(8,128)(2,1)S(1)} fusion(f32[2048,96]{0,1:T(8,128)S(1)} %get-tuple-element.24, f32[96]{0:T(128)S(1)} %copy-done.8, f32[2048]{0:T(1024)S(1)} %add_rsqrt_fusion, f32[2048]{0:T(1024)S(1)} %broadcast_multiply_fusion.1, bf16[2,384,96]{1,2,0:T(8,128)(2,1)S(1)} %copy-done.9, bf16[2,96,384]{2,1,0:T(8,128)(2,1)S(1)} %copy-done.10), kind=kOutput, calls=%fused_computation.32 | convolution fusion | flops 310247424 | bytes 2130432 | tf_op jit(solution)/shard_map/dot_general | solution.py:27
  72.6 0.3 copy.47
  72.9 0.3 copy.48
  73.2 15.0 %all_to_all.11 = bf16[8,256,96]{1,2,0:T(8,128)(2,1)S(1)} all-to-all(bf16[8,256,96]{1,2,0:T(8,128)(2,1)S(1)} %copy.48), channel_id=1, replica_groups=mesh['groups'=2,'gz'=8,'tile'=2] {'gz'}, dimensions={0} | all-to-all | bytes 786432 | tf_op jit(solution)/shard_map/all_to_all | solution.py:136
  88.2 0.3 copy.49
  88.5 1.5 %reshape.313 = bf16[1,16,12288]{2,1,0:T(8,128)(2,1)} reshape(bf16[8,256,96]{2,1,0:T(8,128)(2,1)S(1)} %copy.49) | data formatting | bytes 786432 | tf_op jit(solution)/shard_map/reshape | solution.py:143
  (48 shorter events, 0.8 us)
Async XLA Ops:
  1.0 8.6 %collective-permute-start = (bf16[4,12288]{1,0:T(4,128)(2,1)S(1)}, bf16[4,12288]{1,0:T(4,128)(2,1)S(1)}, u32[]{:S(2)}, u32[]{:S(2)}) collective-permute-start(bf16[4,12288]{1,0:T(4,128)(2,1)S(1)} %slice_bitcast_fusion.9), channel_id=1, source_target_pairs={{0,1},{1,0},{2,3},{3,2},{4,5},{5,4},{6,7},{7,6},{8,9},{9,8},{10,11... | collective-permute-start | bytes 294920 | tf_op jit(solution)/shard_map/ppermute | solution.py:11
  5.3 17.2 %copy-start.6 = (bf16[3,96]{1,0:T(4,128)(2,1)}, bf16[3,96]{1,0:T(4,128)(2,1)S(1)}, u32[]{:S(2)}) copy-start(bf16[3,96]{1,0:T(4,128)(2,1)S(1)} %fusion.106) | copy-start | bytes 1732
  22.5 2.6 %copy-start.3 = (bf16[2,96,96]{2,1,0:T(8,128)(2,1)S(1)}, bf16[2,96,96]{2,1,0:T(8,128)(2,1)}, u32[]{:S(2)}) copy-start(bf16[2,96,96]{2,1,0:T(8,128)(2,1)} %param.10) | copy-start | bytes 110596
  26.3 1.4 %collective-permute-start.1 = (bf16[4,12288]{1,0:T(4,128)(2,1)S(1)}, bf16[4,12288]{1,0:T(4,128)(2,1)S(1)}, u32[]{:S(2)}, u32[]{:S(2)}) collective-permute-start(bf16[4,12288]{1,0:T(4,128)(2,1)S(1)} %pad_maximum_fusion.2), channel_id=1, source_target_pairs={{0,1},{1,0},{2,3},{3,2},{4,5},{5,4},{6,7},{7,6},{8,9},{9,8},{10,11... | collective-permute-start | bytes 294920 | tf_op jit(solution)/shard_map/ppermute | solution.py:11
  28.6 3.4 %copy-start = (bf16[1,16,12288]{2,1,0:T(8,128)(2,1)S(1)}, bf16[1,16,12288]{2,1,0:T(8,128)(2,1)}, u32[]{:S(2)}) copy-start(bf16[1,16,12288]{2,1,0:T(8,128)(2,1)} %param.7) | copy-start | bytes 1179652
  28.6 3.4 %copy-start.1 = (f32[12288]{0:T(1024)S(1)}, f32[12288]{0:T(1024)}, u32[]{:S(2)}) copy-start(f32[12288]{0:T(1024)} %mul.230) | copy-start | bytes 147460
  33.8 22.0 %copy-start.5 = (f32[96]{0:T(128)S(1)}, f32[96]{0:T(128)}, u32[]{:S(2)}) copy-start(f32[96]{0:T(128)} %get-tuple-element.18) | copy-start | bytes 1156
  36.1 20.2 %copy-start.2 = (bf16[2,96,288]{2,1,0:T(8,128)(2,1)S(1)}, bf16[2,96,288]{2,1,0:T(8,128)(2,1)}, u32[]{:S(2)}) copy-start(bf16[2,96,288]{2,1,0:T(8,128)(2,1)} %param.9) | copy-start | bytes 331780
  56.4 1.6 %copy-start.7 = (bf16[3,96]{1,0:T(4,128)(2,1)S(1)}, bf16[3,96]{1,0:T(4,128)(2,1)}, u32[]{:S(2)}) copy-start(bf16[3,96]{1,0:T(4,128)(2,1)} %copy-done.6) | copy-start | bytes 1732
  67.1 0.8 copy-start.4
  67.9 3.1 %copy-start.8 = (f32[96]{0:T(128)S(1)}, f32[96]{0:T(128)}, u32[]{:S(2)}) copy-start(f32[96]{0:T(128)} %get-tuple-element.15) | copy-start | bytes 1156
  67.9 3.1 %copy-start.9 = (bf16[2,384,96]{1,2,0:T(8,128)(2,1)S(1)}, bf16[2,384,96]{1,2,0:T(8,128)(2,1)}, u32[]{:S(2)}) copy-start(bf16[2,384,96]{1,2,0:T(8,128)(2,1)} %param.12) | copy-start | bytes 442372
  67.9 3.1 %copy-start.10 = (bf16[2,96,384]{2,1,0:T(8,128)(2,1)S(1)}, bf16[2,96,384]{2,1,0:T(8,128)(2,1)}, u32[]{:S(2)}) copy-start(bf16[2,96,384]{2,1,0:T(8,128)(2,1)} %param.11) | copy-start | bytes 442372
where the time goes:
time: 90.6 us; the launch traced here: 90 us
  blocking collectives  34.4 us (38%)
  local copies, waits for them, and re-layouts  21.7 us (24%)
  matrix products  20.9 us (23%)
  other arithmetic  11.2 us (12%)
    all_to_all x1, blocking collectives, body(): lax.all_to_all(grouped, 'gz', split_axis=0, concat_axis=0, tiled=True)  19.5 us
    all_to_all x1, blocking collectives, body(): lax.all_to_all(axial_block(pencils, norm_gains, qkv_weight, out_weight, u...  15 us
    dot_general x1, matrix products, axial_block(): jnp.einsum('phzc,pyc->phzy', head_queries, keys, preferred_element_type=j...  5.03 us
    sub x1, matrix products, window_attention(): weights = jax.nn.softmax(scores, axis=-1).astype(jnp.bfloat16)  4.29 us
    sub x1, other arithmetic, axial_block(): jax.nn.softmax(scores * head_size ** (-0.5), axis=-1).astype(jnp.bfloat16)  4.03 us
    dot_general x2, matrix products, feed_forward(): jnp.dot(hidden, down_matrix, preferred_element_type=jnp.float32)  3.84 us
    mul x9, local copies, waits for them, and re-layouts, layer_norm(): centered * lax.rsqrt(variance + epsilon) * gain  3.81 us
    sub x4, local copies, waits for them, and re-layouts, layer_norm(): centered = values - average  3.21 us
  transfers between devices with their start and end apart: 2, of which 1 were waited for; matrix products, arithmetic and copies ran while one was open for 10% of the time, Pallas kernels for 0%

commit v1 on v0

--- a/solution.py
+++ b/solution.py
@@ -1,6 +1,8 @@
 import jax
 import jax.numpy as jnp
 from jax import lax
+from jax.experimental import pallas as pl
+from jax.experimental.pallas import tpu as pltpu
 from jax.sharding import PartitionSpec as P
 
 epsilon = 1e-05
@@ -109,7 +111,7 @@
     return jnp.transpose(mixed, (1, 0, 2))
 
 
-def body(volume, norm_gains, qkv_weight, out_weight, up_weight, down_weight, window_bias):
+def general_body(volume, norm_gains, qkv_weight, out_weight, up_weight, down_weight, window_bias):
     rows_here = volume.shape[1]
     row_width = volume.shape[2]
     channels = norm_gains.shape[1]
@@ -143,12 +145,274 @@
     return returned.reshape(1, rows_here, row_width)
 
 
+LOG2E = 1.4426950408889634
+
+
+def normalised(tokens):
+    average = jnp.mean(tokens, 0, keepdims=True)
+    centered = tokens - average
+    variance = jnp.mean(centered * centered, 0, keepdims=True)
+    return (centered * lax.rsqrt(variance + epsilon)).astype(jnp.bfloat16)
+
+
+def product(left, right):
+    return jnp.dot(left, right, preferred_element_type=jnp.float32)
+
+
+def gated(hidden):
+    inner = hidden * (0.7978845608028654 + 0.035677408136300125 * (hidden * hidden))
+    half = 0.5 * hidden
+    return (half + half * jnp.tanh(inner)).astype(jnp.bfloat16)
+
+
+def column_feed_forward(tokens, up, down):
+    return tokens + product(down, gated(product(up, normalised(tokens))))
+
+
+def pack_kernel(volume_ref, packed_ref):
+    windows, channels, _ = packed_ref.shape
+    width = 8 * channels
+    half = width // 2
+    for window in range(windows):
+        start = window * width + half
+        if window < windows - 1:
+            chunk = volume_ref[:, start : start + width]
+        else:
+            chunk = jnp.concatenate([volume_ref[:, start:], volume_ref[:, :half]], axis=1)
+        chunk = chunk.astype(jnp.float32)
+        rolled = jnp.concatenate([chunk[4:], chunk[:4]], axis=0)
+        pieces = [
+            rolled[8 * part : 8 * part + 8, channels * column : channels * (column + 1)]
+            for part in range(2)
+            for column in range(8)
+        ]
+        tokens = jnp.concatenate(pieces, axis=0)
+        packed_ref[window] = tokens.T.astype(jnp.bfloat16)
+
+
+def unpack_kernel(packed_ref, volume_ref):
+    windows, channels, _ = packed_ref.shape
+    width = 8 * channels
+    half = width // 2
+    for window in range(windows):
+        tokens = packed_ref[window].astype(jnp.float32).T
+        parts = [
+            jnp.concatenate(
+                [tokens[64 * part + 8 * column : 64 * part + 8 * column + 8] for column in range(8)], axis=1
+            )
+            for part in range(2)
+        ]
+        rows = jnp.concatenate([parts[1][4:], parts[0], parts[1][:4]], axis=0).astype(jnp.bfloat16)
+        start = window * width + half
+        if window < windows - 1:
+            volume_ref[:, start : start + width] = rows
+        else:
+            volume_ref[:, start:] = rows[:, :half]
+            volume_ref[:, :half] = rows[:, half:]
+
+
+def blocks_kernel(
+    tokens_ref,
+    bias_ref,
+    qkv_ref,
+    out_ref,
+    up_ref,
+    down_ref,
+    gather_ref,
+    result_ref,
+    planar_ref,
+    query_ref,
+    key_ref,
+    value_ref,
+):
+    planes, channels, _ = planar_ref.shape
+    heads = bias_ref.shape[1] // 64
+    head_size = channels // heads
+    scale = LOG2E * head_size ** (-0.5)
+    lane = lax.broadcasted_iota(jnp.int32, (1, 128), 1)
+    own = (lane < 64) | (lane % 8 < 4)
+    first = lane < 64
+
+    def lateral(plane, carry):
+        one = tokens_ref[2 * plane].astype(jnp.float32)
+        two = tokens_ref[2 * plane + 1].astype(jnp.float32)
+        tokens = jnp.concatenate([jnp.where(own, one, two), jnp.where(own, two, one)], axis=1)
+        packed = product(qkv_ref[0], normalised(tokens))
+        queries = packed[:channels] * scale
+        keys = packed[channels : 2 * channels]
+        values = packed[2 * channels :].astype(jnp.bfloat16)
+        blank = jnp.zeros((128 - channels, 128), jnp.bfloat16)
+        attended = []
+        for pair in range(2):
+            lanes = slice(128 * pair, 128 * pair + 128)
+            query = queries[:, lanes]
+            right = jnp.concatenate(
+                [
+                    jnp.where(first, query, 0.0).astype(jnp.bfloat16),
+                    blank,
+                    jnp.where(first, 0.0, query).astype(jnp.bfloat16),
+                    blank,
+                ],
+                axis=0,
+            )
+            key = jnp.concatenate([keys[:, lanes], jnp.zeros((128 - channels, 128), jnp.float32)], axis=0).T
+            left = []
+            for head in range(heads):
+                mine = lane // head_size == head
+                masked = jnp.where(mine, key, 0.0).astype(jnp.bfloat16)
+                left.append(jnp.concatenate([masked[:64], masked[64:]], axis=1))
+            scores = product(jnp.concatenate(left, axis=0), right) + bias_ref[pair]
+            for head in range(heads):
+                own_scores = scores[64 * head : 64 * head + 64]
+                weights = jnp.exp2(own_scores - jnp.max(own_scores, axis=0, keepdims=True))
+                total = jnp.sum(weights, axis=0, keepdims=True)
+                spread = jnp.concatenate(
+                    [
+                        jnp.where(first, weights, 0.0).astype(jnp.bfloat16),
+                        jnp.where(first, 0.0, weights).astype(jnp.bfloat16),
+                    ],
+                    axis=0,
+                )
+                mixed = product(values[head_size * head : head_size * (head + 1), lanes], spread)
+                attended.append((mixed * (1.0 / total)).astype(jnp.bfloat16))
+        attended = jnp.concatenate(
+            [jnp.concatenate(attended[:heads], axis=0), jnp.concatenate(attended[heads:], axis=0)], axis=1
+        )
+        middle = tokens + product(out_ref[0], attended)
+        planar = column_feed_forward(middle, up_ref[0], down_ref[0])
+        planar_ref[plane] = planar
+        packed = product(qkv_ref[1], normalised(planar))
+        query_ref[plane] = (packed[:channels] * scale).astype(jnp.bfloat16)
+        key_ref[plane] = packed[channels : 2 * channels].astype(jnp.bfloat16)
+        value_ref[plane] = packed[2 * channels :]
+        return carry
+
+    def axial(plane, carry):
+        query = query_ref[plane]
+        pairs = jnp.concatenate([query * key_ref[other] for other in range(planes)], axis=0)
+        scores = product(gather_ref[...], pairs)
+        attended = []
+        for head in range(heads):
+            own_scores = scores[planes * head : planes * (head + 1)]
+            weights = jnp.exp2(own_scores - jnp.max(own_scores, axis=0, keepdims=True))
+            weights = weights / jnp.sum(weights, axis=0, keepdims=True)
+            mixed = jnp.zeros((head_size, 256), jnp.float32)
+            for other in range(planes):
+                value = value_ref[other, head_size * head : head_size * (head + 1), :]
+                mixed += weights[other : other + 1] * value
+            attended.append(mixed.astype(jnp.bfloat16))
+        after = planar_ref[plane] + product(out_ref[1], jnp.concatenate(attended, axis=0))
+        mixed = column_feed_forward(after, up_ref[1], down_ref[1])
+        one, two = mixed[:, :128], mixed[:, 128:]
+        result_ref[2 * plane] = jnp.where(own, one, two).astype(jnp.bfloat16)
+        result_ref[2 * plane + 1] = jnp.where(own, two, one).astype(jnp.bfloat16)
+        return carry
+
+    lax.fori_loop(0, planes, lateral, 0)
+    lax.fori_loop(0, planes, axial, 0)
+
+
+def pack(rows, windows, channels):
+    return pl.pallas_call(
+        pack_kernel,
+        out_shape=jax.ShapeDtypeStruct((windows, channels, 128), jnp.bfloat16),
+        name="pack_windows",
+    )(rows)
+
+
+def unpack(packed, rows, width):
+    return pl.pallas_call(
+        unpack_kernel,
+        out_shape=jax.ShapeDtypeStruct((rows, width), jnp.bfloat16),
+        name="unpack_windows",
+    )(packed)
+
+
+def blocks(tokens, bias, qkv, out, up, down, gather):
+    sources, channels, _ = tokens.shape
+    planes = sources // 2
+    return pl.pallas_call(
+        blocks_kernel,
+        out_shape=jax.ShapeDtypeStruct(tokens.shape, jnp.bfloat16),
+        scratch_shapes=[
+            pltpu.VMEM((planes, channels, 256), jnp.float32),
+            pltpu.VMEM((planes, channels, 256), jnp.bfloat16),
+            pltpu.VMEM((planes, channels, 256), jnp.bfloat16),
+            pltpu.VMEM((planes, channels, 256), jnp.float32),
+        ],
+        compiler_params=pltpu.CompilerParams(vmem_limit_bytes=40 * 1024 * 1024),
+        name="both_blocks",
+    )(tokens, bias, qkv, out, up, down, gather)
+
+
+def pair_bias(window_bias, last):
+    heads = window_bias.shape[0]
+    split = window_bias.reshape(heads, 8, 8, 8, 8).transpose(0, 4, 3, 2, 1).reshape(heads, 64, 64) * LOG2E
+    index = jnp.arange(64, dtype=jnp.int32)
+    column_side = (index // 8 < 4).astype(jnp.int32)
+    row_side = (index % 8 < 4).astype(jnp.int32)
+    column_cut = (column_side[:, None] != column_side[None, :]) & last
+    row_cut = row_side[:, None] != row_side[None, :]
+    plain = jnp.where(column_cut[None], -jnp.inf, split)
+    cut = jnp.where(row_cut[None], -jnp.inf, plain)
+    one = jnp.concatenate([plain, plain], axis=2).reshape(heads * 64, 128)
+    two = jnp.concatenate([plain, cut], axis=2).reshape(heads * 64, 128)
+    return jnp.stack([one, two])
+
+
+def folded(gain, matrix):
+    return (gain[:, None] * matrix.astype(jnp.float32)).T.astype(jnp.bfloat16)
+
+
+def window_body(volume, norm_gains, qkv_weight, out_weight, up_weight, down_weight, window_bias):
+    rows = volume.shape[1]
+    width = volume.shape[2]
+    channels = norm_gains.shape[1]
+    heads = window_bias.shape[0]
+    planes = lax.axis_size("gz")
+    windows = width // channels // 8
+    position = lax.axis_index("gz") * lax.axis_size("tile") + lax.axis_index("tile")
+    packed = pack(volume.reshape(rows, width), windows, channels)
+    tokens = lax.all_to_all(packed, ("gz", "tile"), split_axis=0, concat_axis=0, tiled=True)
+    bias = pair_bias(window_bias, position == windows - 1)
+    qkv = jnp.stack([folded(norm_gains[0], qkv_weight[0]), folded(norm_gains[2], qkv_weight[1])])
+    up = jnp.stack([folded(norm_gains[1], up_weight[0]), folded(norm_gains[3], up_weight[1])])
+    out = jnp.transpose(out_weight, (0, 2, 1))
+    down = jnp.transpose(down_weight, (0, 2, 1))
+    row = jnp.arange(heads * planes, dtype=jnp.int32)[:, None]
+    column = jnp.arange(planes * channels, dtype=jnp.int32)[None, :]
+    gather = (
+        (row // planes == column % channels // (channels // heads)) & (row % planes == column // channels)
+    ).astype(jnp.bfloat16)
+    mixed = blocks(tokens, bias, qkv, out, up, down, gather)
+    returned = lax.all_to_all(mixed, ("gz", "tile"), split_axis=0, concat_axis=0, tiled=True)
+    return unpack(returned, rows, width).reshape(1, rows, width)
+
+
+def fits_windows(mesh, volume, norm_gains, window_bias):
+    planes, tiles = mesh.shape["gz"], mesh.shape["tile"]
+    channels, heads = norm_gains.shape[1], window_bias.shape[0]
+    return (
+        tiles == 2
+        and planes == 8
+        and volume.shape[1] == 16 * tiles
+        and volume.shape[2] == 8 * channels * planes * tiles
+        and channels == 96
+        and heads == 3
+    )
+
+
 def solution(mesh):
     placed = (P(("groups", "gz"), "tile", None), P(), P(), P(), P(), P(), P())
-    return jax.shard_map(
-        body,
-        mesh=mesh,
-        in_specs=placed,
-        out_specs=P(("groups", "gz"), "tile", None),
-        check_vma=False,
-    )
+
+    def run(volume, norm_gains, *weights):
+        chosen = window_body if fits_windows(mesh, volume, norm_gains, weights[-1]) else general_body
+        return jax.shard_map(
+            chosen,
+            mesh=mesh,
+            in_specs=placed,
+            out_specs=P(("groups", "gz"), "tile", None),
+            check_vma=False,
+        )(volume, norm_gains, *weights)
+
+    return run

time: 90.6 us -> 60.3 us (0.67)
  Pallas kernels: 0 us -> 24.5 us
  matrix products: 20.9 us -> 0 us
  blocking collectives: 34.4 us -> 15.6 us
  local copies, waits for them, and re-layouts: 21.7 us -> 4.29 us
  other arithmetic: 11.2 us -> 0.57 us
  starting transfers between devices: 0.65 us -> 7.49 us
  waiting for transfers between devices: 0.44 us -> 7.13 us
    pallas_call x0 -> x3, Pallas kernels: none -> 24.5 us  [the longest x1 20.1 us: blocks(): pl.pallas_call(blocks_kernel, out_shape=jax.ShapeDtypeStruct(tokens.shape...]
    all_to_all x2 -> x1, blocking collectives: 34.4 us -> 15.6 us  [window_body(): lax.all_to_all(mixed, ('gz', 'tile'), split_axis=0, concat_axis=0, tiled=...]
    dot_general x8 -> x0, matrix products: 16.6 us -> none  [the longest x1 5.03 us: axial_block(): jnp.einsum('phzc,pyc->phzy', head_queries, keys, preferred_element_type=j...]
    convert_element_type x14 -> x0, local copies, waits for them, and re-layouts: 7.55 us -> none  [the longest x2 1.76 us: body(): plane.astype(jnp.float32) + lateral.astype(jnp.float32)]
    all_to_all x0 -> x1, starting transfers between devices: none -> 7.49 us  [window_body(): lax.all_to_all(packed, ('gz', 'tile'), split_axis=0, concat_axis=0, tiled...]
    all_to_all x0 -> x1, waiting for transfers between devices: none -> 7.13 us  [window_body(): lax.all_to_all(packed, ('gz', 'tile'), split_axis=0, concat_axis=0, tiled...]
    sub x1 -> x0, matrix products: 4.29 us -> none  [window_attention(): weights = jax.nn.softmax(scores, axis=-1).astype(jnp.bfloat16)]
    sub x1 -> x0, other arithmetic: 4.03 us -> none  [axial_block(): jax.nn.softmax(scores * head_size ** (-0.5), axis=-1).astype(jnp.bfloat16)]
  transfers between devices with their start and end apart: 2 -> 1, of which waited for: 1 -> 1; matrix products, arithmetic and copies ran while one was open for 10% -> 3% of each run, Pallas kernels for 0% -> 0%
where the time goes in v1:
time: 60.3 us; the launch traced here: 59.8 us
  Pallas kernels  24.5 us (41%)
  blocking collectives  15.6 us (26%)
  starting transfers between devices  7.49 us (12%)
  waiting for transfers between devices  7.13 us (12%)
  local copies, waits for them, and re-layouts  4.29 us (7%)
    pallas_call x1, Pallas kernels, blocks(): pl.pallas_call(blocks_kernel, out_shape=jax.ShapeDtypeStruct(tokens.shape...  20.1 us
    all_to_all x1, blocking collectives, window_body(): lax.all_to_all(mixed, ('gz', 'tile'), split_axis=0, concat_axis=0, tiled=...  15.6 us
    all_to_all x1, starting transfers between devices, window_body(): lax.all_to_all(packed, ('gz', 'tile'), split_axis=0, concat_axis=0, tiled...  7.49 us
    all_to_all x1, waiting for transfers between devices, window_body(): lax.all_to_all(packed, ('gz', 'tile'), split_axis=0, concat_axis=0, tiled...  7.13 us
    unnamed x17, local copies, waits for them, and re-layouts  3.37 us
    pallas_call x1, Pallas kernels, pack(): pl.pallas_call(pack_kernel, out_shape=jax.ShapeDtypeStruct((windows, chan...  2.33 us
    pallas_call x1, Pallas kernels, unpack(): pl.pallas_call(unpack_kernel, out_shape=jax.ShapeDtypeStruct((rows, width...  2.08 us
  transfers between devices with their start and end apart: 1, of which 1 were waited for; matrix products, arithmetic and copies ran while one was open for 3% of the time, Pallas kernels for 0%

profile of v1, /device:TPU:0, one launch (start us, length us, event | category | flops | bytes accessed | tf_op | source)
XLA Modules:
  0.0 59.8 jit_solution(1595878946537520319)
XLA Ops:
  0.0 2.3 %pack_windows.1 = bf16[16,96,128]{2,1,0:T(8,128)(2,1)} custom-call(bf16[16,12288]{1,0:T(8,128)(2,1)} %bitcast.55), custom_call_target="tpu_custom_call" | custom-call | tf_op jit(solution)/shard_map/pack_windows/pallas_call | solution.py:316
  2.3 0.0 copy-start.1
  2.3 7.5 %all-to-all-start = ((bf16[16,96,128]{2,1,0:T(8,128)(2,1)}), bf16[16,96,128]{2,1,0:T(8,128)(2,1)S(1)}, u32[]{:S(2)}, u32[]{:S(2)}) async-start(bf16[16,96,128]{2,1,0:T(8,128)(2,1)} %pack_windows.1), calls=%async_computation | async-start | bytes 786432 | tf_op jit(solution)/shard_map/all_to_all | solution.py:376
  9.9 0.0 copy-start.5
  9.9 0.7 %copy-done.5 = f32[4,96]{1,0:T(4,128)S(1)} copy-done((f32[4,96]{1,0:T(4,128)S(1)}, f32[4,96]{1,0:T(4,128)}, u32[]{:S(2)}) %copy-start.5) | copy-done | bytes 1560
  10.5 0.0 copy-done.1
  10.6 0.0 copy-start.2
  10.6 0.1 copy.23
  10.7 0.1 copy.24
  10.8 0.6 %copy-done.2 = bf16[2,96,288]{2,1,0:T(8,128)(2,1)S(1)} copy-done((bf16[2,96,288]{2,1,0:T(8,128)(2,1)S(1)}, bf16[2,96,288]{2,1,0:T(8,128)(2,1)}, u32[]{:S(2)}) %copy-start.2) | copy-done | bytes 110616
  11.5 0.1 copy.21
  11.6 0.0 copy-start.3
  11.6 0.1 copy.22
  11.8 0.8 %copy-done.3 = f32[3,64,64]{2,1,0:T(8,128)S(1)} copy-done((f32[3,64,64]{2,1,0:T(8,128)S(1)}, f32[3,64,64]{2,1,0:T(8,128)}, u32[]{:S(2)}) %copy-start.3) | copy-done | bytes 49176
  12.5 0.1 broadcast_compare_fusion
  12.7 0.1 compare_and_fusion
  12.8 0.2 mul.74
  13.1 0.3 copy.14
  13.4 0.3 mul.76
  13.6 0.0 copy-start.4
  13.7 0.1 copy.15
  13.7 0.7 %copy-done.4 = bf16[2,96,96]{2,1,0:T(8,128)(2,1)S(1)} copy-done((bf16[2,96,96]{2,1,0:T(8,128)(2,1)S(1)}, bf16[2,96,96]{2,1,0:T(8,128)(2,1)}, u32[]{:S(2)}) %copy-start.4) | copy-done | bytes 36888
  14.4 0.1 copy.18
  14.7 0.0 copy-start
  14.7 0.1 maximum_maximum_fusion.bias_ref
  14.8 0.1 and_convert_fusion.gather_ref
  14.9 7.1 %all-to-all-done.tokens_ref = bf16[16,96,128]{2,1,0:T(8,128)(2,1)S(1)} async-done(((bf16[16,96,128]{2,1,0:T(8,128)(2,1)}), bf16[16,96,128]{2,1,0:T(8,128)(2,1)S(1)}, u32[]{:S(2)}, u32[]{:S(2)}) %all-to-all-start) | async-done | bytes 393248 | tf_op jit(solution)/shard_map/all_to_all | solution.py:376
  22.0 0.0 copy-done
  22.0 20.1 %both_blocks.1 = bf16[16,96,128]{2,1,0:T(8,128)(2,1)S(1)} custom-call(bf16[16,96,128]{2,1,0:T(8,128)(2,1)S(1)} %all-to-all-done.tokens_ref, f32[2,192,128]{2,1,0:T(8,128)S(1)} %maximum_maximum_fusion.bias_ref, bf16[2,288,96]{2,1,0:T(8,128)(2,1)S(1)} %pad_maximum_fusion.1.qkv_ref, bf16[2,96,96]{2,1,0:T(8,128)(2,1)S(1)} %bitcast.52, ...), custom_call_target="tpu_custom_call" | custom-call | tf_op jit(solution)/shard_map/both_blocks/pallas_call | solution.py:334
  42.1 15.6 %all_to_all.10.packed_ref = bf16[16,96,128]{2,1,0:T(8,128)(2,1)} all-to-all(bf16[16,96,128]{2,1,0:T(8,128)(2,1)S(1)} %both_blocks.1), channel_id=1, replica_groups=mesh['groups'=2,'gz'=8,'tile'=2] {'gz','tile'}, dimensions={0} | all-to-all | bytes 786432 | tf_op jit(solution)/shard_map/all_to_all | solution.py:388
  57.7 2.1 %unpack_windows.1 = bf16[16,12288]{1,0:T(8,128)(2,1)} custom-call(bf16[16,96,128]{2,1,0:T(8,128)(2,1)} %all_to_all.10.packed_ref), custom_call_target="tpu_custom_call" | custom-call | tf_op jit(solution)/shard_map/unpack_windows/pallas_call | solution.py:324
  (15 shorter events, 0.3 us)
Async XLA Ops:
  2.3 8.2 %copy-start.1 = (bf16[2,96,384]{2,1,0:T(8,128)(2,1)S(1)}, bf16[2,96,384]{2,1,0:T(8,128)(2,1)}, u32[]{:S(2)}) copy-start(bf16[2,96,384]{2,1,0:T(8,128)(2,1)} %param.11) | copy-start | bytes 442372
  2.3 19.7 %all-to-all-start = ((bf16[16,96,128]{2,1,0:T(8,128)(2,1)}), bf16[16,96,128]{2,1,0:T(8,128)(2,1)S(1)}, u32[]{:S(2)}, u32[]{:S(2)}) async-start(bf16[16,96,128]{2,1,0:T(8,128)(2,1)} %pack_windows.1), calls=%async_computation | async-start | bytes 786432 | tf_op jit(solution)/shard_map/all_to_all | solution.py:376
  9.9 0.7 %copy-start.5 = (f32[4,96]{1,0:T(4,128)S(1)}, f32[4,96]{1,0:T(4,128)}, u32[]{:S(2)}) copy-start(f32[4,96]{1,0:T(4,128)} %param.8) | copy-start | bytes 4612
  10.6 0.9 %copy-start.2 = (bf16[2,96,288]{2,1,0:T(8,128)(2,1)S(1)}, bf16[2,96,288]{2,1,0:T(8,128)(2,1)}, u32[]{:S(2)}) copy-start(bf16[2,96,288]{2,1,0:T(8,128)(2,1)} %param.9) | copy-start | bytes 331780
  11.6 0.9 %copy-start.3 = (f32[3,64,64]{2,1,0:T(8,128)S(1)}, f32[3,64,64]{2,1,0:T(8,128)}, u32[]{:S(2)}) copy-start(f32[3,64,64]{2,1,0:T(8,128)} %param.13) | copy-start | bytes 147460
  13.6 0.8 %copy-start.4 = (bf16[2,96,96]{2,1,0:T(8,128)(2,1)S(1)}, bf16[2,96,96]{2,1,0:T(8,128)(2,1)}, u32[]{:S(2)}) copy-start(bf16[2,96,96]{2,1,0:T(8,128)(2,1)} %param.10) | copy-start | bytes 110596
  14.7 7.4 %copy-start = (bf16[2,384,96]{1,2,0:T(8,128)(2,1)S(1)}, bf16[2,384,96]{1,2,0:T(8,128)(2,1)}, u32[]{:S(2)}) copy-start(bf16[2,384,96]{1,2,0:T(8,128)(2,1)} %param.12) | copy-start | bytes 442372

commit v2 on v1

--- a/solution.py
+++ b/solution.py
@@ -159,10 +159,10 @@
     return jnp.dot(left, right, preferred_element_type=jnp.float32)
 
 
-def gated(hidden):
-    inner = hidden * (0.7978845608028654 + 0.035677408136300125 * (hidden * hidden))
-    half = 0.5 * hidden
-    return (half + half * jnp.tanh(inner)).astype(jnp.bfloat16)
+def gated(half):
+    half = half.astype(jnp.bfloat16)
+    inner = half * (1.5957691216057308 + 0.285419265090401 * (half * half))
+    return half + half * jnp.tanh(inner)
 
 
 def column_feed_forward(tokens, up, down):
@@ -211,11 +211,15 @@
             volume_ref[:, :half] = rows[:, half:]
 
 
+GROUP = 8
+
+
 def blocks_kernel(
     tokens_ref,
     bias_ref,
     qkv_ref,
     out_ref,
+    mix_ref,
     up_ref,
     down_ref,
     gather_ref,
@@ -225,25 +229,28 @@
     key_ref,
     value_ref,
 ):
-    planes, channels, _ = planar_ref.shape
+    channels = tokens_ref.shape[1]
+    planes = tokens_ref.shape[0] // 2
     heads = bias_ref.shape[1] // 64
     head_size = channels // heads
-    scale = LOG2E * head_size ** (-0.5)
     lane = lax.broadcasted_iota(jnp.int32, (1, 128), 1)
     own = (lane < 64) | (lane % 8 < 4)
     first = lane < 64
 
-    def lateral(plane, carry):
-        one = tokens_ref[2 * plane].astype(jnp.float32)
-        two = tokens_ref[2 * plane + 1].astype(jnp.float32)
-        tokens = jnp.concatenate([jnp.where(own, one, two), jnp.where(own, two, one)], axis=1)
+    def lateral(step, carry):
+        tokens = []
+        for plane in range(GROUP):
+            one = tokens_ref[2 * (step * GROUP + plane)].astype(jnp.float32)
+            two = tokens_ref[2 * (step * GROUP + plane) + 1].astype(jnp.float32)
+            tokens += [jnp.where(own, one, two), jnp.where(own, two, one)]
+        tokens = jnp.concatenate(tokens, axis=1)
         packed = product(qkv_ref[0], normalised(tokens))
-        queries = packed[:channels] * scale
+        queries = packed[:channels]
         keys = packed[channels : 2 * channels]
         values = packed[2 * channels :].astype(jnp.bfloat16)
         blank = jnp.zeros((128 - channels, 128), jnp.bfloat16)
-        attended = []
-        for pair in range(2):
+        scores = []
+        for pair in range(2 * GROUP):
             lanes = slice(128 * pair, 128 * pair + 128)
             query = queries[:, lanes]
             right = jnp.concatenate(
@@ -261,9 +268,13 @@
                 mine = lane // head_size == head
                 masked = jnp.where(mine, key, 0.0).astype(jnp.bfloat16)
                 left.append(jnp.concatenate([masked[:64], masked[64:]], axis=1))
-            scores = product(jnp.concatenate(left, axis=0), right) + bias_ref[pair]
+            scores.append(product(jnp.concatenate(left, axis=0), right) + bias_ref[pair % 2])
+        attended = []
+        for pair in range(2 * GROUP):
+            lanes = slice(128 * pair, 128 * pair + 128)
+            mixed = []
             for head in range(heads):
-                own_scores = scores[64 * head : 64 * head + 64]
+                own_scores = scores[pair][64 * head : 64 * head + 64]
                 weights = jnp.exp2(own_scores - jnp.max(own_scores, axis=0, keepdims=True))
                 total = jnp.sum(weights, axis=0, keepdims=True)
                 spread = jnp.concatenate(
@@ -273,43 +284,61 @@
                     ],
                     axis=0,
                 )
-                mixed = product(values[head_size * head : head_size * (head + 1), lanes], spread)
-                attended.append((mixed * (1.0 / total)).astype(jnp.bfloat16))
-        attended = jnp.concatenate(
-            [jnp.concatenate(attended[:heads], axis=0), jnp.concatenate(attended[heads:], axis=0)], axis=1
-        )
-        middle = tokens + product(out_ref[0], attended)
+                head_mixed = product(values[head_size * head : head_size * (head + 1), lanes], spread)
+                mixed.append((head_mixed * (1.0 / total)).astype(jnp.bfloat16))
+            attended.append(jnp.concatenate(mixed, axis=0))
+        attended = jnp.concatenate(attended, axis=1)
+        middle = tokens + product(out_ref[...], attended)
         planar = column_feed_forward(middle, up_ref[0], down_ref[0])
-        planar_ref[plane] = planar
-        packed = product(qkv_ref[1], normalised(planar))
-        query_ref[plane] = (packed[:channels] * scale).astype(jnp.bfloat16)
-        key_ref[plane] = packed[channels : 2 * channels].astype(jnp.bfloat16)
-        value_ref[plane] = packed[2 * channels :]
+        packed = product(qkv_ref[1], normalised(planar)).astype(jnp.bfloat16)
+        for plane in range(GROUP):
+            here = pl.ds(pl.multiple_of((step * GROUP + plane) * channels, channels), channels)
+            lanes = slice(256 * plane, 256 * plane + 256)
+            planar_ref[here, :] = planar[:, lanes]
+            query_ref[here, :] = packed[:channels, lanes]
+            key_ref[here, :] = packed[channels : 2 * channels, lanes]
+            value_ref[here, :] = packed[2 * channels :, lanes]
         return carry
 
-    def axial(plane, carry):
-        query = query_ref[plane]
-        pairs = jnp.concatenate([query * key_ref[other] for other in range(planes)], axis=0)
-        scores = product(gather_ref[...], pairs)
-        attended = []
-        for head in range(heads):
-            own_scores = scores[planes * head : planes * (head + 1)]
-            weights = jnp.exp2(own_scores - jnp.max(own_scores, axis=0, keepdims=True))
-            weights = weights / jnp.sum(weights, axis=0, keepdims=True)
-            mixed = jnp.zeros((head_size, 256), jnp.float32)
+    def axial(step, carry):
+        scores = []
+        for plane in range(GROUP):
+            here = pl.ds(pl.multiple_of((step * GROUP + plane) * channels, channels), channels)
+            query = query_ref[here, :]
+            pairs = jnp.concatenate(
+                [query * key_ref[channels * other : channels * (other + 1), :] for other in range(planes)], axis=0
+            )
+            scores.append(product(gather_ref[...], pairs))
+        after = []
+        for plane in range(GROUP):
+            here = pl.ds(pl.multiple_of((step * GROUP + plane) * channels, channels), channels)
+            weights = []
+            for head in range(heads):
+                own_scores = scores[plane][planes * head : planes * (head + 1)]
+                own_weights = jnp.exp2(own_scores - jnp.max(own_scores, axis=0, keepdims=True))
+                weights.append(own_weights * (1.0 / jnp.sum(own_weights, axis=0, keepdims=True)))
+            spread = []
             for other in range(planes):
-                value = value_ref[other, head_size * head : head_size * (head + 1), :]
-                mixed += weights[other : other + 1] * value
-            attended.append(mixed.astype(jnp.bfloat16))
-        after = planar_ref[plane] + product(out_ref[1], jnp.concatenate(attended, axis=0))
+                wide = jnp.concatenate(
+                    [
+                        jnp.broadcast_to(weights[head][other : other + 1], (head_size, 256)).astype(jnp.bfloat16)
+                        for head in range(heads)
+                    ],
+                    axis=0,
+                )
+                spread.append(wide * value_ref[channels * other : channels * (other + 1), :])
+            after.append(planar_ref[here, :] + product(mix_ref[...], jnp.concatenate(spread, axis=0)))
+        after = jnp.concatenate(after, axis=1)
         mixed = column_feed_forward(after, up_ref[1], down_ref[1])
-        one, two = mixed[:, :128], mixed[:, 128:]
-        result_ref[2 * plane] = jnp.where(own, one, two).astype(jnp.bfloat16)
-        result_ref[2 * plane + 1] = jnp.where(own, two, one).astype(jnp.bfloat16)
+        for plane in range(GROUP):
+            one = mixed[:, 256 * plane : 256 * plane + 128]
+            two = mixed[:, 256 * plane + 128 : 256 * plane + 256]
+            result_ref[2 * (step * GROUP + plane)] = jnp.where(own, one, two).astype(jnp.bfloat16)
+            result_ref[2 * (step * GROUP + plane) + 1] = jnp.where(own, two, one).astype(jnp.bfloat16)
         return carry
 
-    lax.fori_loop(0, planes, lateral, 0)
-    lax.fori_loop(0, planes, axial, 0)
+    lax.fori_loop(0, planes // GROUP, lateral, 0)
+    lax.fori_loop(0, planes // GROUP, axial, 0)
 
 
 def pack(rows, windows, channels):
@@ -328,21 +357,21 @@
     )(packed)
 
 
-def blocks(tokens, bias, qkv, out, up, down, gather):
+def blocks(tokens, *operands):
     sources, channels, _ = tokens.shape
-    planes = sources // 2
+    rows = sources // 2 * channels
     return pl.pallas_call(
         blocks_kernel,
         out_shape=jax.ShapeDtypeStruct(tokens.shape, jnp.bfloat16),
         scratch_shapes=[
-            pltpu.VMEM((planes, channels, 256), jnp.float32),
-            pltpu.VMEM((planes, channels, 256), jnp.bfloat16),
-            pltpu.VMEM((planes, channels, 256), jnp.bfloat16),
-            pltpu.VMEM((planes, channels, 256), jnp.float32),
+            pltpu.VMEM((rows, 256), jnp.float32),
+            pltpu.VMEM((rows, 256), jnp.bfloat16),
+            pltpu.VMEM((rows, 256), jnp.bfloat16),
+            pltpu.VMEM((rows, 256), jnp.bfloat16),
         ],
         compiler_params=pltpu.CompilerParams(vmem_limit_bytes=40 * 1024 * 1024),
         name="both_blocks",
-    )(tokens, bias, qkv, out, up, down, gather)
+    )(tokens, *operands)
 
 
 def pair_bias(window_bias, last):
@@ -360,8 +389,8 @@
     return jnp.stack([one, two])
 
 
-def folded(gain, matrix):
-    return (gain[:, None] * matrix.astype(jnp.float32)).T.astype(jnp.bfloat16)
+def folded(gain, matrix, scale):
+    return (gain[:, None] * matrix.astype(jnp.float32) * scale).T.astype(jnp.bfloat16)
 
 
 def window_body(volume, norm_gains, qkv_weight, out_weight, up_weight, down_weight, window_bias):
@@ -375,16 +404,19 @@
     packed = pack(volume.reshape(rows, width), windows, channels)
     tokens = lax.all_to_all(packed, ("gz", "tile"), split_axis=0, concat_axis=0, tiled=True)
     bias = pair_bias(window_bias, position == windows - 1)
-    qkv = jnp.stack([folded(norm_gains[0], qkv_weight[0]), folded(norm_gains[2], qkv_weight[1])])
-    up = jnp.stack([folded(norm_gains[1], up_weight[0]), folded(norm_gains[3], up_weight[1])])
-    out = jnp.transpose(out_weight, (0, 2, 1))
+    is_query = jnp.arange(3 * channels, dtype=jnp.int32) < channels
+    scale = jnp.where(is_query, LOG2E * (channels // heads) ** (-0.5), 1.0)[None, :]
+    qkv = jnp.stack([folded(norm_gains[0], qkv_weight[0], scale), folded(norm_gains[2], qkv_weight[1], scale)])
+    up = jnp.stack([folded(norm_gains[1], up_weight[0], 0.5), folded(norm_gains[3], up_weight[1], 0.5)])
+    out = out_weight[0].T
+    mix = jnp.tile(out_weight[1].T, (1, planes))
     down = jnp.transpose(down_weight, (0, 2, 1))
     row = jnp.arange(heads * planes, dtype=jnp.int32)[:, None]
     column = jnp.arange(planes * channels, dtype=jnp.int32)[None, :]
     gather = (
         (row // planes == column % channels // (channels // heads)) & (row % planes == column // channels)
     ).astype(jnp.bfloat16)
-    mixed = blocks(tokens, bias, qkv, out, up, down, gather)
+    mixed = blocks(tokens, bias, qkv, out, mix, up, down, gather)
     returned = lax.all_to_all(mixed, ("gz", "tile"), split_axis=0, concat_axis=0, tiled=True)
     return unpack(returned, rows, width).reshape(1, rows, width)
 

time: 60.3 us -> 44.8 us (0.74)
  Pallas kernels: 24.5 us -> 9 us
    pallas_call x1, Pallas kernels: 20.1 us -> 4.6 us  [blocks(): pl.pallas_call(blocks_kernel, out_shape=jax.ShapeDtypeStruct(tokens.shape...]
  transfers between devices with their start and end apart: 1 -> 1, of which waited for: 1 -> 1; matrix products, arithmetic and copies ran while one was open for 3% -> 6% of each run, Pallas kernels for 0% -> 0%
where the time goes in v2:
time: 44.8 us; the launch traced here: 44.3 us
  blocking collectives  15.6 us (35%)
  Pallas kernels  9 us (20%)
  starting transfers between devices  7.49 us (17%)
  waiting for transfers between devices  6.7 us (15%)
  local copies, waits for them, and re-layouts  4.61 us (10%)
  other arithmetic  0.66 us (1%)
    all_to_all x1, blocking collectives, window_body(): lax.all_to_all(mixed, ('gz', 'tile'), split_axis=0, concat_axis=0, tiled=...  15.6 us
    all_to_all x1, starting transfers between devices, window_body(): lax.all_to_all(packed, ('gz', 'tile'), split_axis=0, concat_axis=0, tiled...  7.49 us
    all_to_all x1, waiting for transfers between devices, window_body(): lax.all_to_all(packed, ('gz', 'tile'), split_axis=0, concat_axis=0, tiled...  6.7 us
    pallas_call x1, Pallas kernels, blocks(): pl.pallas_call(blocks_kernel, out_shape=jax.ShapeDtypeStruct(tokens.shape...  4.6 us
    unnamed x17, local copies, waits for them, and re-layouts  3.38 us
    pallas_call x1, Pallas kernels, pack(): pl.pallas_call(pack_kernel, out_shape=jax.ShapeDtypeStruct((windows, chan...  2.33 us
    pallas_call x1, Pallas kernels, unpack(): pl.pallas_call(unpack_kernel, out_shape=jax.ShapeDtypeStruct((rows, width...  2.08 us
  transfers between devices with their start and end apart: 1, of which 1 were waited for; matrix products, arithmetic and copies ran while one was open for 6% of the time, Pallas kernels for 0%

profile of v2, /device:TPU:0, one launch (start us, length us, event | category | flops | bytes accessed | tf_op | source)
XLA Modules:
  0.0 44.3 jit_solution(12669791277267631332)
XLA Ops:
  0.0 2.3 %pack_windows.1 = bf16[16,96,128]{2,1,0:T(8,128)(2,1)} custom-call(bf16[16,12288]{1,0:T(8,128)(2,1)} %bitcast.61), custom_call_target="tpu_custom_call" | custom-call | tf_op jit(solution)/shard_map/pack_windows/pallas_call | solution.py:345
  2.3 0.0 copy-start.1
  2.3 7.5 %all-to-all-start = ((bf16[16,96,128]{2,1,0:T(8,128)(2,1)}), bf16[16,96,128]{2,1,0:T(8,128)(2,1)S(1)}, u32[]{:S(2)}, u32[]{:S(2)}) async-start(bf16[16,96,128]{2,1,0:T(8,128)(2,1)} %pack_windows.1), calls=%async_computation | async-start | bytes 786432 | tf_op jit(solution)/shard_map/all_to_all | solution.py:405
  9.9 0.0 copy-start.5
  9.9 0.7 %copy-done.5 = f32[4,96]{1,0:T(4,128)S(1)} copy-done((f32[4,96]{1,0:T(4,128)S(1)}, f32[4,96]{1,0:T(4,128)}, u32[]{:S(2)}) %copy-start.5) | copy-done | bytes 1560
  10.6 0.0 copy-done.1
  10.6 0.0 copy-start.2
  10.6 0.1 copy.26
  10.7 0.1 copy.27
  10.8 0.6 %copy-done.2 = bf16[2,96,288]{2,1,0:T(8,128)(2,1)S(1)} copy-done((bf16[2,96,288]{2,1,0:T(8,128)(2,1)S(1)}, bf16[2,96,288]{2,1,0:T(8,128)(2,1)}, u32[]{:S(2)}) %copy-start.2) | copy-done | bytes 110616
  11.5 0.1 copy.23
  11.6 0.0 copy-start.3
  11.6 0.1 copy.24
  11.8 0.8 %copy-done.3 = f32[3,64,64]{2,1,0:T(8,128)S(1)} copy-done((f32[3,64,64]{2,1,0:T(8,128)S(1)}, f32[3,64,64]{2,1,0:T(8,128)}, u32[]{:S(2)}) %copy-start.3) | copy-done | bytes 49176
  12.5 0.0 copy-start.4
  12.5 0.1 broadcast_compare_fusion
  12.6 0.7 %copy-done.4 = bf16[2,96,96]{2,1,0:T(8,128)(2,1)S(1)} copy-done((bf16[2,96,96]{2,1,0:T(8,128)(2,1)S(1)}, bf16[2,96,96]{2,1,0:T(8,128)(2,1)}, u32[]{:S(2)}) %copy-start.4) | copy-done | bytes 36888
  13.3 0.1 fusion.10
  13.5 0.1 compare_and_fusion
  13.6 0.1 fusion.8
  13.7 0.2 mul.96
  13.9 0.3 copy.15
  14.2 0.3 mul.98
  14.5 0.1 copy.16
  14.5 0.1 copy.20
  14.7 0.2 tile.10.mix_ref
  14.9 0.1 copy.25
  15.1 0.0 copy-start
  15.1 0.1 maximum_maximum_fusion.bias_ref
  15.2 0.1 and_convert_fusion.gather_ref
  15.3 6.7 %all-to-all-done.tokens_ref = bf16[16,96,128]{2,1,0:T(8,128)(2,1)S(1)} async-done(((bf16[16,96,128]{2,1,0:T(8,128)(2,1)}), bf16[16,96,128]{2,1,0:T(8,128)(2,1)S(1)}, u32[]{:S(2)}, u32[]{:S(2)}) %all-to-all-start) | async-done | bytes 393248 | tf_op jit(solution)/shard_map/all_to_all | solution.py:405
  22.0 0.0 copy-done
  22.0 4.6 %both_blocks.1 = bf16[16,96,128]{2,1,0:T(8,128)(2,1)S(1)} custom-call(bf16[16,96,128]{2,1,0:T(8,128)(2,1)S(1)} %all-to-all-done.tokens_ref, f32[2,192,128]{2,1,0:T(8,128)S(1)} %maximum_maximum_fusion.bias_ref, bf16[2,288,96]{2,1,0:T(8,128)(2,1)S(1)} %pad_maximum_fusion.1.qkv_ref, bf16[96,96]{1,0:T(8,128)(2,1)S(1)} %bitcast.59, ...), custom_call_target="tpu_custom_call" | custom-call | tf_op jit(solution)/shard_map/both_blocks/pallas_call | solution.py:363
  26.6 15.6 %all_to_all.10.packed_ref = bf16[16,96,128]{2,1,0:T(8,128)(2,1)} all-to-all(bf16[16,96,128]{2,1,0:T(8,128)(2,1)S(1)} %both_blocks.1), channel_id=1, replica_groups=mesh['groups'=2,'gz'=8,'tile'=2] {'gz','tile'}, dimensions={0} | all-to-all | bytes 786432 | tf_op jit(solution)/shard_map/all_to_all | solution.py:420
  42.3 2.1 %unpack_windows.1 = bf16[16,12288]{1,0:T(8,128)(2,1)} custom-call(bf16[16,96,128]{2,1,0:T(8,128)(2,1)} %all_to_all.10.packed_ref), custom_call_target="tpu_custom_call" | custom-call | tf_op jit(solution)/shard_map/unpack_windows/pallas_call | solution.py:353
  (16 shorter events, 0.2 us)
Async XLA Ops:
  2.3 8.2 %copy-start.1 = (bf16[2,96,384]{2,1,0:T(8,128)(2,1)S(1)}, bf16[2,96,384]{2,1,0:T(8,128)(2,1)}, u32[]{:S(2)}) copy-start(bf16[2,96,384]{2,1,0:T(8,128)(2,1)} %param.11) | copy-start | bytes 442372
  2.3 19.7 %all-to-all-start = ((bf16[16,96,128]{2,1,0:T(8,128)(2,1)}), bf16[16,96,128]{2,1,0:T(8,128)(2,1)S(1)}, u32[]{:S(2)}, u32[]{:S(2)}) async-start(bf16[16,96,128]{2,1,0:T(8,128)(2,1)} %pack_windows.1), calls=%async_computation | async-start | bytes 786432 | tf_op jit(solution)/shard_map/all_to_all | solution.py:405
  9.9 0.7 %copy-start.5 = (f32[4,96]{1,0:T(4,128)S(1)}, f32[4,96]{1,0:T(4,128)}, u32[]{:S(2)}) copy-start(f32[4,96]{1,0:T(4,128)} %param.8) | copy-start | bytes 4612
  10.6 0.9 %copy-start.2 = (bf16[2,96,288]{2,1,0:T(8,128)(2,1)S(1)}, bf16[2,96,288]{2,1,0:T(8,128)(2,1)}, u32[]{:S(2)}) copy-start(bf16[2,96,288]{2,1,0:T(8,128)(2,1)} %param.9) | copy-start | bytes 331780
  11.6 0.9 %copy-start.3 = (f32[3,64,64]{2,1,0:T(8,128)S(1)}, f32[3,64,64]{2,1,0:T(8,128)}, u32[]{:S(2)}) copy-start(f32[3,64,64]{2,1,0:T(8,128)} %param.13) | copy-start | bytes 147460
  12.5 0.8 %copy-start.4 = (bf16[2,96,96]{2,1,0:T(8,128)(2,1)S(1)}, bf16[2,96,96]{2,1,0:T(8,128)(2,1)}, u32[]{:S(2)}) copy-start(bf16[2,96,96]{2,1,0:T(8,128)(2,1)} %param.10) | copy-start | bytes 110596
  15.1 6.9 %copy-start = (bf16[2,384,96]{1,2,0:T(8,128)(2,1)S(1)}, bf16[2,384,96]{1,2,0:T(8,128)(2,1)}, u32[]{:S(2)}) copy-start(bf16[2,384,96]{1,2,0:T(8,128)(2,1)} %param.12) | copy-start | bytes 442372

commit v3 on v2

--- a/solution.py
+++ b/solution.py
@@ -159,14 +159,14 @@
     return jnp.dot(left, right, preferred_element_type=jnp.float32)
 
 
-def gated(half):
-    half = half.astype(jnp.bfloat16)
-    inner = half * (1.5957691216057308 + 0.285419265090401 * (half * half))
-    return half + half * jnp.tanh(inner)
-
-
-def column_feed_forward(tokens, up, down):
-    return tokens + product(down, gated(product(up, normalised(tokens))))
+GELU_IN = 0.035677408136300125 ** (1 / 3)
+GELU_LINEAR = 0.7978845608028654 / GELU_IN
+GELU_OUT = 0.5 / GELU_IN
+
+
+def gated(scaled):
+    scaled = scaled.astype(jnp.bfloat16)
+    return scaled + scaled * jnp.tanh(scaled * (GELU_LINEAR + scaled * scaled))
 
 
 def pack_kernel(volume_ref, packed_ref):
@@ -211,7 +211,17 @@
             volume_ref[:, :half] = rows[:, half:]
 
 
-GROUP = 8
+TOGETHER = 8
+LAG = 1
+
+
+def in_waves(stages, members, together, lag):
+    groups = [members[start : start + together] for start in range(0, len(members), together)]
+    for step in range(len(stages) + lag * (len(groups) - 1)):
+        for index, group in enumerate(groups):
+            if 0 <= step - lag * index < len(stages):
+                for member in group:
+                    stages[step - lag * index](member)
 
 
 def blocks_kernel(
@@ -236,21 +246,31 @@
     lane = lax.broadcasted_iota(jnp.int32, (1, 128), 1)
     own = (lane < 64) | (lane % 8 < 4)
     first = lane < 64
-
-    def lateral(step, carry):
-        tokens = []
-        for plane in range(GROUP):
-            one = tokens_ref[2 * (step * GROUP + plane)].astype(jnp.float32)
-            two = tokens_ref[2 * (step * GROUP + plane) + 1].astype(jnp.float32)
-            tokens += [jnp.where(own, one, two), jnp.where(own, two, one)]
-        tokens = jnp.concatenate(tokens, axis=1)
-        packed = product(qkv_ref[0], normalised(tokens))
-        queries = packed[:channels]
-        keys = packed[channels : 2 * channels]
-        values = packed[2 * channels :].astype(jnp.bfloat16)
-        blank = jnp.zeros((128 - channels, 128), jnp.bfloat16)
+    blank = jnp.zeros((128 - channels, 128), jnp.bfloat16)
+    blank_rows = jnp.zeros((128 - channels, 128), jnp.float32)
+    held = [{} for _ in range(planes)]
+
+    def rows_of(plane):
+        return slice(plane * channels, (plane + 1) * channels)
+
+    def load(plane):
+        one, two = tokens_ref[2 * plane], tokens_ref[2 * plane + 1]
+        tokens = jnp.concatenate([jnp.where(own, one, two), jnp.where(own, two, one)], axis=1)
+        held[plane]["x"] = tokens.astype(jnp.float32)
+
+    def norm(plane):
+        held[plane]["n"] = normalised(held[plane]["x"])
+
+    def lateral_qkv(plane):
+        packed = product(qkv_ref[0], held[plane].pop("n"))
+        held[plane]["q"] = packed[:channels]
+        held[plane]["k"] = packed[channels : 2 * channels]
+        held[plane]["v"] = packed[2 * channels :].astype(jnp.bfloat16)
+
+    def lateral_scores(plane):
+        queries, keys = held[plane].pop("q"), held[plane].pop("k")
         scores = []
-        for pair in range(2 * GROUP):
+        for pair in range(2):
             lanes = slice(128 * pair, 128 * pair + 128)
             query = queries[:, lanes]
             right = jnp.concatenate(
@@ -262,17 +282,18 @@
                 ],
                 axis=0,
             )
-            key = jnp.concatenate([keys[:, lanes], jnp.zeros((128 - channels, 128), jnp.float32)], axis=0).T
+            key = jnp.concatenate([keys[:, lanes], blank_rows], axis=0).T
             left = []
             for head in range(heads):
-                mine = lane // head_size == head
-                masked = jnp.where(mine, key, 0.0).astype(jnp.bfloat16)
+                masked = jnp.where(lane // head_size == head, key, 0.0).astype(jnp.bfloat16)
                 left.append(jnp.concatenate([masked[:64], masked[64:]], axis=1))
-            scores.append(product(jnp.concatenate(left, axis=0), right) + bias_ref[pair % 2])
-        attended = []
-        for pair in range(2 * GROUP):
-            lanes = slice(128 * pair, 128 * pair + 128)
-            mixed = []
+            scores.append(product(jnp.concatenate(left, axis=0), right) + bias_ref[pair])
+        held[plane]["s"] = scores
+
+    def lateral_weights(plane):
+        scores = held[plane].pop("s")
+        held[plane]["w"] = []
+        for pair in range(2):
             for head in range(heads):
                 own_scores = scores[pair][64 * head : 64 * head + 64]
                 weights = jnp.exp2(own_scores - jnp.max(own_scores, axis=0, keepdims=True))
@@ -284,67 +305,93 @@
                     ],
                     axis=0,
                 )
-                head_mixed = product(values[head_size * head : head_size * (head + 1), lanes], spread)
-                mixed.append((head_mixed * (1.0 / total)).astype(jnp.bfloat16))
+                held[plane]["w"].append((spread, 1.0 / total))
+
+    def lateral_values(plane):
+        weights, values = held[plane].pop("w"), held[plane].pop("v")
+        attended = []
+        for pair in range(2):
+            lanes = slice(128 * pair, 128 * pair + 128)
+            mixed = []
+            for head in range(heads):
+                spread, inverse = weights[heads * pair + head]
+                own_mixed = product(values[head_size * head : head_size * (head + 1), lanes], spread)
+                mixed.append((own_mixed * inverse).astype(jnp.bfloat16))
             attended.append(jnp.concatenate(mixed, axis=0))
-        attended = jnp.concatenate(attended, axis=1)
-        middle = tokens + product(out_ref[...], attended)
-        planar = column_feed_forward(middle, up_ref[0], down_ref[0])
-        packed = product(qkv_ref[1], normalised(planar)).astype(jnp.bfloat16)
-        for plane in range(GROUP):
-            here = pl.ds(pl.multiple_of((step * GROUP + plane) * channels, channels), channels)
-            lanes = slice(256 * plane, 256 * plane + 256)
-            planar_ref[here, :] = planar[:, lanes]
-            query_ref[here, :] = packed[:channels, lanes]
-            key_ref[here, :] = packed[channels : 2 * channels, lanes]
-            value_ref[here, :] = packed[2 * channels :, lanes]
-        return carry
-
-    def axial(step, carry):
-        scores = []
-        for plane in range(GROUP):
-            here = pl.ds(pl.multiple_of((step * GROUP + plane) * channels, channels), channels)
-            query = query_ref[here, :]
-            pairs = jnp.concatenate(
-                [query * key_ref[channels * other : channels * (other + 1), :] for other in range(planes)], axis=0
+        held[plane]["a"] = jnp.concatenate(attended, axis=1)
+
+    def lateral_out(plane):
+        held[plane]["x"] = held[plane]["x"] + product(out_ref[...], held[plane].pop("a"))
+
+    def raised(layer):
+        def stage(plane):
+            held[plane]["h"] = product(up_ref[layer], held[plane].pop("n"))
+
+        return stage
+
+    def gelu(plane):
+        held[plane]["g"] = gated(held[plane].pop("h"))
+
+    def lowered(layer):
+        def stage(plane):
+            held[plane]["x"] = held[plane]["x"] + product(down_ref[layer], held[plane].pop("g"))
+
+        return stage
+
+    def axial_qkv(plane):
+        packed = product(qkv_ref[1], held[plane].pop("n")).astype(jnp.bfloat16)
+        planar_ref[rows_of(plane), :] = held[plane].pop("x")
+        query_ref[rows_of(plane), :] = packed[:channels]
+        key_ref[rows_of(plane), :] = packed[channels : 2 * channels]
+        value_ref[rows_of(plane), :] = packed[2 * channels :]
+
+    def axial_scores(plane):
+        query = query_ref[rows_of(plane), :]
+        pairs = jnp.concatenate([query * key_ref[rows_of(other), :] for other in range(planes)], axis=0)
+        held[plane]["s"] = product(gather_ref[...], pairs)
+
+    def axial_weights(plane):
+        scores = held[plane].pop("s")
+        weights = []
+        for head in range(heads):
+            own_scores = scores[planes * head : planes * (head + 1)]
+            own_weights = jnp.exp2(own_scores - jnp.max(own_scores, axis=0, keepdims=True))
+            weights.append(own_weights * (1.0 / jnp.sum(own_weights, axis=0, keepdims=True)))
+        held[plane]["w"] = weights
+
+    def axial_values(plane):
+        weights = held[plane].pop("w")
+        spread = []
+        for other in range(planes):
+            wide = jnp.concatenate(
+                [
+                    jnp.broadcast_to(weights[head][other : other + 1], (head_size, 256)).astype(jnp.bfloat16)
+                    for head in range(heads)
+                ],
+                axis=0,
             )
-            scores.append(product(gather_ref[...], pairs))
-        after = []
-        for plane in range(GROUP):
-            here = pl.ds(pl.multiple_of((step * GROUP + plane) * channels, channels), channels)
-            weights = []
-            for head in range(heads):
-                own_scores = scores[plane][planes * head : planes * (head + 1)]
-                own_weights = jnp.exp2(own_scores - jnp.max(own_scores, axis=0, keepdims=True))
-                weights.append(own_weights * (1.0 / jnp.sum(own_weights, axis=0, keepdims=True)))
-            spread = []
-            for other in range(planes):
-                wide = jnp.concatenate(
-                    [
-                        jnp.broadcast_to(weights[head][other : other + 1], (head_size, 256)).astype(jnp.bfloat16)
-                        for head in range(heads)
-                    ],
-                    axis=0,
-                )
-                spread.append(wide * value_ref[channels * other : channels * (other + 1), :])
-            after.append(planar_ref[here, :] + product(mix_ref[...], jnp.concatenate(spread, axis=0)))
-        after = jnp.concatenate(after, axis=1)
-        mixed = column_feed_forward(after, up_ref[1], down_ref[1])
-        for plane in range(GROUP):
-            one = mixed[:, 256 * plane : 256 * plane + 128]
-            two = mixed[:, 256 * plane + 128 : 256 * plane + 256]
-            result_ref[2 * (step * GROUP + plane)] = jnp.where(own, one, two).astype(jnp.bfloat16)
-            result_ref[2 * (step * GROUP + plane) + 1] = jnp.where(own, two, one).astype(jnp.bfloat16)
-        return carry
-
-    lax.fori_loop(0, planes // GROUP, lateral, 0)
-    lax.fori_loop(0, planes // GROUP, axial, 0)
+            spread.append(wide * value_ref[rows_of(other), :])
+        held[plane]["x"] = planar_ref[rows_of(plane), :] + product(mix_ref[...], jnp.concatenate(spread, axis=0))
+
+    def store(plane):
+        mixed = held[plane].pop("x").astype(jnp.bfloat16)
+        one, two = mixed[:, :128], mixed[:, 128:]
+        result_ref[2 * plane] = jnp.where(own, one, two)
+        result_ref[2 * plane + 1] = jnp.where(own, two, one)
+
+    members = list(range(planes))
+    lateral = [load, norm, lateral_qkv, lateral_scores, lateral_weights, lateral_values, lateral_out]
+    lateral += [norm, raised(0), gelu, lowered(0), norm, axial_qkv]
+    axial = [axial_scores, axial_weights, axial_values, norm, raised(1), gelu, lowered(1), store]
+    in_waves(lateral, members, TOGETHER, LAG)
+    in_waves(axial, members, TOGETHER, LAG)
 
 
 def pack(rows, windows, channels):
     return pl.pallas_call(
         pack_kernel,
         out_shape=jax.ShapeDtypeStruct((windows, channels, 128), jnp.bfloat16),
+        compiler_params=pltpu.CompilerParams(vmem_limit_bytes=16 * 1024 * 1024),
         name="pack_windows",
     )(rows)
 
@@ -353,6 +400,7 @@
     return pl.pallas_call(
         unpack_kernel,
         out_shape=jax.ShapeDtypeStruct((rows, width), jnp.bfloat16),
+        compiler_params=pltpu.CompilerParams(vmem_limit_bytes=16 * 1024 * 1024),
         name="unpack_windows",
     )(packed)
 
@@ -407,10 +455,10 @@
     is_query = jnp.arange(3 * channels, dtype=jnp.int32) < channels
     scale = jnp.where(is_query, LOG2E * (channels // heads) ** (-0.5), 1.0)[None, :]
     qkv = jnp.stack([folded(norm_gains[0], qkv_weight[0], scale), folded(norm_gains[2], qkv_weight[1], scale)])
-    up = jnp.stack([folded(norm_gains[1], up_weight[0], 0.5), folded(norm_gains[3], up_weight[1], 0.5)])
+    up = jnp.stack([folded(norm_gains[1], up_weight[0], GELU_IN), folded(norm_gains[3], up_weight[1], GELU_IN)])
     out = out_weight[0].T
     mix = jnp.tile(out_weight[1].T, (1, planes))
-    down = jnp.transpose(down_weight, (0, 2, 1))
+    down = (jnp.transpose(down_weight, (0, 2, 1)).astype(jnp.float32) * GELU_OUT).astype(jnp.bfloat16)
     row = jnp.arange(heads * planes, dtype=jnp.int32)[:, None]
     column = jnp.arange(planes * channels, dtype=jnp.int32)[None, :]
     gather = (

time: 44.8 us -> 43.7 us (0.975)
  Pallas kernels: 9 us -> 7 us
  local copies, waits for them, and re-layouts: 4.61 us -> 6.19 us
  waiting for transfers between devices: 6.7 us -> 6.07 us
    unnamed x17 -> x19, local copies, waits for them, and re-layouts: 3.38 us -> 4.97 us
    pallas_call x1, Pallas kernels: 2.08 us -> 1.09 us  [unpack(): pl.pallas_call(unpack_kernel, out_shape=jax.ShapeDtypeStruct((rows, width...]
    pallas_call x1, Pallas kernels: 2.33 us -> 1.33 us  [pack(): pl.pallas_call(pack_kernel, out_shape=jax.ShapeDtypeStruct((windows, chan...]
    all_to_all x1, waiting for transfers between devices: 6.7 us -> 6.07 us  [window_body(): lax.all_to_all(packed, ('gz', 'tile'), split_axis=0, concat_axis=0, tiled...]
where the time goes in v3:
time: 43.7 us; the launch traced here: 43.2 us
  blocking collectives  15.5 us (35%)
  starting transfers between devices  7.49 us (17%)
  Pallas kernels  7 us (16%)
  local copies, waits for them, and re-layouts  6.19 us (14%)
  waiting for transfers between devices  6.07 us (14%)
  other arithmetic  0.69 us (2%)
    all_to_all x1, blocking collectives, window_body(): lax.all_to_all(mixed, ('gz', 'tile'), split_axis=0, concat_axis=0, tiled=...  15.5 us
    all_to_all x1, starting transfers between devices, window_body(): lax.all_to_all(packed, ('gz', 'tile'), split_axis=0, concat_axis=0, tiled...  7.49 us
    all_to_all x1, waiting for transfers between devices, window_body(): lax.all_to_all(packed, ('gz', 'tile'), split_axis=0, concat_axis=0, tiled...  6.07 us
    unnamed x19, local copies, waits for them, and re-layouts  4.97 us
    pallas_call x1, Pallas kernels, blocks(): pl.pallas_call(blocks_kernel, out_shape=jax.ShapeDtypeStruct(tokens.shape...  4.59 us
    pallas_call x1, Pallas kernels, pack(): pl.pallas_call(pack_kernel, out_shape=jax.ShapeDtypeStruct((windows, chan...  1.33 us
    pallas_call x1, Pallas kernels, unpack(): pl.pallas_call(unpack_kernel, out_shape=jax.ShapeDtypeStruct((rows, width...  1.09 us
  transfers between devices with their start and end apart: 1, of which 1 were waited for; matrix products, arithmetic and copies ran while one was open for 6% of the time, Pallas kernels for 0%

profile of v3, /device:TPU:0, one launch (start us, length us, event | category | flops | bytes accessed | tf_op | source)
XLA Modules:
  0.0 43.2 jit_solution(5363796748944150751)
XLA Ops:
  0.0 0.0 copy-start
  0.0 1.0 %copy-done = bf16[1,16,12288]{2,1,0:T(8,128)(2,1)S(1)} copy-done((bf16[1,16,12288]{2,1,0:T(8,128)(2,1)S(1)}, bf16[1,16,12288]{2,1,0:T(8,128)(2,1)}, u32[]{:S(2)}) %copy-start) | copy-done | bytes 393240
  1.0 1.3 %pack_windows.1 = bf16[16,96,128]{2,1,0:T(8,128)(2,1)} custom-call(bf16[16,12288]{1,0:T(8,128)(2,1)S(1)} %bitcast.59), custom_call_target="tpu_custom_call" | custom-call | tf_op jit(solution)/shard_map/pack_windows/pallas_call | solution.py:391
  2.3 0.0 copy-start.1
  2.3 7.5 %all-to-all-start = ((bf16[16,96,128]{2,1,0:T(8,128)(2,1)}), bf16[16,96,128]{2,1,0:T(8,128)(2,1)S(1)}, u32[]{:S(2)}, u32[]{:S(2)}) async-start(bf16[16,96,128]{2,1,0:T(8,128)(2,1)} %pack_windows.1), calls=%async_computation | async-start | bytes 786432 | tf_op jit(solution)/shard_map/all_to_all | solution.py:453
  9.9 0.0 copy-start.6
  9.9 0.7 %copy-done.6 = f32[4,96]{1,0:T(4,128)S(1)} copy-done((f32[4,96]{1,0:T(4,128)S(1)}, f32[4,96]{1,0:T(4,128)}, u32[]{:S(2)}) %copy-start.6) | copy-done | bytes 1560
  10.6 0.0 copy-done.1
  10.6 0.0 copy-start.2
  10.6 0.1 copy.26
  10.7 0.1 copy.27
  10.8 0.6 %copy-done.2 = bf16[2,96,288]{2,1,0:T(8,128)(2,1)S(1)} copy-done((bf16[2,96,288]{2,1,0:T(8,128)(2,1)S(1)}, bf16[2,96,288]{2,1,0:T(8,128)(2,1)}, u32[]{:S(2)}) %copy-start.2) | copy-done | bytes 110616
  11.5 0.1 copy.23
  11.6 0.0 copy-start.4
  11.6 0.1 copy.24
  11.8 0.8 %copy-done.4 = f32[3,64,64]{2,1,0:T(8,128)S(1)} copy-done((f32[3,64,64]{2,1,0:T(8,128)S(1)}, f32[3,64,64]{2,1,0:T(8,128)}, u32[]{:S(2)}) %copy-start.4) | copy-done | bytes 49176
  12.5 0.2 mul.103
  12.8 0.3 copy.15
  13.1 0.3 mul.105
  13.3 0.0 copy-start.5
  13.4 0.1 copy.16
  13.5 0.1 broadcast_compare_fusion
  13.5 0.6 %copy-done.5 = bf16[2,96,96]{2,1,0:T(8,128)(2,1)S(1)} copy-done((bf16[2,96,96]{2,1,0:T(8,128)(2,1)S(1)}, bf16[2,96,96]{2,1,0:T(8,128)(2,1)}, u32[]{:S(2)}) %copy-start.5) | copy-done | bytes 36888
  14.2 0.1 fusion.11
  14.3 0.1 compare_and_fusion
  14.5 0.1 fusion.9
  14.5 0.1 copy.20
  14.7 0.2 tile.10.mix_ref
  14.9 0.1 copy.25
  15.0 0.0 copy-start.3
  15.0 0.1 maximum_maximum_fusion.bias_ref
  15.2 0.1 and_convert_fusion.gather_ref
  15.2 0.7 %copy-done.3 = bf16[2,384,96]{1,2,0:T(8,128)(2,1)S(1)} copy-done((bf16[2,384,96]{1,2,0:T(8,128)(2,1)S(1)}, bf16[2,384,96]{1,2,0:T(8,128)(2,1)}, u32[]{:S(2)}) %copy-start.3) | copy-done | bytes 147480
  16.0 6.1 %all-to-all-done.tokens_ref = bf16[16,96,128]{2,1,0:T(8,128)(2,1)S(1)} async-done(((bf16[16,96,128]{2,1,0:T(8,128)(2,1)}), bf16[16,96,128]{2,1,0:T(8,128)(2,1)S(1)}, u32[]{:S(2)}, u32[]{:S(2)}) %all-to-all-start) | async-done | bytes 393248 | tf_op jit(solution)/shard_map/all_to_all | solution.py:453
  22.0 4.6 %both_blocks.1 = bf16[16,96,128]{2,1,0:T(8,128)(2,1)S(1)} custom-call(bf16[16,96,128]{2,1,0:T(8,128)(2,1)S(1)} %all-to-all-done.tokens_ref, f32[2,192,128]{2,1,0:T(8,128)S(1)} %maximum_maximum_fusion.bias_ref, bf16[2,288,96]{2,1,0:T(8,128)(2,1)S(1)} %pad_maximum_fusion.1.qkv_ref, bf16[96,96]{1,0:T(8,128)(2,1)S(1)} %bitcast.60, ...), custom_call_target="tpu_custom_call" | custom-call | tf_op jit(solution)/shard_map/both_blocks/pallas_call | solution.py:411
  26.6 15.5 %all_to_all.10.packed_ref = bf16[16,96,128]{2,1,0:T(8,128)(2,1)S(1)} all-to-all(bf16[16,96,128]{2,1,0:T(8,128)(2,1)S(1)} %both_blocks.1), channel_id=1, replica_groups=mesh['groups'=2,'gz'=8,'tile'=2] {'gz','tile'}, dimensions={0} | all-to-all | bytes 786432 | tf_op jit(solution)/shard_map/all_to_all | solution.py:468
  42.1 1.1 %unpack_windows.1 = bf16[16,12288]{1,0:T(8,128)(2,1)} custom-call(bf16[16,96,128]{2,1,0:T(8,128)(2,1)S(1)} %all_to_all.10.packed_ref), custom_call_target="tpu_custom_call" | custom-call | tf_op jit(solution)/shard_map/unpack_windows/pallas_call | solution.py:400
  (17 shorter events, 0.3 us)
Async XLA Ops:
  0.0 1.0 %copy-start = (bf16[1,16,12288]{2,1,0:T(8,128)(2,1)S(1)}, bf16[1,16,12288]{2,1,0:T(8,128)(2,1)}, u32[]{:S(2)}) copy-start(bf16[1,16,12288]{2,1,0:T(8,128)(2,1)} %param.7) | copy-start | bytes 1179652
  2.3 8.2 %copy-start.1 = (bf16[2,96,384]{2,1,0:T(8,128)(2,1)S(1)}, bf16[2,96,384]{2,1,0:T(8,128)(2,1)}, u32[]{:S(2)}) copy-start(bf16[2,96,384]{2,1,0:T(8,128)(2,1)} %param.11) | copy-start | bytes 442372
  2.3 19.7 %all-to-all-start = ((bf16[16,96,128]{2,1,0:T(8,128)(2,1)}), bf16[16,96,128]{2,1,0:T(8,128)(2,1)S(1)}, u32[]{:S(2)}, u32[]{:S(2)}) async-start(bf16[16,96,128]{2,1,0:T(8,128)(2,1)} %pack_windows.1), calls=%async_computation | async-start | bytes 786432 | tf_op jit(solution)/shard_map/all_to_all | solution.py:453
  9.9 0.7 %copy-start.6 = (f32[4,96]{1,0:T(4,128)S(1)}, f32[4,96]{1,0:T(4,128)}, u32[]{:S(2)}) copy-start(f32[4,96]{1,0:T(4,128)} %param.8) | copy-start | bytes 4612
  10.6 0.9 %copy-start.2 = (bf16[2,96,288]{2,1,0:T(8,128)(2,1)S(1)}, bf16[2,96,288]{2,1,0:T(8,128)(2,1)}, u32[]{:S(2)}) copy-start(bf16[2,96,288]{2,1,0:T(8,128)(2,1)} %param.9) | copy-start | bytes 331780
  11.6 0.9 %copy-start.4 = (f32[3,64,64]{2,1,0:T(8,128)S(1)}, f32[3,64,64]{2,1,0:T(8,128)}, u32[]{:S(2)}) copy-start(f32[3,64,64]{2,1,0:T(8,128)} %param.13) | copy-start | bytes 147460
  13.3 0.8 %copy-start.5 = (bf16[2,96,96]{2,1,0:T(8,128)(2,1)S(1)}, bf16[2,96,96]{2,1,0:T(8,128)(2,1)}, u32[]{:S(2)}) copy-start(bf16[2,96,96]{2,1,0:T(8,128)(2,1)} %param.10) | copy-start | bytes 110596
  15.0 0.9 %copy-start.3 = (bf16[2,384,96]{1,2,0:T(8,128)(2,1)S(1)}, bf16[2,384,96]{1,2,0:T(8,128)(2,1)}, u32[]{:S(2)}) copy-start(bf16[2,384,96]{1,2,0:T(8,128)(2,1)} %param.12) | copy-start | bytes 442372

commit v4 on v3

--- a/solution.py
+++ b/solution.py
@@ -1,5 +1,6 @@
 import jax
 import jax.numpy as jnp
+import numpy as np
 from jax import lax
 from jax.experimental import pallas as pl
 from jax.experimental.pallas import tpu as pltpu
@@ -164,6 +165,10 @@
 GELU_OUT = 0.5 / GELU_IN
 
 
+def across(left, right):
+    return lax.dot_general(left, right, (((1,), (1,)), ((), ())), preferred_element_type=jnp.float32)
+
+
 def gated(scaled):
     scaled = scaled.astype(jnp.bfloat16)
     return scaled + scaled * jnp.tanh(scaled * (GELU_LINEAR + scaled * scaled))
@@ -211,29 +216,25 @@
             volume_ref[:, :half] = rows[:, half:]
 
 
-TOGETHER = 8
-LAG = 1
-
-
-def in_waves(stages, members, together, lag):
-    groups = [members[start : start + together] for start in range(0, len(members), together)]
-    for step in range(len(stages) + lag * (len(groups) - 1)):
-        for index, group in enumerate(groups):
-            if 0 <= step - lag * index < len(stages):
-                for member in group:
-                    stages[step - lag * index](member)
+def in_lockstep(stages, planes):
+    for stage in stages:
+        for plane in range(planes):
+            stage(plane)
 
 
 def blocks_kernel(
     tokens_ref,
-    bias_ref,
-    qkv_ref,
-    out_ref,
-    mix_ref,
-    up_ref,
-    down_ref,
+    gains_ref,
+    qkv_weight_ref,
+    out_weight_ref,
+    up_weight_ref,
+    down_weight_ref,
+    window_bias_ref,
+    order_ref,
+    placed_order_ref,
     gather_ref,
     result_ref,
+    bias_ref,
     planar_ref,
     query_ref,
     key_ref,
@@ -241,13 +242,47 @@
 ):
     channels = tokens_ref.shape[1]
     planes = tokens_ref.shape[0] // 2
-    heads = bias_ref.shape[1] // 64
+    heads = window_bias_ref.shape[0] // 64
     head_size = channels // heads
     lane = lax.broadcasted_iota(jnp.int32, (1, 128), 1)
     own = (lane < 64) | (lane % 8 < 4)
     first = lane < 64
     blank = jnp.zeros((128 - channels, 128), jnp.bfloat16)
     blank_rows = jnp.zeros((128 - channels, 128), jnp.float32)
+
+    def turned(ref, layer):
+        return ref[layer].astype(jnp.float32).T
+
+    def gain(norm, scale):
+        return gains_ref[norm : norm + 1, :] * scale
+
+    def turned_qkv(layer):
+        matrix = turned(qkv_weight_ref, layer)
+        queries = matrix[:channels] * gain(2 * layer, LOG2E * head_size ** (-0.5))
+        return jnp.concatenate([queries, matrix[channels:] * gain(2 * layer, 1.0)], axis=0).astype(jnp.bfloat16)
+
+    qkv = [turned_qkv(layer) for layer in range(2)]
+    up = [(turned(up_weight_ref, layer) * gain(2 * layer + 1, GELU_IN)).astype(jnp.bfloat16) for layer in range(2)]
+    down = [(down_weight_ref[layer].astype(jnp.float32) * GELU_OUT).astype(jnp.bfloat16) for layer in range(2)]
+    out = turned(out_weight_ref, 0).astype(jnp.bfloat16)
+    mix = jnp.concatenate([turned(out_weight_ref, 1).astype(jnp.bfloat16)] * planes, axis=1)
+
+    high = window_bias_ref[...].astype(jnp.bfloat16)
+    low = (window_bias_ref[...] - high.astype(jnp.float32)).astype(jnp.bfloat16)
+    parts = [across(order_ref[...], part).astype(jnp.bfloat16) for part in (high, low)]
+    position = lax.axis_index("gz") * lax.axis_size("tile") + lax.axis_index("tile")
+    last = position == lax.axis_size("gz") * lax.axis_size("tile") - 1
+    key_row = lax.broadcasted_iota(jnp.int32, (64, 128), 0)
+    query_lane = lax.broadcasted_iota(jnp.int32, (64, 128), 1)
+    column_cut = ((key_row < 32) != (query_lane % 64 < 32)) & last
+    row_cut = ((key_row % 8 < 4) != (query_lane % 8 < 4)) & (query_lane >= 64)
+    for head in range(heads):
+        placed = placed_order_ref[128 * head : 128 * (head + 1), :]
+        plain = (across(parts[0], placed) + across(parts[1], placed)) * LOG2E
+        plain = jnp.where(column_cut, -jnp.inf, plain)
+        bias_ref[0, 64 * head : 64 * (head + 1), :] = plain
+        bias_ref[1, 64 * head : 64 * (head + 1), :] = jnp.where(row_cut, -jnp.inf, plain)
+
     held = [{} for _ in range(planes)]
 
     def rows_of(plane):
@@ -262,7 +297,7 @@
         held[plane]["n"] = normalised(held[plane]["x"])
 
     def lateral_qkv(plane):
-        packed = product(qkv_ref[0], held[plane].pop("n"))
+        packed = product(qkv[0], held[plane].pop("n"))
         held[plane]["q"] = packed[:channels]
         held[plane]["k"] = packed[channels : 2 * channels]
         held[plane]["v"] = packed[2 * channels :].astype(jnp.bfloat16)
@@ -321,11 +356,11 @@
         held[plane]["a"] = jnp.concatenate(attended, axis=1)
 
     def lateral_out(plane):
-        held[plane]["x"] = held[plane]["x"] + product(out_ref[...], held[plane].pop("a"))
+        held[plane]["x"] = held[plane]["x"] + product(out, held[plane].pop("a"))
 
     def raised(layer):
         def stage(plane):
-            held[plane]["h"] = product(up_ref[layer], held[plane].pop("n"))
+            held[plane]["h"] = product(up[layer], held[plane].pop("n"))
 
         return stage
 
@@ -334,12 +369,12 @@
 
     def lowered(layer):
         def stage(plane):
-            held[plane]["x"] = held[plane]["x"] + product(down_ref[layer], held[plane].pop("g"))
+            held[plane]["x"] = held[plane]["x"] + product(down[layer], held[plane].pop("g"))
 
         return stage
 
     def axial_qkv(plane):
-        packed = product(qkv_ref[1], held[plane].pop("n")).astype(jnp.bfloat16)
+        packed = product(qkv[1], held[plane].pop("n")).astype(jnp.bfloat16)
         planar_ref[rows_of(plane), :] = held[plane].pop("x")
         query_ref[rows_of(plane), :] = packed[:channels]
         key_ref[rows_of(plane), :] = packed[channels : 2 * channels]
@@ -371,7 +406,7 @@
                 axis=0,
             )
             spread.append(wide * value_ref[rows_of(other), :])
-        held[plane]["x"] = planar_ref[rows_of(plane), :] + product(mix_ref[...], jnp.concatenate(spread, axis=0))
+        held[plane]["x"] = planar_ref[rows_of(plane), :] + product(mix, jnp.concatenate(spread, axis=0))
 
     def store(plane):
         mixed = held[plane].pop("x").astype(jnp.bfloat16)
@@ -379,12 +414,10 @@
         result_ref[2 * plane] = jnp.where(own, one, two)
         result_ref[2 * plane + 1] = jnp.where(own, two, one)
 
-    members = list(range(planes))
     lateral = [load, norm, lateral_qkv, lateral_scores, lateral_weights, lateral_values, lateral_out]
     lateral += [norm, raised(0), gelu, lowered(0), norm, axial_qkv]
     axial = [axial_scores, axial_weights, axial_values, norm, raised(1), gelu, lowered(1), store]
-    in_waves(lateral, members, TOGETHER, LAG)
-    in_waves(axial, members, TOGETHER, LAG)
+    in_lockstep(lateral + axial, planes)
 
 
 def pack(rows, windows, channels):
@@ -408,10 +441,12 @@
 def blocks(tokens, *operands):
     sources, channels, _ = tokens.shape
     rows = sources // 2 * channels
+    heads = operands[5].shape[0] // 64
     return pl.pallas_call(
         blocks_kernel,
         out_shape=jax.ShapeDtypeStruct(tokens.shape, jnp.bfloat16),
         scratch_shapes=[
+            pltpu.VMEM((2, heads * 64, 128), jnp.float32),
             pltpu.VMEM((rows, 256), jnp.float32),
             pltpu.VMEM((rows, 256), jnp.bfloat16),
             pltpu.VMEM((rows, 256), jnp.bfloat16),
@@ -422,23 +457,18 @@
     )(tokens, *operands)
 
 
-def pair_bias(window_bias, last):
-    heads = window_bias.shape[0]
-    split = window_bias.reshape(heads, 8, 8, 8, 8).transpose(0, 4, 3, 2, 1).reshape(heads, 64, 64) * LOG2E
-    index = jnp.arange(64, dtype=jnp.int32)
-    column_side = (index // 8 < 4).astype(jnp.int32)
-    row_side = (index % 8 < 4).astype(jnp.int32)
-    column_cut = (column_side[:, None] != column_side[None, :]) & last
-    row_cut = row_side[:, None] != row_side[None, :]
-    plain = jnp.where(column_cut[None], -jnp.inf, split)
-    cut = jnp.where(row_cut[None], -jnp.inf, plain)
-    one = jnp.concatenate([plain, plain], axis=2).reshape(heads * 64, 128)
-    two = jnp.concatenate([plain, cut], axis=2).reshape(heads * 64, 128)
-    return jnp.stack([one, two])
-
-
-def folded(gain, matrix, scale):
-    return (gain[:, None] * matrix.astype(jnp.float32) * scale).T.astype(jnp.bfloat16)
+def constants(heads, channels, planes):
+    order = np.zeros((64, 64), np.float32)
+    index = np.arange(64)
+    order[index, index % 8 * 8 + index // 8] = 1.0
+    placed = np.zeros((heads, 2, 64, heads, 64), np.float32)
+    for head in range(heads):
+        placed[head, :, :, head, :] = order
+    row = np.arange(heads * planes)[:, None]
+    column = np.arange(planes * channels)[None, :]
+    gather = (row // planes == column % channels // (channels // heads)) & (row % planes == column // channels)
+    placed = placed.reshape(heads * 128, heads * 64)
+    return order.astype(jnp.bfloat16), placed.astype(jnp.bfloat16), gather.astype(jnp.bfloat16)
 
 
 def window_body(volume, norm_gains, qkv_weight, out_weight, up_weight, down_weight, window_bias):
@@ -448,23 +478,21 @@
     heads = window_bias.shape[0]
     planes = lax.axis_size("gz")
     windows = width // channels // 8
-    position = lax.axis_index("gz") * lax.axis_size("tile") + lax.axis_index("tile")
     packed = pack(volume.reshape(rows, width), windows, channels)
     tokens = lax.all_to_all(packed, ("gz", "tile"), split_axis=0, concat_axis=0, tiled=True)
-    bias = pair_bias(window_bias, position == windows - 1)
-    is_query = jnp.arange(3 * channels, dtype=jnp.int32) < channels
-    scale = jnp.where(is_query, LOG2E * (channels // heads) ** (-0.5), 1.0)[None, :]
-    qkv = jnp.stack([folded(norm_gains[0], qkv_weight[0], scale), folded(norm_gains[2], qkv_weight[1], scale)])
-    up = jnp.stack([folded(norm_gains[1], up_weight[0], GELU_IN), folded(norm_gains[3], up_weight[1], GELU_IN)])
-    out = out_weight[0].T
-    mix = jnp.tile(out_weight[1].T, (1, planes))
-    down = (jnp.transpose(down_weight, (0, 2, 1)).astype(jnp.float32) * GELU_OUT).astype(jnp.bfloat16)
-    row = jnp.arange(heads * planes, dtype=jnp.int32)[:, None]
-    column = jnp.arange(planes * channels, dtype=jnp.int32)[None, :]
-    gather = (
-        (row // planes == column % channels // (channels // heads)) & (row % planes == column // channels)
-    ).astype(jnp.bfloat16)
-    mixed = blocks(tokens, bias, qkv, out, mix, up, down, gather)
+    order, placed_order, gather = constants(heads, channels, planes)
+    mixed = blocks(
+        tokens,
+        norm_gains,
+        qkv_weight,
+        out_weight,
+        up_weight,
+        jnp.transpose(down_weight, (0, 2, 1)),
+        window_bias.reshape(heads * 64, 64),
+        order,
+        placed_order,
+        gather,
+    )
     returned = lax.all_to_all(mixed, ("gz", "tile"), split_axis=0, concat_axis=0, tiled=True)
     return unpack(returned, rows, width).reshape(1, rows, width)
 

time: 43.7 us -> 43.4 us (level)
  blocking collectives: 15.5 us -> 35 us
  starting transfers between devices: 7.49 us -> 0 us
  waiting for transfers between devices: 6.07 us -> 0 us
  local copies, waits for them, and re-layouts: 6.19 us -> 1.66 us
  other arithmetic: 0.69 us -> 0 us
  Pallas kernels: 7 us -> 6.42 us
    all_to_all x0 -> x1, blocking collectives: none -> 19.5 us  [window_body(): lax.all_to_all(packed, ('gz', 'tile'), split_axis=0, concat_axis=0, tiled...]
    all_to_all x1 -> x0, starting transfers between devices: 7.49 us -> none  [window_body(): lax.all_to_all(packed, ('gz', 'tile'), split_axis=0, concat_axis=0, tiled...]
    all_to_all x1 -> x0, waiting for transfers between devices: 6.07 us -> none  [window_body(): lax.all_to_all(packed, ('gz', 'tile'), split_axis=0, concat_axis=0, tiled...]
    unnamed x19 -> x20, local copies, waits for them, and re-layouts: 4.97 us -> 1.66 us
    mul x5 -> x0, local copies, waits for them, and re-layouts: 0.87 us -> none  [the longest x4 0.86 us: pair_bias(): window_bias.reshape(heads, 8, 8, 8, 8).transpose(0, 4, 3, 2, 1)]
    pallas_call x1, Pallas kernels: 1.33 us -> 0.58 us  [pack(): pl.pallas_call(pack_kernel, out_shape=jax.ShapeDtypeStruct((windows, chan...]
  transfers between devices with their start and end apart: 1 -> 0, of which waited for: 1 -> 0; matrix products, arithmetic and copies ran while one was open for 6% -> 0% of each run, Pallas kernels for 0% -> 0%
where the time goes in v4:
time: 43.4 us; the launch traced here: 43.2 us
  blocking collectives  35 us (81%)
  Pallas kernels  6.42 us (15%)
  local copies, waits for them, and re-layouts  1.66 us (4%)
    all_to_all x1, blocking collectives, window_body(): lax.all_to_all(packed, ('gz', 'tile'), split_axis=0, concat_axis=0, tiled...  19.5 us
    all_to_all x1, blocking collectives, window_body(): lax.all_to_all(mixed, ('gz', 'tile'), split_axis=0, concat_axis=0, tiled=...  15.5 us
    pallas_call x1, Pallas kernels, blocks(): pl.pallas_call(blocks_kernel, out_shape=jax.ShapeDtypeStruct(tokens.shape...  4.75 us
    unnamed x20, local copies, waits for them, and re-layouts  1.66 us
    pallas_call x1, Pallas kernels, unpack(): pl.pallas_call(unpack_kernel, out_shape=jax.ShapeDtypeStruct((rows, width...  1.09 us

profile of v4, /device:TPU:0, one launch (start us, length us, event | category | flops | bytes accessed | tf_op | source)
XLA Modules:
  0.0 43.2 jit_solution(9039994348366322940)
XLA Ops:
  0.0 0.0 copy-start
  0.0 1.0 %copy-done = bf16[1,16,12288]{2,1,0:T(8,128)(2,1)S(1)} copy-done((bf16[1,16,12288]{2,1,0:T(8,128)(2,1)S(1)}, bf16[1,16,12288]{2,1,0:T(8,128)(2,1)}, u32[]{:S(2)}) %copy-start) | copy-done | bytes 393240
  1.0 0.0 copy-start.7
  1.0 0.0 copy-start.8
  1.0 0.6 %pack_windows.1 = bf16[16,96,128]{2,1,0:T(8,128)(2,1)S(1)} custom-call(bf16[16,12288]{1,0:T(8,128)(2,1)S(1)} %bitcast.4), custom_call_target="tpu_custom_call" | custom-call | tf_op jit(solution)/shard_map/pack_windows/pallas_call | solution.py:424
  1.6 0.0 copy-start.1
  1.6 0.0 copy-start.2
  1.6 0.0 copy-start.3
  1.6 0.0 copy-start.4
  1.6 0.0 copy-start.5
  1.6 0.0 copy-start.6
  1.7 19.5 %all_to_all.10.tokens_ref = bf16[16,96,128]{2,1,0:T(8,128)(2,1)S(1)} all-to-all(bf16[16,96,128]{2,1,0:T(8,128)(2,1)S(1)} %pack_windows.1), channel_id=1, replica_groups=mesh['groups'=2,'gz'=8,'tile'=2] {'gz','tile'}, dimensions={0} | all-to-all | bytes 786432 | tf_op jit(solution)/shard_map/all_to_all | solution.py:482
  21.1 0.0 copy-start.9
  21.1 0.0 copy-done.7
  21.2 0.0 copy-done.8
  21.2 0.0 copy-done.1
  21.2 0.0 copy-done.2
  21.2 0.0 copy-done.3
  21.2 0.0 copy-done.4
  21.2 0.0 copy-done.5
  21.2 0.0 copy-done.6
  21.2 0.6 %copy-done.9 = f32[4,96]{1,0:T(4,128)S(1)} copy-done((f32[4,96]{1,0:T(4,128)S(1)}, f32[4,96]{1,0:T(4,128)}, u32[]{:S(2)}) %copy-start.9) | copy-done | bytes 1560
  21.8 4.8 %both_blocks.1 = bf16[16,96,128]{2,1,0:T(8,128)(2,1)S(1)} custom-call(bf16[16,96,128]{2,1,0:T(8,128)(2,1)S(1)} %all_to_all.10.tokens_ref, f32[4,96]{1,0:T(4,128)S(1)} %copy-done.9, bf16[2,96,288]{2,1,0:T(8,128)(2,1)S(1)} %copy-done.2, bf16[2,96,96]{2,1,0:T(8,128)(2,1)S(1)} %copy-done.6, bf16[2,96,384]{2,1,0:T(8,128)(2,1)S(1)} %copy-done.3, ...), custom_call_target="tpu_custom_call" | custom-call | tf_op jit(solution)/shard_map/both_blocks/pallas_call | solution.py:445
  26.6 15.5 %all_to_all.11.packed_ref = bf16[16,96,128]{2,1,0:T(8,128)(2,1)S(1)} all-to-all(bf16[16,96,128]{2,1,0:T(8,128)(2,1)S(1)} %both_blocks.1), channel_id=1, replica_groups=mesh['groups'=2,'gz'=8,'tile'=2] {'gz','tile'}, dimensions={0} | all-to-all | bytes 786432 | tf_op jit(solution)/shard_map/all_to_all | solution.py:496
  42.1 1.1 %unpack_windows.1 = bf16[16,12288]{1,0:T(8,128)(2,1)} custom-call(bf16[16,96,128]{2,1,0:T(8,128)(2,1)S(1)} %all_to_all.11.packed_ref), custom_call_target="tpu_custom_call" | custom-call | tf_op jit(solution)/shard_map/unpack_windows/pallas_call | solution.py:433
Async XLA Ops:
  0.0 1.0 %copy-start = (bf16[1,16,12288]{2,1,0:T(8,128)(2,1)S(1)}, bf16[1,16,12288]{2,1,0:T(8,128)(2,1)}, u32[]{:S(2)}) copy-start(bf16[1,16,12288]{2,1,0:T(8,128)(2,1)} %param.10) | copy-start | bytes 1179652
  1.0 20.2 %copy-start.7 = (bf16[24,768]{1,0:T(8,128)(2,1)S(1)}, bf16[24,768]{1,0:T(8,128)(2,1)}, u32[]{:S(2)}) copy-start(bf16[24,768]{1,0:T(8,128)(2,1)} %constant.8.clone.gather_ref) | copy-start | bytes 110596
  1.0 20.2 %copy-start.8 = (bf16[64,64]{1,0:T(8,128)(2,1)S(1)}, bf16[64,64]{1,0:T(8,128)(2,1)}, u32[]{:S(2)}) copy-start(bf16[64,64]{1,0:T(8,128)(2,1)} %constant.6.clone.order_ref) | copy-start | bytes 24580
  1.6 19.6 %copy-start.1 = (bf16[384,192]{1,0:T(8,128)(2,1)S(1)}, bf16[384,192]{1,0:T(8,128)(2,1)}, u32[]{:S(2)}) copy-start(bf16[384,192]{1,0:T(8,128)(2,1)} %constant.7.clone.placed_order_ref) | copy-start | bytes 442372
  1.6 19.6 %copy-start.2 = (bf16[2,96,288]{2,1,0:T(8,128)(2,1)S(1)}, bf16[2,96,288]{2,1,0:T(8,128)(2,1)}, u32[]{:S(2)}) copy-start(bf16[2,96,288]{2,1,0:T(8,128)(2,1)} %qkv_weight_ref.1) | copy-start | bytes 331780
  1.6 19.6 %copy-start.3 = (bf16[2,96,384]{2,1,0:T(8,128)(2,1)S(1)}, bf16[2,96,384]{2,1,0:T(8,128)(2,1)}, u32[]{:S(2)}) copy-start(bf16[2,96,384]{2,1,0:T(8,128)(2,1)} %up_weight_ref.1) | copy-start | bytes 442372
  1.6 19.6 %copy-start.4 = (bf16[2,384,96]{1,2,0:T(8,128)(2,1)S(1)}, bf16[2,384,96]{1,2,0:T(8,128)(2,1)}, u32[]{:S(2)}) copy-start(bf16[2,384,96]{1,2,0:T(8,128)(2,1)} %param.15) | copy-start | bytes 442372
  1.6 19.6 %copy-start.5 = (f32[3,64,64]{2,1,0:T(8,128)S(1)}, f32[3,64,64]{2,1,0:T(8,128)}, u32[]{:S(2)}) copy-start(f32[3,64,64]{2,1,0:T(8,128)} %param.16) | copy-start | bytes 147460
  1.6 19.6 %copy-start.6 = (bf16[2,96,96]{2,1,0:T(8,128)(2,1)S(1)}, bf16[2,96,96]{2,1,0:T(8,128)(2,1)}, u32[]{:S(2)}) copy-start(bf16[2,96,96]{2,1,0:T(8,128)(2,1)} %out_weight_ref.1) | copy-start | bytes 110596
  21.1 0.7 %copy-start.9 = (f32[4,96]{1,0:T(4,128)S(1)}, f32[4,96]{1,0:T(4,128)}, u32[]{:S(2)}) copy-start(f32[4,96]{1,0:T(4,128)} %gains_ref.1) | copy-start | bytes 4612

commit v5 on v4

--- a/solution.py
+++ b/solution.py
@@ -231,8 +231,6 @@
     down_weight_ref,
     window_bias_ref,
     order_ref,
-    placed_order_ref,
-    gather_ref,
     result_ref,
     bias_ref,
     planar_ref,
@@ -265,11 +263,17 @@
     up = [(turned(up_weight_ref, layer) * gain(2 * layer + 1, GELU_IN)).astype(jnp.bfloat16) for layer in range(2)]
     down = [(down_weight_ref[layer].astype(jnp.float32) * GELU_OUT).astype(jnp.bfloat16) for layer in range(2)]
     out = turned(out_weight_ref, 0).astype(jnp.bfloat16)
-    mix = jnp.concatenate([turned(out_weight_ref, 1).astype(jnp.bfloat16)] * planes, axis=1)
+    mix = jnp.concatenate([turned(out_weight_ref, 1).astype(jnp.bfloat16)] * 2, axis=1)
+
+    shape = (heads * planes, planes * channels // 2)
+    row = lax.broadcasted_iota(jnp.int32, shape, 0)
+    column = lax.broadcasted_iota(jnp.int32, shape, 1)
+    mine = lax.div(column, head_size // 2) == lax.rem(row, planes) * heads + lax.div(row, planes)
+    gather = jnp.where(mine, 1.0, 0.0).astype(jnp.bfloat16)
 
     high = window_bias_ref[...].astype(jnp.bfloat16)
     low = (window_bias_ref[...] - high.astype(jnp.float32)).astype(jnp.bfloat16)
-    parts = [across(order_ref[...], part).astype(jnp.bfloat16) for part in (high, low)]
+    parts = [across(order_ref[:64, :64], part).astype(jnp.bfloat16) for part in (high, low)]
     position = lax.axis_index("gz") * lax.axis_size("tile") + lax.axis_index("tile")
     last = position == lax.axis_size("gz") * lax.axis_size("tile") - 1
     key_row = lax.broadcasted_iota(jnp.int32, (64, 128), 0)
@@ -277,7 +281,7 @@
     column_cut = ((key_row < 32) != (query_lane % 64 < 32)) & last
     row_cut = ((key_row % 8 < 4) != (query_lane % 8 < 4)) & (query_lane >= 64)
     for head in range(heads):
-        placed = placed_order_ref[128 * head : 128 * (head + 1), :]
+        placed = order_ref[128 * head : 128 * (head + 1), :]
         plain = (across(parts[0], placed) + across(parts[1], placed)) * LOG2E
         plain = jnp.where(column_cut, -jnp.inf, plain)
         bias_ref[0, 64 * head : 64 * (head + 1), :] = plain
@@ -322,7 +326,7 @@
             for head in range(heads):
                 masked = jnp.where(lane // head_size == head, key, 0.0).astype(jnp.bfloat16)
                 left.append(jnp.concatenate([masked[:64], masked[64:]], axis=1))
-            scores.append(product(jnp.concatenate(left, axis=0), right) + bias_ref[pair])
+            scores.append((jnp.concatenate(left, axis=0), right))
         held[plane]["s"] = scores
 
     def lateral_weights(plane):
@@ -342,6 +346,9 @@
                 )
                 held[plane]["w"].append((spread, 1.0 / total))
 
+    def lateral_products(plane):
+        held[plane]["s"] = [product(*held[plane]["s"][pair]) + bias_ref[pair] for pair in range(2)]
+
     def lateral_values(plane):
         weights, values = held[plane].pop("w"), held[plane].pop("v")
         attended = []
@@ -382,8 +389,15 @@
 
     def axial_scores(plane):
         query = query_ref[rows_of(plane), :]
-        pairs = jnp.concatenate([query * key_ref[rows_of(other), :] for other in range(planes)], axis=0)
-        held[plane]["s"] = product(gather_ref[...], pairs)
+        half = head_size // 2
+        pairs = []
+        for other in range(planes):
+            pair = query * key_ref[rows_of(other), :]
+            for head in range(heads):
+                top = head_size * head
+                pairs.append(pair[top : top + half] + pair[top + half : top + head_size])
+        pairs = jnp.concatenate(pairs, axis=0)
+        held[plane]["s"] = product(gather, pairs)
 
     def axial_weights(plane):
         scores = held[plane].pop("s")
@@ -406,7 +420,10 @@
                 axis=0,
             )
             spread.append(wide * value_ref[rows_of(other), :])
-        held[plane]["x"] = planar_ref[rows_of(plane), :] + product(mix, jnp.concatenate(spread, axis=0))
+        while len(spread) > 2:
+            spread = [one + two for one, two in zip(spread[::2], spread[1::2])]
+        spread = jnp.concatenate(spread, axis=0)
+        held[plane]["x"] = planar_ref[rows_of(plane), :] + product(mix, spread)
 
     def store(plane):
         mixed = held[plane].pop("x").astype(jnp.bfloat16)
@@ -414,7 +431,7 @@
         result_ref[2 * plane] = jnp.where(own, one, two)
         result_ref[2 * plane + 1] = jnp.where(own, two, one)
 
-    lateral = [load, norm, lateral_qkv, lateral_scores, lateral_weights, lateral_values, lateral_out]
+    lateral = [load, norm, lateral_qkv, lateral_scores, lateral_products, lateral_weights, lateral_values, lateral_out]
     lateral += [norm, raised(0), gelu, lowered(0), norm, axial_qkv]
     axial = [axial_scores, axial_weights, axial_values, norm, raised(1), gelu, lowered(1), store]
     in_lockstep(lateral + axial, planes)
@@ -457,18 +474,12 @@
     )(tokens, *operands)
 
 
-def constants(heads, channels, planes):
-    order = np.zeros((64, 64), np.float32)
+def token_order(heads):
     index = np.arange(64)
-    order[index, index % 8 * 8 + index // 8] = 1.0
     placed = np.zeros((heads, 2, 64, heads, 64), np.float32)
     for head in range(heads):
-        placed[head, :, :, head, :] = order
-    row = np.arange(heads * planes)[:, None]
-    column = np.arange(planes * channels)[None, :]
-    gather = (row // planes == column % channels // (channels // heads)) & (row % planes == column // channels)
-    placed = placed.reshape(heads * 128, heads * 64)
-    return order.astype(jnp.bfloat16), placed.astype(jnp.bfloat16), gather.astype(jnp.bfloat16)
+        placed[head, :, index, head, index % 8 * 8 + index // 8] = 1.0
+    return placed.reshape(heads * 128, heads * 64).astype(jnp.bfloat16)
 
 
 def window_body(volume, norm_gains, qkv_weight, out_weight, up_weight, down_weight, window_bias):
@@ -480,7 +491,6 @@
     windows = width // channels // 8
     packed = pack(volume.reshape(rows, width), windows, channels)
     tokens = lax.all_to_all(packed, ("gz", "tile"), split_axis=0, concat_axis=0, tiled=True)
-    order, placed_order, gather = constants(heads, channels, planes)
     mixed = blocks(
         tokens,
         norm_gains,
@@ -489,9 +499,7 @@
         up_weight,
         jnp.transpose(down_weight, (0, 2, 1)),
         window_bias.reshape(heads * 64, 64),
-        order,
-        placed_order,
-        gather,
+        token_order(heads),
     )
     returned = lax.all_to_all(mixed, ("gz", "tile"), split_axis=0, concat_axis=0, tiled=True)
     return unpack(returned, rows, width).reshape(1, rows, width)

time: 43.4 us -> 43.2 us (level)
    unnamed x20 -> x16, local copies, waits for them, and re-layouts: 1.66 us -> 1.67 us
where the time goes in v5:
time: 43.2 us; the launch traced here: 42.9 us
  blocking collectives  35 us (81%)
  Pallas kernels  6.17 us (14%)
  local copies, waits for them, and re-layouts  1.67 us (4%)
    all_to_all x1, blocking collectives, window_body(): lax.all_to_all(packed, ('gz', 'tile'), split_axis=0, concat_axis=0, tiled...  19.5 us
    all_to_all x1, blocking collectives, window_body(): lax.all_to_all(mixed, ('gz', 'tile'), split_axis=0, concat_axis=0, tiled=...  15.5 us
    pallas_call x1, Pallas kernels, blocks(): pl.pallas_call(blocks_kernel, out_shape=jax.ShapeDtypeStruct(tokens.shape...  4.5 us
    unnamed x16, local copies, waits for them, and re-layouts  1.67 us
    pallas_call x1, Pallas kernels, unpack(): pl.pallas_call(unpack_kernel, out_shape=jax.ShapeDtypeStruct((rows, width...  1.09 us

profile of v5, /device:TPU:0, one launch (start us, length us, event | category | flops | bytes accessed | tf_op | source)
XLA Modules:
  0.0 42.9 jit_solution(8070923620550829137)
XLA Ops:
  0.0 0.0 copy-start
  0.0 1.0 %copy-done = bf16[1,16,12288]{2,1,0:T(8,128)(2,1)S(1)} copy-done((bf16[1,16,12288]{2,1,0:T(8,128)(2,1)S(1)}, bf16[1,16,12288]{2,1,0:T(8,128)(2,1)}, u32[]{:S(2)}) %copy-start) | copy-done | bytes 393240
  1.0 0.6 %pack_windows.1 = bf16[16,96,128]{2,1,0:T(8,128)(2,1)S(1)} custom-call(bf16[16,12288]{1,0:T(8,128)(2,1)S(1)} %bitcast.4), custom_call_target="tpu_custom_call" | custom-call | tf_op jit(solution)/shard_map/pack_windows/pallas_call | solution.py:441
  1.6 0.0 copy-start.1
  1.6 0.0 copy-start.2
  1.6 0.0 copy-start.3
  1.6 0.0 copy-start.4
  1.6 0.0 copy-start.5
  1.6 0.0 copy-start.6
  1.7 19.5 %all_to_all.10.tokens_ref = bf16[16,96,128]{2,1,0:T(8,128)(2,1)S(1)} all-to-all(bf16[16,96,128]{2,1,0:T(8,128)(2,1)S(1)} %pack_windows.1), channel_id=1, replica_groups=mesh['groups'=2,'gz'=8,'tile'=2] {'gz','tile'}, dimensions={0} | all-to-all | bytes 786432 | tf_op jit(solution)/shard_map/all_to_all | solution.py:493
  21.1 0.0 copy-start.7
  21.1 0.0 copy-done.1
  21.1 0.0 copy-done.2
  21.1 0.0 copy-done.3
  21.2 0.0 copy-done.4
  21.2 0.0 copy-done.5
  21.2 0.0 copy-done.6
  21.2 0.6 %copy-done.7 = f32[4,96]{1,0:T(4,128)S(1)} copy-done((f32[4,96]{1,0:T(4,128)S(1)}, f32[4,96]{1,0:T(4,128)}, u32[]{:S(2)}) %copy-start.7) | copy-done | bytes 1560
  21.8 4.5 %both_blocks.1 = bf16[16,96,128]{2,1,0:T(8,128)(2,1)S(1)} custom-call(bf16[16,96,128]{2,1,0:T(8,128)(2,1)S(1)} %all_to_all.10.tokens_ref, f32[4,96]{1,0:T(4,128)S(1)} %copy-done.7, bf16[2,96,288]{2,1,0:T(8,128)(2,1)S(1)} %copy-done.2, bf16[2,96,96]{2,1,0:T(8,128)(2,1)S(1)} %copy-done.6, bf16[2,96,384]{2,1,0:T(8,128)(2,1)S(1)} %copy-done.3, ...), custom_call_target="tpu_custom_call" | custom-call | tf_op jit(solution)/shard_map/both_blocks/pallas_call | solution.py:462
  26.3 15.5 %all_to_all.11.packed_ref = bf16[16,96,128]{2,1,0:T(8,128)(2,1)S(1)} all-to-all(bf16[16,96,128]{2,1,0:T(8,128)(2,1)S(1)} %both_blocks.1), channel_id=1, replica_groups=mesh['groups'=2,'gz'=8,'tile'=2] {'gz','tile'}, dimensions={0} | all-to-all | bytes 786432 | tf_op jit(solution)/shard_map/all_to_all | solution.py:504
  41.9 1.1 %unpack_windows.1 = bf16[16,12288]{1,0:T(8,128)(2,1)} custom-call(bf16[16,96,128]{2,1,0:T(8,128)(2,1)S(1)} %all_to_all.11.packed_ref), custom_call_target="tpu_custom_call" | custom-call | tf_op jit(solution)/shard_map/unpack_windows/pallas_call | solution.py:450
Async XLA Ops:
  0.0 1.0 %copy-start = (bf16[1,16,12288]{2,1,0:T(8,128)(2,1)S(1)}, bf16[1,16,12288]{2,1,0:T(8,128)(2,1)}, u32[]{:S(2)}) copy-start(bf16[1,16,12288]{2,1,0:T(8,128)(2,1)} %param.8) | copy-start | bytes 1179652
  1.6 19.6 %copy-start.1 = (bf16[384,192]{1,0:T(8,128)(2,1)S(1)}, bf16[384,192]{1,0:T(8,128)(2,1)}, u32[]{:S(2)}) copy-start(bf16[384,192]{1,0:T(8,128)(2,1)} %constant.2.clone.order_ref) | copy-start | bytes 442372
  1.6 19.6 %copy-start.2 = (bf16[2,96,288]{2,1,0:T(8,128)(2,1)S(1)}, bf16[2,96,288]{2,1,0:T(8,128)(2,1)}, u32[]{:S(2)}) copy-start(bf16[2,96,288]{2,1,0:T(8,128)(2,1)} %qkv_weight_ref.1) | copy-start | bytes 331780
  1.6 19.5 %copy-start.3 = (bf16[2,96,384]{2,1,0:T(8,128)(2,1)S(1)}, bf16[2,96,384]{2,1,0:T(8,128)(2,1)}, u32[]{:S(2)}) copy-start(bf16[2,96,384]{2,1,0:T(8,128)(2,1)} %up_weight_ref.1) | copy-start | bytes 442372
  1.6 19.5 %copy-start.4 = (bf16[2,384,96]{1,2,0:T(8,128)(2,1)S(1)}, bf16[2,384,96]{1,2,0:T(8,128)(2,1)}, u32[]{:S(2)}) copy-start(bf16[2,384,96]{1,2,0:T(8,128)(2,1)} %param.13) | copy-start | bytes 442372
  1.6 19.5 %copy-start.5 = (f32[3,64,64]{2,1,0:T(8,128)S(1)}, f32[3,64,64]{2,1,0:T(8,128)}, u32[]{:S(2)}) copy-start(f32[3,64,64]{2,1,0:T(8,128)} %param.14) | copy-start | bytes 147460
  1.6 19.5 %copy-start.6 = (bf16[2,96,96]{2,1,0:T(8,128)(2,1)S(1)}, bf16[2,96,96]{2,1,0:T(8,128)(2,1)}, u32[]{:S(2)}) copy-start(bf16[2,96,96]{2,1,0:T(8,128)(2,1)} %out_weight_ref.1) | copy-start | bytes 110596
  21.1 0.7 %copy-start.7 = (f32[4,96]{1,0:T(4,128)S(1)}, f32[4,96]{1,0:T(4,128)}, u32[]{:S(2)}) copy-start(f32[4,96]{1,0:T(4,128)} %gains_ref.1) | copy-start | bytes 4612

commit v6 on v5

--- a/solution.py
+++ b/solution.py
@@ -174,16 +174,32 @@
     return scaled + scaled * jnp.tanh(scaled * (GELU_LINEAR + scaled * scaled))
 
 
-def pack_kernel(volume_ref, packed_ref):
+def run_copies(source_ref, target_ref, sems, cut):
+    width = source_ref.shape[1]
+    runs = (pl.ds(0, cut), pl.ds(cut, width - cut))
+    return [
+        pltpu.make_async_copy(source_ref.at[:, run], target_ref.at[:, run], sems.at[index])
+        for index, run in enumerate(runs)
+    ]
+
+
+def pack_kernel(volume_ref, gains_ref, packed_ref, held_gains_ref, rows_ref, sems):
     windows, channels, _ = packed_ref.shape
     width = 8 * channels
     half = width // 2
+    copies = run_copies(volume_ref, rows_ref, sems, windows // 2 * width + half)
+    copies.append(pltpu.make_async_copy(gains_ref, held_gains_ref, sems.at[2]))
+    for copy in copies:
+        copy.start()
+    copies[0].wait()
     for window in range(windows):
+        if window == windows // 2:
+            copies[1].wait()
         start = window * width + half
         if window < windows - 1:
-            chunk = volume_ref[:, start : start + width]
+            chunk = rows_ref[:, start : start + width]
         else:
-            chunk = jnp.concatenate([volume_ref[:, start:], volume_ref[:, :half]], axis=1)
+            chunk = jnp.concatenate([rows_ref[:, start:], rows_ref[:, :half]], axis=1)
         chunk = chunk.astype(jnp.float32)
         rolled = jnp.concatenate([chunk[4:], chunk[:4]], axis=0)
         pieces = [
@@ -191,15 +207,16 @@
             for part in range(2)
             for column in range(8)
         ]
-        tokens = jnp.concatenate(pieces, axis=0)
-        packed_ref[window] = tokens.T.astype(jnp.bfloat16)
-
-
-def unpack_kernel(packed_ref, volume_ref):
+        packed_ref[window] = jnp.concatenate(pieces, axis=0).T.astype(jnp.bfloat16)
+    copies[2].wait()
+
+
+def unpack_kernel(packed_ref, volume_ref, rows_ref, sems):
     windows, channels, _ = packed_ref.shape
     width = 8 * channels
     half = width // 2
-    for window in range(windows):
+    copies = run_copies(rows_ref, volume_ref, sems, windows // 2 * width + half)
+    for window in [windows - 1, *range(windows - 1)]:
         tokens = packed_ref[window].astype(jnp.float32).T
         parts = [
             jnp.concatenate(
@@ -210,10 +227,15 @@
         rows = jnp.concatenate([parts[1][4:], parts[0], parts[1][:4]], axis=0).astype(jnp.bfloat16)
         start = window * width + half
         if window < windows - 1:
-            volume_ref[:, start : start + width] = rows
+            rows_ref[:, start : start + width] = rows
         else:
-            volume_ref[:, start:] = rows[:, :half]
-            volume_ref[:, :half] = rows[:, half:]
+            rows_ref[:, start:] = rows[:, :half]
+            rows_ref[:, :half] = rows[:, half:]
+        if window == windows // 2 - 1:
+            copies[0].start()
+    copies[1].start()
+    for copy in copies:
+        copy.wait()
 
 
 def in_lockstep(stages, planes):
@@ -437,19 +459,26 @@
     in_lockstep(lateral + axial, planes)
 
 
-def pack(rows, windows, channels):
+def pack(rows, gains, windows):
     return pl.pallas_call(
         pack_kernel,
-        out_shape=jax.ShapeDtypeStruct((windows, channels, 128), jnp.bfloat16),
+        out_shape=(
+            jax.ShapeDtypeStruct((windows, gains.shape[1], 128), jnp.bfloat16),
+            jax.ShapeDtypeStruct(gains.shape, gains.dtype),
+        ),
+        in_specs=[pl.BlockSpec(memory_space=pltpu.HBM)] * 2,
+        scratch_shapes=[pltpu.VMEM(rows.shape, rows.dtype), pltpu.SemaphoreType.DMA((3,))],
         compiler_params=pltpu.CompilerParams(vmem_limit_bytes=16 * 1024 * 1024),
         name="pack_windows",
-    )(rows)
+    )(*(pltpu.with_memory_space_constraint(operand, pltpu.HBM) for operand in (rows, gains)))
 
 
 def unpack(packed, rows, width):
     return pl.pallas_call(
         unpack_kernel,
         out_shape=jax.ShapeDtypeStruct((rows, width), jnp.bfloat16),
+        out_specs=pl.BlockSpec(memory_space=pltpu.HBM),
+        scratch_shapes=[pltpu.VMEM((rows, width), jnp.bfloat16), pltpu.SemaphoreType.DMA((2,))],
         compiler_params=pltpu.CompilerParams(vmem_limit_bytes=16 * 1024 * 1024),
         name="unpack_windows",
     )(packed)
@@ -489,11 +518,11 @@
     heads = window_bias.shape[0]
     planes = lax.axis_size("gz")
     windows = width // channels // 8
-    packed = pack(volume.reshape(rows, width), windows, channels)
+    packed, held_gains = pack(volume.reshape(rows, width), norm_gains, windows)
     tokens = lax.all_to_all(packed, ("gz", "tile"), split_axis=0, concat_axis=0, tiled=True)
     mixed = blocks(
         tokens,
-        norm_gains,
+        held_gains,
         qkv_weight,
         out_weight,
         up_weight,

time: 43.2 us -> 42.6 us (0.986)
  local copies, waits for them, and re-layouts: 1.67 us -> 0.04 us
  Pallas kernels: 6.17 us -> 7.24 us
    unnamed x16 -> x12, local copies, waits for them, and re-layouts: 1.67 us -> 0.04 us
    pallas_call x1, Pallas kernels: 0.58 us -> 1.67 us  [pack(): pl.pallas_call(pack_kernel, out_shape=(jax.ShapeDtypeStruct((windows, gai...]
where the time goes in v6:
time: 42.6 us; the launch traced here: 42.4 us
  blocking collectives  35 us (82%)
  Pallas kernels  7.24 us (17%)
    all_to_all x1, blocking collectives, window_body(): lax.all_to_all(packed, ('gz', 'tile'), split_axis=0, concat_axis=0, tiled...  19.5 us
    all_to_all x1, blocking collectives, window_body(): lax.all_to_all(mixed, ('gz', 'tile'), split_axis=0, concat_axis=0, tiled=...  15.5 us
    pallas_call x1, Pallas kernels, blocks(): pl.pallas_call(blocks_kernel, out_shape=jax.ShapeDtypeStruct(tokens.shape...  4.51 us
    pallas_call x1, Pallas kernels, pack(): pl.pallas_call(pack_kernel, out_shape=(jax.ShapeDtypeStruct((windows, gai...  1.67 us
    pallas_call x1, Pallas kernels, unpack(): pl.pallas_call(unpack_kernel, out_shape=jax.ShapeDtypeStruct((rows, width...  1.06 us

profile of v6, /device:TPU:0, one launch (start us, length us, event | category | flops | bytes accessed | tf_op | source)
XLA Modules:
  0.0 42.4 jit_solution(4677211281873499256)
XLA Ops:
  0.0 1.7 %pack_windows.1 = (bf16[16,96,128]{2,1,0:T(8,128)(2,1)S(1)}, f32[4,96]{1,0:T(4,128)S(1)}) custom-call(bf16[16,12288]{1,0:T(8,128)(2,1)} %bitcast.6, f32[4,96]{1,0:T(4,128)} %gains_ref.1), custom_call_target="tpu_custom_call" | custom-call | tf_op jit(solution)/shard_map/pack_windows/pallas_call | solution.py:463
  1.7 0.0 copy-start
  1.7 0.0 copy-start.1
  1.7 0.0 copy-start.2
  1.7 0.0 copy-start.3
  1.7 0.0 copy-start.4
  1.7 0.0 copy-start.5
  1.8 19.5 %all_to_all.10.tokens_ref = bf16[16,96,128]{2,1,0:T(8,128)(2,1)S(1)} all-to-all(bf16[16,96,128]{2,1,0:T(8,128)(2,1)S(1)} %get-tuple-element.7), channel_id=1, replica_groups=mesh['groups'=2,'gz'=8,'tile'=2] {'gz','tile'}, dimensions={0} | all-to-all | bytes 786432 | tf_op jit(solution)/shard_map/all_to_all | solution.py:522
  21.2 0.0 copy-done
  21.2 0.0 copy-done.1
  21.2 0.0 copy-done.2
  21.2 0.0 copy-done.3
  21.3 0.0 copy-done.4
  21.3 0.0 copy-done.5
  21.3 4.5 %both_blocks.1 = bf16[16,96,128]{2,1,0:T(8,128)(2,1)S(1)} custom-call(bf16[16,96,128]{2,1,0:T(8,128)(2,1)S(1)} %all_to_all.10.tokens_ref, f32[4,96]{1,0:T(4,128)S(1)} %get-tuple-element.8.gains_ref, bf16[2,96,288]{2,1,0:T(8,128)(2,1)S(1)} %copy-done.1, bf16[2,96,96]{2,1,0:T(8,128)(2,1)S(1)} %copy-done.5, bf16[2,96,384]{2,1,0:T(8,128)(2,1)S(1)} %copy-done.2, ...), custom_call_target="tpu_custom_call" | custom-call | tf_op jit(solution)/shard_map/both_blocks/pallas_call | solution.py:491
  25.8 15.5 %all_to_all.11.packed_ref = bf16[16,96,128]{2,1,0:T(8,128)(2,1)S(1)} all-to-all(bf16[16,96,128]{2,1,0:T(8,128)(2,1)S(1)} %both_blocks.1), channel_id=1, replica_groups=mesh['groups'=2,'gz'=8,'tile'=2] {'gz','tile'}, dimensions={0} | all-to-all | bytes 786432 | tf_op jit(solution)/shard_map/all_to_all | solution.py:533
  41.3 1.1 %unpack_windows.1 = bf16[16,12288]{1,0:T(8,128)(2,1)} custom-call(bf16[16,96,128]{2,1,0:T(8,128)(2,1)S(1)} %all_to_all.11.packed_ref), custom_call_target="tpu_custom_call" | custom-call | tf_op jit(solution)/shard_map/unpack_windows/pallas_call | solution.py:477
Async XLA Ops:
  1.7 19.6 %copy-start = (bf16[384,192]{1,0:T(8,128)(2,1)S(1)}, bf16[384,192]{1,0:T(8,128)(2,1)}, u32[]{:S(2)}) copy-start(bf16[384,192]{1,0:T(8,128)(2,1)} %constant.2.clone.order_ref) | copy-start | bytes 442372
  1.7 19.6 %copy-start.1 = (bf16[2,96,288]{2,1,0:T(8,128)(2,1)S(1)}, bf16[2,96,288]{2,1,0:T(8,128)(2,1)}, u32[]{:S(2)}) copy-start(bf16[2,96,288]{2,1,0:T(8,128)(2,1)} %qkv_weight_ref.1) | copy-start | bytes 331780
  1.7 19.5 %copy-start.2 = (bf16[2,96,384]{2,1,0:T(8,128)(2,1)S(1)}, bf16[2,96,384]{2,1,0:T(8,128)(2,1)}, u32[]{:S(2)}) copy-start(bf16[2,96,384]{2,1,0:T(8,128)(2,1)} %up_weight_ref.1) | copy-start | bytes 442372
  1.7 19.5 %copy-start.3 = (bf16[2,384,96]{1,2,0:T(8,128)(2,1)S(1)}, bf16[2,384,96]{1,2,0:T(8,128)(2,1)}, u32[]{:S(2)}) copy-start(bf16[2,384,96]{1,2,0:T(8,128)(2,1)} %param.13) | copy-start | bytes 442372
  1.7 19.5 %copy-start.4 = (f32[3,64,64]{2,1,0:T(8,128)S(1)}, f32[3,64,64]{2,1,0:T(8,128)}, u32[]{:S(2)}) copy-start(f32[3,64,64]{2,1,0:T(8,128)} %param.14) | copy-start | bytes 147460
  1.7 19.5 %copy-start.5 = (bf16[2,96,96]{2,1,0:T(8,128)(2,1)S(1)}, bf16[2,96,96]{2,1,0:T(8,128)(2,1)}, u32[]{:S(2)}) copy-start(bf16[2,96,96]{2,1,0:T(8,128)(2,1)} %out_weight_ref.1) | copy-start | bytes 110596

commit v7 on v6

--- a/solution.py
+++ b/solution.py
@@ -174,68 +174,49 @@
     return scaled + scaled * jnp.tanh(scaled * (GELU_LINEAR + scaled * scaled))
 
 
-def run_copies(source_ref, target_ref, sems, cut):
-    width = source_ref.shape[1]
-    runs = (pl.ds(0, cut), pl.ds(cut, width - cut))
-    return [
-        pltpu.make_async_copy(source_ref.at[:, run], target_ref.at[:, run], sems.at[index])
-        for index, run in enumerate(runs)
-    ]
-
-
 def pack_kernel(volume_ref, gains_ref, packed_ref, held_gains_ref, rows_ref, sems):
     windows, channels, _ = packed_ref.shape
     width = 8 * channels
     half = width // 2
-    copies = run_copies(volume_ref, rows_ref, sems, windows // 2 * width + half)
-    copies.append(pltpu.make_async_copy(gains_ref, held_gains_ref, sems.at[2]))
+    copies = [
+        pltpu.make_async_copy(volume_ref, rows_ref, sems.at[0]),
+        pltpu.make_async_copy(gains_ref, held_gains_ref, sems.at[1]),
+    ]
     for copy in copies:
         copy.start()
-    copies[0].wait()
+    for copy in copies:
+        copy.wait()
+    tokens = []
     for window in range(windows):
-        if window == windows // 2:
-            copies[1].wait()
         start = window * width + half
         if window < windows - 1:
             chunk = rows_ref[:, start : start + width]
         else:
             chunk = jnp.concatenate([rows_ref[:, start:], rows_ref[:, :half]], axis=1)
-        chunk = chunk.astype(jnp.float32)
         rolled = jnp.concatenate([chunk[4:], chunk[:4]], axis=0)
-        pieces = [
-            rolled[8 * part : 8 * part + 8, channels * column : channels * (column + 1)]
-            for part in range(2)
-            for column in range(8)
-        ]
-        packed_ref[window] = jnp.concatenate(pieces, axis=0).T.astype(jnp.bfloat16)
-    copies[2].wait()
+        pieces = [rolled[:, channels * column : channels * (column + 1)] for column in range(8)]
+        tokens.append(jnp.concatenate(pieces, axis=0))
+    for window in range(windows):
+        packed_ref[window] = tokens[window].T
 
 
 def unpack_kernel(packed_ref, volume_ref, rows_ref, sems):
     windows, channels, _ = packed_ref.shape
     width = 8 * channels
     half = width // 2
-    copies = run_copies(rows_ref, volume_ref, sems, windows // 2 * width + half)
-    for window in [windows - 1, *range(windows - 1)]:
-        tokens = packed_ref[window].astype(jnp.float32).T
-        parts = [
-            jnp.concatenate(
-                [tokens[64 * part + 8 * column : 64 * part + 8 * column + 8] for column in range(8)], axis=1
-            )
-            for part in range(2)
-        ]
-        rows = jnp.concatenate([parts[1][4:], parts[0], parts[1][:4]], axis=0).astype(jnp.bfloat16)
+    tokens = [packed_ref[window].T for window in range(windows)]
+    for window in range(windows):
+        rows = jnp.concatenate([tokens[window][16 * column : 16 * column + 16] for column in range(8)], axis=1)
+        rows = jnp.concatenate([rows[12:], rows[:12]], axis=0)
         start = window * width + half
         if window < windows - 1:
             rows_ref[:, start : start + width] = rows
         else:
             rows_ref[:, start:] = rows[:, :half]
             rows_ref[:, :half] = rows[:, half:]
-        if window == windows // 2 - 1:
-            copies[0].start()
-    copies[1].start()
-    for copy in copies:
-        copy.wait()
+    copy = pltpu.make_async_copy(rows_ref, volume_ref, sems.at[0])
+    copy.start()
+    copy.wait()
 
 
 def in_lockstep(stages, planes):
@@ -265,8 +246,10 @@
     heads = window_bias_ref.shape[0] // 64
     head_size = channels // heads
     lane = lax.broadcasted_iota(jnp.int32, (1, 128), 1)
-    own = (lane < 64) | (lane % 8 < 4)
-    first = lane < 64
+    own = lane % 16 < 12
+    first = lane % 16 < 8
+    shape = (128, 128)
+    same = lax.broadcasted_iota(jnp.int32, shape, 0) % 16 // 8 == lax.broadcasted_iota(jnp.int32, shape, 1) % 16 // 8
     blank = jnp.zeros((128 - channels, 128), jnp.bfloat16)
     blank_rows = jnp.zeros((128 - channels, 128), jnp.float32)
 
@@ -300,10 +283,10 @@
     last = position == lax.axis_size("gz") * lax.axis_size("tile") - 1
     key_row = lax.broadcasted_iota(jnp.int32, (64, 128), 0)
     query_lane = lax.broadcasted_iota(jnp.int32, (64, 128), 1)
-    column_cut = ((key_row < 32) != (query_lane % 64 < 32)) & last
-    row_cut = ((key_row % 8 < 4) != (query_lane % 8 < 4)) & (query_lane >= 64)
+    column_cut = ((key_row < 32) != (query_lane < 64)) & last
+    row_cut = ((key_row % 8 < 4) != (query_lane % 8 < 4)) & (query_lane % 16 >= 8)
     for head in range(heads):
-        placed = order_ref[128 * head : 128 * (head + 1), :]
+        placed = order_ref[64 + 128 * head : 64 + 128 * (head + 1), :]
         plain = (across(parts[0], placed) + across(parts[1], placed)) * LOG2E
         plain = jnp.where(column_cut, -jnp.inf, plain)
         bias_ref[0, 64 * head : 64 * (head + 1), :] = plain
@@ -346,8 +329,9 @@
             key = jnp.concatenate([keys[:, lanes], blank_rows], axis=0).T
             left = []
             for head in range(heads):
-                masked = jnp.where(lane // head_size == head, key, 0.0).astype(jnp.bfloat16)
-                left.append(jnp.concatenate([masked[:64], masked[64:]], axis=1))
+                masked = jnp.where(lane // head_size == head, key, 0.0).reshape(8, 2, 8, 128)
+                windows = [masked[:, window].reshape(64, 128).astype(jnp.bfloat16) for window in range(2)]
+                left.append(jnp.concatenate(windows, axis=1))
             scores.append((jnp.concatenate(left, axis=0), right))
         held[plane]["s"] = scores
 
@@ -359,13 +343,9 @@
                 own_scores = scores[pair][64 * head : 64 * head + 64]
                 weights = jnp.exp2(own_scores - jnp.max(own_scores, axis=0, keepdims=True))
                 total = jnp.sum(weights, axis=0, keepdims=True)
-                spread = jnp.concatenate(
-                    [
-                        jnp.where(first, weights, 0.0).astype(jnp.bfloat16),
-                        jnp.where(first, 0.0, weights).astype(jnp.bfloat16),
-                    ],
-                    axis=0,
-                )
+                columns = weights.reshape(8, 1, 8, 128)
+                both = jnp.concatenate([columns, columns], axis=1).reshape(128, 128).astype(jnp.bfloat16)
+                spread = jnp.where(same, both, jnp.bfloat16(0))
                 held[plane]["w"].append((spread, 1.0 / total))
 
     def lateral_products(plane):
@@ -467,7 +447,7 @@
             jax.ShapeDtypeStruct(gains.shape, gains.dtype),
         ),
         in_specs=[pl.BlockSpec(memory_space=pltpu.HBM)] * 2,
-        scratch_shapes=[pltpu.VMEM(rows.shape, rows.dtype), pltpu.SemaphoreType.DMA((3,))],
+        scratch_shapes=[pltpu.VMEM(rows.shape, rows.dtype), pltpu.SemaphoreType.DMA((2,))],
         compiler_params=pltpu.CompilerParams(vmem_limit_bytes=16 * 1024 * 1024),
         name="pack_windows",
     )(*(pltpu.with_memory_space_constraint(operand, pltpu.HBM) for operand in (rows, gains)))
@@ -478,7 +458,7 @@
         unpack_kernel,
         out_shape=jax.ShapeDtypeStruct((rows, width), jnp.bfloat16),
         out_specs=pl.BlockSpec(memory_space=pltpu.HBM),
-        scratch_shapes=[pltpu.VMEM((rows, width), jnp.bfloat16), pltpu.SemaphoreType.DMA((2,))],
+        scratch_shapes=[pltpu.VMEM((rows, width), jnp.bfloat16), pltpu.SemaphoreType.DMA((1,))],
         compiler_params=pltpu.CompilerParams(vmem_limit_bytes=16 * 1024 * 1024),
         name="unpack_windows",
     )(packed)
@@ -505,10 +485,13 @@
 
 def token_order(heads):
     index = np.arange(64)
-    placed = np.zeros((heads, 2, 64, heads, 64), np.float32)
+    order = np.zeros((64, heads * 64), np.float32)
+    order[index, index % 8 * 8 + index // 8] = 1.0
+    lane = np.arange(128)
+    placed = np.zeros((heads, 128, heads, 64), np.float32)
     for head in range(heads):
-        placed[head, :, index, head, index % 8 * 8 + index // 8] = 1.0
-    return placed.reshape(heads * 128, heads * 64).astype(jnp.bfloat16)
+        placed[head, lane, head, lane % 8 * 8 + lane // 16] = 1.0
+    return np.concatenate([order, placed.reshape(heads * 128, heads * 64)]).astype(jnp.bfloat16)
 
 
 def window_body(volume, norm_gains, qkv_weight, out_weight, up_weight, down_weight, window_bias):

time: 42.6 us -> 42.3 us (level)
  no operation moved by 1% of the time
where the time goes in v7:
time: 42.3 us; the launch traced here: 42.1 us
  blocking collectives  35 us (83%)
  Pallas kernels  6.95 us (16%)
    all_to_all x1, blocking collectives, window_body(): lax.all_to_all(packed, ('gz', 'tile'), split_axis=0, concat_axis=0, tiled...  19.5 us
    all_to_all x1, blocking collectives, window_body(): lax.all_to_all(mixed, ('gz', 'tile'), split_axis=0, concat_axis=0, tiled=...  15.5 us
    pallas_call x1, Pallas kernels, blocks(): pl.pallas_call(blocks_kernel, out_shape=jax.ShapeDtypeStruct(tokens.shape...  4.49 us
    pallas_call x1, Pallas kernels, pack(): pl.pallas_call(pack_kernel, out_shape=(jax.ShapeDtypeStruct((windows, gai...  1.39 us
    pallas_call x1, Pallas kernels, unpack(): pl.pallas_call(unpack_kernel, out_shape=jax.ShapeDtypeStruct((rows, width...  1.06 us

profile of v7, /device:TPU:0, one launch (start us, length us, event | category | flops | bytes accessed | tf_op | source)
XLA Modules:
  0.0 42.1 jit_solution(10386954608060640402)
XLA Ops:
  0.0 0.0 copy-start.5
  0.0 1.4 %pack_windows.1 = (bf16[16,96,128]{2,1,0:T(8,128)(2,1)S(1)}, f32[4,96]{1,0:T(4,128)S(1)}) custom-call(bf16[16,12288]{1,0:T(8,128)(2,1)} %bitcast.6, f32[4,96]{1,0:T(4,128)} %gains_ref.1), custom_call_target="tpu_custom_call" | custom-call | tf_op jit(solution)/shard_map/pack_windows/pallas_call | solution.py:443
  1.4 0.0 copy-start
  1.4 0.0 copy-start.1
  1.4 0.0 copy-start.2
  1.4 0.0 copy-start.3
  1.5 0.0 copy-start.4
  1.5 19.5 %all_to_all.10.tokens_ref = bf16[16,96,128]{2,1,0:T(8,128)(2,1)S(1)} all-to-all(bf16[16,96,128]{2,1,0:T(8,128)(2,1)S(1)} %get-tuple-element.7), channel_id=1, replica_groups=mesh['groups'=2,'gz'=8,'tile'=2] {'gz','tile'}, dimensions={0} | all-to-all | bytes 786432 | tf_op jit(solution)/shard_map/all_to_all | solution.py:505
  21.0 0.0 copy-done.5
  21.0 0.0 copy-done
  21.0 0.0 copy-done.1
  21.0 0.0 copy-done.2
  21.0 0.0 copy-done.3
  21.0 0.0 copy-done.4
  21.0 4.5 %both_blocks.1 = bf16[16,96,128]{2,1,0:T(8,128)(2,1)S(1)} custom-call(bf16[16,96,128]{2,1,0:T(8,128)(2,1)S(1)} %all_to_all.10.tokens_ref, f32[4,96]{1,0:T(4,128)S(1)} %get-tuple-element.8.gains_ref, bf16[2,96,288]{2,1,0:T(8,128)(2,1)S(1)} %copy-done.1, bf16[2,96,96]{2,1,0:T(8,128)(2,1)S(1)} %copy-done.5, bf16[2,96,384]{2,1,0:T(8,128)(2,1)S(1)} %copy-done.2, ...), custom_call_target="tpu_custom_call" | custom-call | tf_op jit(solution)/shard_map/both_blocks/pallas_call | solution.py:471
  25.5 15.5 %all_to_all.11.packed_ref = bf16[16,96,128]{2,1,0:T(8,128)(2,1)S(1)} all-to-all(bf16[16,96,128]{2,1,0:T(8,128)(2,1)S(1)} %both_blocks.1), channel_id=1, replica_groups=mesh['groups'=2,'gz'=8,'tile'=2] {'gz','tile'}, dimensions={0} | all-to-all | bytes 786432 | tf_op jit(solution)/shard_map/all_to_all | solution.py:516
  41.0 1.1 %unpack_windows.1 = bf16[16,12288]{1,0:T(8,128)(2,1)} custom-call(bf16[16,96,128]{2,1,0:T(8,128)(2,1)S(1)} %all_to_all.11.packed_ref), custom_call_target="tpu_custom_call" | custom-call | tf_op jit(solution)/shard_map/unpack_windows/pallas_call | solution.py:457
Async XLA Ops:
  0.0 21.0 %copy-start.5 = (bf16[2,96,96]{2,1,0:T(8,128)(2,1)S(1)}, bf16[2,96,96]{2,1,0:T(8,128)(2,1)}, u32[]{:S(2)}) copy-start(bf16[2,96,96]{2,1,0:T(8,128)(2,1)} %out_weight_ref.1) | copy-start | bytes 110596
  1.4 19.6 %copy-start = (bf16[448,192]{1,0:T(8,128)(2,1)S(1)}, bf16[448,192]{1,0:T(8,128)(2,1)}, u32[]{:S(2)}) copy-start(bf16[448,192]{1,0:T(8,128)(2,1)} %constant.2.clone.order_ref) | copy-start | bytes 516100
  1.4 19.5 %copy-start.1 = (bf16[2,96,288]{2,1,0:T(8,128)(2,1)S(1)}, bf16[2,96,288]{2,1,0:T(8,128)(2,1)}, u32[]{:S(2)}) copy-start(bf16[2,96,288]{2,1,0:T(8,128)(2,1)} %qkv_weight_ref.1) | copy-start | bytes 331780
  1.4 19.5 %copy-start.2 = (bf16[2,96,384]{2,1,0:T(8,128)(2,1)S(1)}, bf16[2,96,384]{2,1,0:T(8,128)(2,1)}, u32[]{:S(2)}) copy-start(bf16[2,96,384]{2,1,0:T(8,128)(2,1)} %up_weight_ref.1) | copy-start | bytes 442372
  1.4 19.5 %copy-start.3 = (bf16[2,384,96]{1,2,0:T(8,128)(2,1)S(1)}, bf16[2,384,96]{1,2,0:T(8,128)(2,1)}, u32[]{:S(2)}) copy-start(bf16[2,384,96]{1,2,0:T(8,128)(2,1)} %param.13) | copy-start | bytes 442372
  1.5 19.5 %copy-start.4 = (f32[3,64,64]{2,1,0:T(8,128)S(1)}, f32[3,64,64]{2,1,0:T(8,128)}, u32[]{:S(2)}) copy-start(f32[3,64,64]{2,1,0:T(8,128)} %param.14) | copy-start | bytes 147460

commit v8 on v7

--- a/solution.py
+++ b/solution.py
@@ -219,10 +219,16 @@
     copy.wait()
 
 
+LAG = 4
+
+
 def in_lockstep(stages, planes):
-    for stage in stages:
-        for plane in range(planes):
-            stage(plane)
+    for group in stages:
+        group = group if isinstance(group, tuple) else (group,)
+        for step in range(planes + LAG * (len(group) - 1)):
+            for index, stage in enumerate(group):
+                if 0 <= step - LAG * index < planes:
+                    stage(step - LAG * index)
 
 
 def blocks_kernel(
@@ -248,8 +254,8 @@
     lane = lax.broadcasted_iota(jnp.int32, (1, 128), 1)
     own = lane % 16 < 12
     first = lane % 16 < 8
-    shape = (128, 128)
-    same = lax.broadcasted_iota(jnp.int32, shape, 0) % 16 // 8 == lax.broadcasted_iota(jnp.int32, shape, 1) % 16 // 8
+    place = lax.broadcasted_iota(jnp.int32, (channels, 128), 1)
+    by_window = place % 64 // 8 * 16 + place // 64 * 8 + place % 8
     blank = jnp.zeros((128 - channels, 128), jnp.bfloat16)
     blank_rows = jnp.zeros((128 - channels, 128), jnp.float32)
 
@@ -293,6 +299,7 @@
         bias_ref[1, 64 * head : 64 * (head + 1), :] = jnp.where(row_cut, -jnp.inf, plain)
 
     held = [{} for _ in range(planes)]
+    tops, totals = [], []
 
     def rows_of(plane):
         return slice(plane * channels, (plane + 1) * channels)
@@ -309,7 +316,11 @@
         packed = product(qkv[0], held[plane].pop("n"))
         held[plane]["q"] = packed[:channels]
         held[plane]["k"] = packed[channels : 2 * channels]
-        held[plane]["v"] = packed[2 * channels :].astype(jnp.bfloat16)
+        values = packed[2 * channels :]
+        held[plane]["v"] = []
+        for lanes in (slice(0, 128), slice(128, 256)):
+            ordered = jnp.take_along_axis(values[:, lanes], by_window, axis=1, mode="promise_in_bounds")
+            held[plane]["v"].append((ordered[:, :64].astype(jnp.bfloat16), ordered[:, 64:].astype(jnp.bfloat16)))
 
     def lateral_scores(plane):
         queries, keys = held[plane].pop("q"), held[plane].pop("k")
@@ -343,10 +354,7 @@
                 own_scores = scores[pair][64 * head : 64 * head + 64]
                 weights = jnp.exp2(own_scores - jnp.max(own_scores, axis=0, keepdims=True))
                 total = jnp.sum(weights, axis=0, keepdims=True)
-                columns = weights.reshape(8, 1, 8, 128)
-                both = jnp.concatenate([columns, columns], axis=1).reshape(128, 128).astype(jnp.bfloat16)
-                spread = jnp.where(same, both, jnp.bfloat16(0))
-                held[plane]["w"].append((spread, 1.0 / total))
+                held[plane]["w"].append((weights.astype(jnp.bfloat16), 1.0 / total))
 
     def lateral_products(plane):
         held[plane]["s"] = [product(*held[plane]["s"][pair]) + bias_ref[pair] for pair in range(2)]
@@ -355,11 +363,12 @@
         weights, values = held[plane].pop("w"), held[plane].pop("v")
         attended = []
         for pair in range(2):
-            lanes = slice(128 * pair, 128 * pair + 128)
             mixed = []
             for head in range(heads):
-                spread, inverse = weights[heads * pair + head]
-                own_mixed = product(values[head_size * head : head_size * (head + 1), lanes], spread)
+                own_weights, inverse = weights[heads * pair + head]
+                rows = slice(head_size * head, head_size * (head + 1))
+                both = product(jnp.concatenate([values[pair][0][rows], values[pair][1][rows]], axis=0), own_weights)
+                own_mixed = jnp.where(first, both[:head_size], both[head_size:])
                 mixed.append((own_mixed * inverse).astype(jnp.bfloat16))
             attended.append(jnp.concatenate(mixed, axis=0))
         held[plane]["a"] = jnp.concatenate(attended, axis=1)
@@ -389,34 +398,37 @@
         key_ref[rows_of(plane), :] = packed[channels : 2 * channels]
         value_ref[rows_of(plane), :] = packed[2 * channels :]
 
-    def axial_scores(plane):
-        query = query_ref[rows_of(plane), :]
+    def axial_scores(other):
+        key = key_ref[rows_of(other), :]
         half = head_size // 2
         pairs = []
-        for other in range(planes):
-            pair = query * key_ref[rows_of(other), :]
+        for plane in range(planes):
+            pair = query_ref[rows_of(plane), :] * key
             for head in range(heads):
                 top = head_size * head
                 pairs.append(pair[top : top + half] + pair[top + half : top + head_size])
-        pairs = jnp.concatenate(pairs, axis=0)
-        held[plane]["s"] = product(gather, pairs)
+        held[other]["s"] = product(gather, jnp.concatenate(pairs, axis=0))
+
+    def axial_top(plane):
+        scores = held[plane]["s"]
+        tops.append(scores if plane == 0 else jnp.maximum(tops[-1], scores))
+
+    def axial_exponentials(plane):
+        held[plane]["s"] = jnp.exp2(held[plane]["s"] - tops[-1])
+        totals.append(held[plane]["s"] if plane == 0 else totals[-1] + held[plane]["s"])
 
     def axial_weights(plane):
-        scores = held[plane].pop("s")
-        weights = []
-        for head in range(heads):
-            own_scores = scores[planes * head : planes * (head + 1)]
-            own_weights = jnp.exp2(own_scores - jnp.max(own_scores, axis=0, keepdims=True))
-            weights.append(own_weights * (1.0 / jnp.sum(own_weights, axis=0, keepdims=True)))
-        held[plane]["w"] = weights
+        if plane == 0:
+            totals.append(1.0 / totals[-1])
+        held[plane]["w"] = held[plane].pop("s") * totals[-1]
 
     def axial_values(plane):
-        weights = held[plane].pop("w")
         spread = []
         for other in range(planes):
+            weights = held[other]["w"]
             wide = jnp.concatenate(
                 [
-                    jnp.broadcast_to(weights[head][other : other + 1], (head_size, 256)).astype(jnp.bfloat16)
+                    jnp.broadcast_to(weights[planes * head + plane][None], (head_size, 256)).astype(jnp.bfloat16)
                     for head in range(heads)
                 ],
                 axis=0,
@@ -433,9 +445,9 @@
         result_ref[2 * plane] = jnp.where(own, one, two)
         result_ref[2 * plane + 1] = jnp.where(own, two, one)
 
-    lateral = [load, norm, lateral_qkv, lateral_scores, lateral_products, lateral_weights, lateral_values, lateral_out]
-    lateral += [norm, raised(0), gelu, lowered(0), norm, axial_qkv]
-    axial = [axial_scores, axial_weights, axial_values, norm, raised(1), gelu, lowered(1), store]
+    lateral = [load, norm, lateral_qkv, lateral_scores, (lateral_products, lateral_weights, lateral_values, lateral_out)]
+    lateral += [norm, (raised(0), gelu, lowered(0)), norm, axial_qkv]
+    axial = [axial_scores, axial_top, axial_exponentials, axial_weights, axial_values, norm, (raised(1), gelu, lowered(1)), store]
     in_lockstep(lateral + axial, planes)
 
 

time: 42.3 us -> 42.2 us (level)
  no operation moved by 1% of the time
where the time goes in v8:
time: 42.2 us; the launch traced here: 42 us
  blocking collectives  35 us (83%)
  Pallas kernels  6.88 us (16%)
    all_to_all x1, blocking collectives, window_body(): lax.all_to_all(packed, ('gz', 'tile'), split_axis=0, concat_axis=0, tiled...  19.5 us
    all_to_all x1, blocking collectives, window_body(): lax.all_to_all(mixed, ('gz', 'tile'), split_axis=0, concat_axis=0, tiled=...  15.5 us
    pallas_call x1, Pallas kernels, blocks(): pl.pallas_call(blocks_kernel, out_shape=jax.ShapeDtypeStruct(tokens.shape...  4.43 us
    pallas_call x1, Pallas kernels, pack(): pl.pallas_call(pack_kernel, out_shape=(jax.ShapeDtypeStruct((windows, gai...  1.39 us
    pallas_call x1, Pallas kernels, unpack(): pl.pallas_call(unpack_kernel, out_shape=jax.ShapeDtypeStruct((rows, width...  1.06 us

profile of v8, /device:TPU:0, one launch (start us, length us, event | category | flops | bytes accessed | tf_op | source)
XLA Modules:
  0.0 42.0 jit_solution(13264470246555845465)
XLA Ops:
  0.0 0.0 copy-start.5
  0.0 1.4 %pack_windows.1 = (bf16[16,96,128]{2,1,0:T(8,128)(2,1)S(1)}, f32[4,96]{1,0:T(4,128)S(1)}) custom-call(bf16[16,12288]{1,0:T(8,128)(2,1)} %bitcast.6, f32[4,96]{1,0:T(4,128)} %gains_ref.1), custom_call_target="tpu_custom_call" | custom-call | tf_op jit(solution)/shard_map/pack_windows/pallas_call | solution.py:455
  1.4 0.0 copy-start
  1.4 0.0 copy-start.1
  1.4 0.0 copy-start.2
  1.4 0.0 copy-start.3
  1.5 0.0 copy-start.4
  1.5 19.5 %all_to_all.10.tokens_ref = bf16[16,96,128]{2,1,0:T(8,128)(2,1)S(1)} all-to-all(bf16[16,96,128]{2,1,0:T(8,128)(2,1)S(1)} %get-tuple-element.7), channel_id=1, replica_groups=mesh['groups'=2,'gz'=8,'tile'=2] {'gz','tile'}, dimensions={0} | all-to-all | bytes 786432 | tf_op jit(solution)/shard_map/all_to_all | solution.py:517
  21.0 0.0 copy-done.5
  21.0 0.0 copy-done
  21.0 0.0 copy-done.1
  21.0 0.0 copy-done.2
  21.0 0.0 copy-done.3
  21.0 0.0 copy-done.4
  21.0 4.4 %both_blocks.1 = bf16[16,96,128]{2,1,0:T(8,128)(2,1)S(1)} custom-call(bf16[16,96,128]{2,1,0:T(8,128)(2,1)S(1)} %all_to_all.10.tokens_ref, f32[4,96]{1,0:T(4,128)S(1)} %get-tuple-element.8.gains_ref, bf16[2,96,288]{2,1,0:T(8,128)(2,1)S(1)} %copy-done.1, bf16[2,96,96]{2,1,0:T(8,128)(2,1)S(1)} %copy-done.5, bf16[2,96,384]{2,1,0:T(8,128)(2,1)S(1)} %copy-done.2, ...), custom_call_target="tpu_custom_call" | custom-call | tf_op jit(solution)/shard_map/both_blocks/pallas_call | solution.py:483
  25.4 15.5 %all_to_all.11.packed_ref = bf16[16,96,128]{2,1,0:T(8,128)(2,1)S(1)} all-to-all(bf16[16,96,128]{2,1,0:T(8,128)(2,1)S(1)} %both_blocks.1), channel_id=1, replica_groups=mesh['groups'=2,'gz'=8,'tile'=2] {'gz','tile'}, dimensions={0} | all-to-all | bytes 786432 | tf_op jit(solution)/shard_map/all_to_all | solution.py:528
  40.9 1.1 %unpack_windows.1 = bf16[16,12288]{1,0:T(8,128)(2,1)} custom-call(bf16[16,96,128]{2,1,0:T(8,128)(2,1)S(1)} %all_to_all.11.packed_ref), custom_call_target="tpu_custom_call" | custom-call | tf_op jit(solution)/shard_map/unpack_windows/pallas_call | solution.py:469
Async XLA Ops:
  0.0 21.0 %copy-start.5 = (bf16[2,96,96]{2,1,0:T(8,128)(2,1)S(1)}, bf16[2,96,96]{2,1,0:T(8,128)(2,1)}, u32[]{:S(2)}) copy-start(bf16[2,96,96]{2,1,0:T(8,128)(2,1)} %out_weight_ref.1) | copy-start | bytes 110596
  1.4 19.6 %copy-start = (bf16[448,192]{1,0:T(8,128)(2,1)S(1)}, bf16[448,192]{1,0:T(8,128)(2,1)}, u32[]{:S(2)}) copy-start(bf16[448,192]{1,0:T(8,128)(2,1)} %constant.2.clone.order_ref) | copy-start | bytes 516100
  1.4 19.5 %copy-start.1 = (bf16[2,96,288]{2,1,0:T(8,128)(2,1)S(1)}, bf16[2,96,288]{2,1,0:T(8,128)(2,1)}, u32[]{:S(2)}) copy-start(bf16[2,96,288]{2,1,0:T(8,128)(2,1)} %qkv_weight_ref.1) | copy-start | bytes 331780
  1.4 19.5 %copy-start.2 = (bf16[2,96,384]{2,1,0:T(8,128)(2,1)S(1)}, bf16[2,96,384]{2,1,0:T(8,128)(2,1)}, u32[]{:S(2)}) copy-start(bf16[2,96,384]{2,1,0:T(8,128)(2,1)} %up_weight_ref.1) | copy-start | bytes 442372
  1.4 19.5 %copy-start.3 = (bf16[2,384,96]{1,2,0:T(8,128)(2,1)S(1)}, bf16[2,384,96]{1,2,0:T(8,128)(2,1)}, u32[]{:S(2)}) copy-start(bf16[2,384,96]{1,2,0:T(8,128)(2,1)} %param.13) | copy-start | bytes 442372
  1.5 19.5 %copy-start.4 = (f32[3,64,64]{2,1,0:T(8,128)S(1)}, f32[3,64,64]{2,1,0:T(8,128)}, u32[]{:S(2)}) copy-start(f32[3,64,64]{2,1,0:T(8,128)} %param.14) | copy-start | bytes 147460

commit v9 on v8

--- a/solution.py
+++ b/solution.py
@@ -175,8 +175,7 @@
 
 
 def pack_kernel(volume_ref, gains_ref, packed_ref, held_gains_ref, rows_ref, sems):
-    windows, channels, _ = packed_ref.shape
-    width = 8 * channels
+    windows, _, width = packed_ref.shape
     half = width // 2
     copies = [
         pltpu.make_async_copy(volume_ref, rows_ref, sems.at[0]),
@@ -186,28 +185,21 @@
         copy.start()
     for copy in copies:
         copy.wait()
-    tokens = []
     for window in range(windows):
         start = window * width + half
         if window < windows - 1:
             chunk = rows_ref[:, start : start + width]
         else:
             chunk = jnp.concatenate([rows_ref[:, start:], rows_ref[:, :half]], axis=1)
-        rolled = jnp.concatenate([chunk[4:], chunk[:4]], axis=0)
-        pieces = [rolled[:, channels * column : channels * (column + 1)] for column in range(8)]
-        tokens.append(jnp.concatenate(pieces, axis=0))
+        packed_ref[window] = jnp.concatenate([chunk[4:], chunk[:4]], axis=0)
+
+
+def unpack_kernel(packed_ref, volume_ref, rows_ref, sems):
+    windows, _, width = packed_ref.shape
+    half = width // 2
     for window in range(windows):
-        packed_ref[window] = tokens[window].T
-
-
-def unpack_kernel(packed_ref, volume_ref, rows_ref, sems):
-    windows, channels, _ = packed_ref.shape
-    width = 8 * channels
-    half = width // 2
-    tokens = [packed_ref[window].T for window in range(windows)]
-    for window in range(windows):
-        rows = jnp.concatenate([tokens[window][16 * column : 16 * column + 16] for column in range(8)], axis=1)
-        rows = jnp.concatenate([rows[12:], rows[:12]], axis=0)
+        chunk = packed_ref[window]
+        rows = jnp.concatenate([chunk[12:], chunk[:12]], axis=0)
         start = window * width + half
         if window < windows - 1:
             rows_ref[:, start : start + width] = rows
@@ -247,7 +239,7 @@
     key_ref,
     value_ref,
 ):
-    channels = tokens_ref.shape[1]
+    channels = gains_ref.shape[1]
     planes = tokens_ref.shape[0] // 2
     heads = window_bias_ref.shape[0] // 64
     head_size = channels // heads
@@ -304,8 +296,14 @@
     def rows_of(plane):
         return slice(plane * channels, (plane + 1) * channels)
 
+    def gather_columns(plane):
+        held[plane]["x"] = [
+            jnp.concatenate([tokens_ref[source, :, channels * c : channels * (c + 1)] for c in range(8)], axis=0)
+            for source in (2 * plane, 2 * plane + 1)
+        ]
+
     def load(plane):
-        one, two = tokens_ref[2 * plane], tokens_ref[2 * plane + 1]
+        one, two = (tokens.T for tokens in held[plane]["x"])
         tokens = jnp.concatenate([jnp.where(own, one, two), jnp.where(own, two, one)], axis=1)
         held[plane]["x"] = tokens.astype(jnp.float32)
 
@@ -439,15 +437,19 @@
         spread = jnp.concatenate(spread, axis=0)
         held[plane]["x"] = planar_ref[rows_of(plane), :] + product(mix, spread)
 
-    def store(plane):
+    def turn(plane):
         mixed = held[plane].pop("x").astype(jnp.bfloat16)
         one, two = mixed[:, :128], mixed[:, 128:]
-        result_ref[2 * plane] = jnp.where(own, one, two)
-        result_ref[2 * plane + 1] = jnp.where(own, two, one)
-
-    lateral = [load, norm, lateral_qkv, lateral_scores, (lateral_products, lateral_weights, lateral_values, lateral_out)]
+        held[plane]["x"] = [jnp.where(own, one, two).T, jnp.where(own, two, one).T]
+
+    def store(plane):
+        for tile, tokens in enumerate(held[plane].pop("x")):
+            rows = jnp.concatenate([tokens[16 * c : 16 * (c + 1)] for c in range(8)], axis=1)
+            result_ref[2 * plane + tile] = rows
+
+    lateral = [gather_columns, load, norm, lateral_qkv, lateral_scores, (lateral_products, lateral_weights, lateral_values, lateral_out)]
     lateral += [norm, (raised(0), gelu, lowered(0)), norm, axial_qkv]
-    axial = [axial_scores, axial_top, axial_exponentials, axial_weights, axial_values, norm, (raised(1), gelu, lowered(1)), store]
+    axial = [axial_scores, axial_top, axial_exponentials, axial_weights, axial_values, norm, (raised(1), gelu, lowered(1)), turn, store]
     in_lockstep(lateral + axial, planes)
 
 
@@ -455,7 +457,7 @@
     return pl.pallas_call(
         pack_kernel,
         out_shape=(
-            jax.ShapeDtypeStruct((windows, gains.shape[1], 128), jnp.bfloat16),
+            jax.ShapeDtypeStruct((windows, rows.shape[0], rows.shape[1] // windows), jnp.bfloat16),
             jax.ShapeDtypeStruct(gains.shape, gains.dtype),
         ),
         in_specs=[pl.BlockSpec(memory_space=pltpu.HBM)] * 2,
@@ -477,8 +479,7 @@
 
 
 def blocks(tokens, *operands):
-    sources, channels, _ = tokens.shape
-    rows = sources // 2 * channels
+    rows = tokens.shape[0] // 2 * operands[0].shape[1]
     heads = operands[5].shape[0] // 64
     return pl.pallas_call(
         blocks_kernel,

time: 42.2 us -> 42.2 us (level)
    pallas_call x1, Pallas kernels: 4.43 us -> 4.92 us  [blocks(): pl.pallas_call(blocks_kernel, out_shape=jax.ShapeDtypeStruct(tokens.shape...]
where the time goes in v9:
time: 42.2 us; the launch traced here: 42 us
  blocking collectives  35 us (83%)
  Pallas kernels  6.85 us (16%)
    all_to_all x1, blocking collectives, window_body(): lax.all_to_all(packed, ('gz', 'tile'), split_axis=0, concat_axis=0, tiled...  19.5 us
    all_to_all x1, blocking collectives, window_body(): lax.all_to_all(mixed, ('gz', 'tile'), split_axis=0, concat_axis=0, tiled=...  15.5 us
    pallas_call x1, Pallas kernels, blocks(): pl.pallas_call(blocks_kernel, out_shape=jax.ShapeDtypeStruct(tokens.shape...  4.92 us
    pallas_call x1, Pallas kernels, pack(): pl.pallas_call(pack_kernel, out_shape=(jax.ShapeDtypeStruct((windows, row...  1.1 us

profile of v9, /device:TPU:0, one launch (start us, length us, event | category | flops | bytes accessed | tf_op | source)
XLA Modules:
  0.0 42.0 jit_solution(13692193053923090214)
XLA Ops:
  0.0 0.0 copy-start.5
  0.0 1.1 %pack_windows.1 = (bf16[16,16,768]{2,1,0:T(8,128)(2,1)S(1)}, f32[4,96]{1,0:T(4,128)S(1)}) custom-call(bf16[16,12288]{1,0:T(8,128)(2,1)} %bitcast.6, f32[4,96]{1,0:T(4,128)} %gains_ref.1), custom_call_target="tpu_custom_call" | custom-call | tf_op jit(solution)/shard_map/pack_windows/pallas_call | solution.py:457
  1.1 0.0 copy-start
  1.1 0.0 copy-start.1
  1.1 0.0 copy-start.2
  1.1 0.0 copy-start.3
  1.2 0.0 copy-start.4
  1.2 19.5 %all_to_all.10.tokens_ref = bf16[16,16,768]{2,1,0:T(8,128)(2,1)S(1)} all-to-all(bf16[16,16,768]{2,1,0:T(8,128)(2,1)S(1)} %get-tuple-element.7), channel_id=1, replica_groups=mesh['groups'=2,'gz'=8,'tile'=2] {'gz','tile'}, dimensions={0} | all-to-all | bytes 786432 | tf_op jit(solution)/shard_map/all_to_all | solution.py:518
  20.7 0.0 copy-done.5
  20.7 0.0 copy-done
  20.7 0.0 copy-done.1
  20.7 0.0 copy-done.2
  20.7 0.0 copy-done.3
  20.7 0.0 copy-done.4
  20.7 4.9 %both_blocks.1 = bf16[16,16,768]{2,1,0:T(8,128)(2,1)S(1)} custom-call(bf16[16,16,768]{2,1,0:T(8,128)(2,1)S(1)} %all_to_all.10.tokens_ref, f32[4,96]{1,0:T(4,128)S(1)} %get-tuple-element.8.gains_ref, bf16[2,96,288]{2,1,0:T(8,128)(2,1)S(1)} %copy-done.1, bf16[2,96,96]{2,1,0:T(8,128)(2,1)S(1)} %copy-done.5, bf16[2,96,384]{2,1,0:T(8,128)(2,1)S(1)} %copy-done.2, ...), custom_call_target="tpu_custom_call" | custom-call | tf_op jit(solution)/shard_map/both_blocks/pallas_call | solution.py:484
  25.6 15.5 %all_to_all.11.packed_ref = bf16[16,16,768]{2,1,0:T(8,128)(2,1)S(1)} all-to-all(bf16[16,16,768]{2,1,0:T(8,128)(2,1)S(1)} %both_blocks.1), channel_id=1, replica_groups=mesh['groups'=2,'gz'=8,'tile'=2] {'gz','tile'}, dimensions={0} | all-to-all | bytes 786432 | tf_op jit(solution)/shard_map/all_to_all | solution.py:529
  41.1 0.8 %unpack_windows.1 = bf16[16,12288]{1,0:T(8,128)(2,1)} custom-call(bf16[16,16,768]{2,1,0:T(8,128)(2,1)S(1)} %all_to_all.11.packed_ref), custom_call_target="tpu_custom_call" | custom-call | tf_op jit(solution)/shard_map/unpack_windows/pallas_call | solution.py:471
Async XLA Ops:
  0.0 20.7 %copy-start.5 = (bf16[2,96,96]{2,1,0:T(8,128)(2,1)S(1)}, bf16[2,96,96]{2,1,0:T(8,128)(2,1)}, u32[]{:S(2)}) copy-start(bf16[2,96,96]{2,1,0:T(8,128)(2,1)} %out_weight_ref.1) | copy-start | bytes 110596
  1.1 19.6 %copy-start = (bf16[448,192]{1,0:T(8,128)(2,1)S(1)}, bf16[448,192]{1,0:T(8,128)(2,1)}, u32[]{:S(2)}) copy-start(bf16[448,192]{1,0:T(8,128)(2,1)} %constant.2.clone.order_ref) | copy-start | bytes 516100
  1.1 19.5 %copy-start.1 = (bf16[2,96,288]{2,1,0:T(8,128)(2,1)S(1)}, bf16[2,96,288]{2,1,0:T(8,128)(2,1)}, u32[]{:S(2)}) copy-start(bf16[2,96,288]{2,1,0:T(8,128)(2,1)} %qkv_weight_ref.1) | copy-start | bytes 331780
  1.1 19.5 %copy-start.2 = (bf16[2,96,384]{2,1,0:T(8,128)(2,1)S(1)}, bf16[2,96,384]{2,1,0:T(8,128)(2,1)}, u32[]{:S(2)}) copy-start(bf16[2,96,384]{2,1,0:T(8,128)(2,1)} %up_weight_ref.1) | copy-start | bytes 442372
  1.1 19.5 %copy-start.3 = (bf16[2,384,96]{1,2,0:T(8,128)(2,1)S(1)}, bf16[2,384,96]{1,2,0:T(8,128)(2,1)}, u32[]{:S(2)}) copy-start(bf16[2,384,96]{1,2,0:T(8,128)(2,1)} %param.13) | copy-start | bytes 442372
  1.2 19.5 %copy-start.4 = (f32[3,64,64]{2,1,0:T(8,128)S(1)}, f32[3,64,64]{2,1,0:T(8,128)}, u32[]{:S(2)}) copy-start(f32[3,64,64]{2,1,0:T(8,128)} %param.14) | copy-start | bytes 147460

commit v10 on v9

--- a/solution.py
+++ b/solution.py
@@ -266,7 +266,7 @@
     up = [(turned(up_weight_ref, layer) * gain(2 * layer + 1, GELU_IN)).astype(jnp.bfloat16) for layer in range(2)]
     down = [(down_weight_ref[layer].astype(jnp.float32) * GELU_OUT).astype(jnp.bfloat16) for layer in range(2)]
     out = turned(out_weight_ref, 0).astype(jnp.bfloat16)
-    mix = jnp.concatenate([turned(out_weight_ref, 1).astype(jnp.bfloat16)] * 2, axis=1)
+    mix = jnp.concatenate([turned(out_weight_ref, 1).astype(jnp.bfloat16)] * 4, axis=1)
 
     shape = (heads * planes, planes * channels // 2)
     row = lax.broadcasted_iota(jnp.int32, shape, 0)
@@ -432,7 +432,7 @@
                 axis=0,
             )
             spread.append(wide * value_ref[rows_of(other), :])
-        while len(spread) > 2:
+        while len(spread) > 4:
             spread = [one + two for one, two in zip(spread[::2], spread[1::2])]
         spread = jnp.concatenate(spread, axis=0)
         held[plane]["x"] = planar_ref[rows_of(plane), :] + product(mix, spread)

time: 42.2 us -> 42.1 us (level)
  no operation moved by 1% of the time
where the time goes in v10:
time: 42.1 us; the launch traced here: 41.9 us
  blocking collectives  35 us (83%)
  Pallas kernels  6.79 us (16%)
    all_to_all x1, blocking collectives, window_body(): lax.all_to_all(packed, ('gz', 'tile'), split_axis=0, concat_axis=0, tiled...  19.5 us
    all_to_all x1, blocking collectives, window_body(): lax.all_to_all(mixed, ('gz', 'tile'), split_axis=0, concat_axis=0, tiled=...  15.5 us
    pallas_call x1, Pallas kernels, blocks(): pl.pallas_call(blocks_kernel, out_shape=jax.ShapeDtypeStruct(tokens.shape...  4.86 us
    pallas_call x1, Pallas kernels, pack(): pl.pallas_call(pack_kernel, out_shape=(jax.ShapeDtypeStruct((windows, row...  1.1 us

profile of v10, /device:TPU:0, one launch (start us, length us, event | category | flops | bytes accessed | tf_op | source)
XLA Modules:
  0.0 41.9 jit_solution(308801717082409140)
XLA Ops:
  0.0 0.0 copy-start.5
  0.0 1.1 %pack_windows.1 = (bf16[16,16,768]{2,1,0:T(8,128)(2,1)S(1)}, f32[4,96]{1,0:T(4,128)S(1)}) custom-call(bf16[16,12288]{1,0:T(8,128)(2,1)} %bitcast.6, f32[4,96]{1,0:T(4,128)} %gains_ref.1), custom_call_target="tpu_custom_call" | custom-call | tf_op jit(solution)/shard_map/pack_windows/pallas_call | solution.py:457
  1.1 0.0 copy-start
  1.1 0.0 copy-start.1
  1.1 0.0 copy-start.2
  1.1 0.0 copy-start.3
  1.2 0.0 copy-start.4
  1.2 19.5 %all_to_all.10.tokens_ref = bf16[16,16,768]{2,1,0:T(8,128)(2,1)S(1)} all-to-all(bf16[16,16,768]{2,1,0:T(8,128)(2,1)S(1)} %get-tuple-element.7), channel_id=1, replica_groups=mesh['groups'=2,'gz'=8,'tile'=2] {'gz','tile'}, dimensions={0} | all-to-all | bytes 786432 | tf_op jit(solution)/shard_map/all_to_all | solution.py:518
  20.7 0.0 copy-done.5
  20.7 0.0 copy-done
  20.7 0.0 copy-done.1
  20.7 0.0 copy-done.2
  20.7 0.0 copy-done.3
  20.7 0.0 copy-done.4
  20.7 4.9 %both_blocks.1 = bf16[16,16,768]{2,1,0:T(8,128)(2,1)S(1)} custom-call(bf16[16,16,768]{2,1,0:T(8,128)(2,1)S(1)} %all_to_all.10.tokens_ref, f32[4,96]{1,0:T(4,128)S(1)} %get-tuple-element.8.gains_ref, bf16[2,96,288]{2,1,0:T(8,128)(2,1)S(1)} %copy-done.1, bf16[2,96,96]{2,1,0:T(8,128)(2,1)S(1)} %copy-done.5, bf16[2,96,384]{2,1,0:T(8,128)(2,1)S(1)} %copy-done.2, ...), custom_call_target="tpu_custom_call" | custom-call | tf_op jit(solution)/shard_map/both_blocks/pallas_call | solution.py:484
  25.6 15.5 %all_to_all.11.packed_ref = bf16[16,16,768]{2,1,0:T(8,128)(2,1)S(1)} all-to-all(bf16[16,16,768]{2,1,0:T(8,128)(2,1)S(1)} %both_blocks.1), channel_id=1, replica_groups=mesh['groups'=2,'gz'=8,'tile'=2] {'gz','tile'}, dimensions={0} | all-to-all | bytes 786432 | tf_op jit(solution)/shard_map/all_to_all | solution.py:529
  41.1 0.8 %unpack_windows.1 = bf16[16,12288]{1,0:T(8,128)(2,1)} custom-call(bf16[16,16,768]{2,1,0:T(8,128)(2,1)S(1)} %all_to_all.11.packed_ref), custom_call_target="tpu_custom_call" | custom-call | tf_op jit(solution)/shard_map/unpack_windows/pallas_call | solution.py:471
Async XLA Ops:
  0.0 20.7 %copy-start.5 = (bf16[2,96,96]{2,1,0:T(8,128)(2,1)S(1)}, bf16[2,96,96]{2,1,0:T(8,128)(2,1)}, u32[]{:S(2)}) copy-start(bf16[2,96,96]{2,1,0:T(8,128)(2,1)} %out_weight_ref.1) | copy-start | bytes 110596
  1.1 19.6 %copy-start = (bf16[448,192]{1,0:T(8,128)(2,1)S(1)}, bf16[448,192]{1,0:T(8,128)(2,1)}, u32[]{:S(2)}) copy-start(bf16[448,192]{1,0:T(8,128)(2,1)} %constant.2.clone.order_ref) | copy-start | bytes 516100
  1.1 19.5 %copy-start.1 = (bf16[2,96,288]{2,1,0:T(8,128)(2,1)S(1)}, bf16[2,96,288]{2,1,0:T(8,128)(2,1)}, u32[]{:S(2)}) copy-start(bf16[2,96,288]{2,1,0:T(8,128)(2,1)} %qkv_weight_ref.1) | copy-start | bytes 331780
  1.1 19.5 %copy-start.2 = (bf16[2,96,384]{2,1,0:T(8,128)(2,1)S(1)}, bf16[2,96,384]{2,1,0:T(8,128)(2,1)}, u32[]{:S(2)}) copy-start(bf16[2,96,384]{2,1,0:T(8,128)(2,1)} %up_weight_ref.1) | copy-start | bytes 442372
  1.1 19.5 %copy-start.3 = (bf16[2,384,96]{1,2,0:T(8,128)(2,1)S(1)}, bf16[2,384,96]{1,2,0:T(8,128)(2,1)}, u32[]{:S(2)}) copy-start(bf16[2,384,96]{1,2,0:T(8,128)(2,1)} %param.13) | copy-start | bytes 442372
  1.2 19.5 %copy-start.4 = (f32[3,64,64]{2,1,0:T(8,128)S(1)}, f32[3,64,64]{2,1,0:T(8,128)}, u32[]{:S(2)}) copy-start(f32[3,64,64]{2,1,0:T(8,128)} %param.14) | copy-start | bytes 147460

commit v11 on v10

--- a/solution.py
+++ b/solution.py
@@ -197,7 +197,13 @@
 def unpack_kernel(packed_ref, volume_ref, rows_ref, sems):
     windows, _, width = packed_ref.shape
     half = width // 2
-    for window in range(windows):
+    cut = windows // 2 * width + half
+    runs = (pl.ds(0, cut), pl.ds(cut, windows * width - cut))
+    copies = [
+        pltpu.make_async_copy(rows_ref.at[:, run], volume_ref.at[:, run], sems.at[index])
+        for index, run in enumerate(runs)
+    ]
+    for window in [windows - 1, *range(windows - 1)]:
         chunk = packed_ref[window]
         rows = jnp.concatenate([chunk[12:], chunk[:12]], axis=0)
         start = window * width + half
@@ -206,9 +212,11 @@
         else:
             rows_ref[:, start:] = rows[:, :half]
             rows_ref[:, :half] = rows[:, half:]
-    copy = pltpu.make_async_copy(rows_ref, volume_ref, sems.at[0])
-    copy.start()
-    copy.wait()
+        if window == windows // 2 - 1:
+            copies[0].start()
+    copies[1].start()
+    for copy in copies:
+        copy.wait()
 
 
 LAG = 4
@@ -472,7 +480,7 @@
         unpack_kernel,
         out_shape=jax.ShapeDtypeStruct((rows, width), jnp.bfloat16),
         out_specs=pl.BlockSpec(memory_space=pltpu.HBM),
-        scratch_shapes=[pltpu.VMEM((rows, width), jnp.bfloat16), pltpu.SemaphoreType.DMA((1,))],
+        scratch_shapes=[pltpu.VMEM((rows, width), jnp.bfloat16), pltpu.SemaphoreType.DMA((2,))],
         compiler_params=pltpu.CompilerParams(vmem_limit_bytes=16 * 1024 * 1024),
         name="unpack_windows",
     )(packed)

time: 42.1 us -> 42.1 us (level)
  no operation moved by 1% of the time
where the time goes in v11:
time: 42.1 us; the launch traced here: 41.9 us
  blocking collectives  35 us (83%)
  Pallas kernels  6.76 us (16%)
    all_to_all x1, blocking collectives, window_body(): lax.all_to_all(packed, ('gz', 'tile'), split_axis=0, concat_axis=0, tiled...  19.5 us
    all_to_all x1, blocking collectives, window_body(): lax.all_to_all(mixed, ('gz', 'tile'), split_axis=0, concat_axis=0, tiled=...  15.5 us
    pallas_call x1, Pallas kernels, blocks(): pl.pallas_call(blocks_kernel, out_shape=jax.ShapeDtypeStruct(tokens.shape...  4.86 us
    pallas_call x1, Pallas kernels, pack(): pl.pallas_call(pack_kernel, out_shape=(jax.ShapeDtypeStruct((windows, row...  1.1 us

profile of v11, /device:TPU:0, one launch (start us, length us, event | category | flops | bytes accessed | tf_op | source)
XLA Modules:
  0.0 41.9 jit_solution(8865984055430496998)
XLA Ops:
  0.0 0.0 copy-start.5
  0.0 1.1 %pack_windows.1 = (bf16[16,16,768]{2,1,0:T(8,128)(2,1)S(1)}, f32[4,96]{1,0:T(4,128)S(1)}) custom-call(bf16[16,12288]{1,0:T(8,128)(2,1)} %bitcast.6, f32[4,96]{1,0:T(4,128)} %gains_ref.1), custom_call_target="tpu_custom_call" | custom-call | tf_op jit(solution)/shard_map/pack_windows/pallas_call | solution.py:465
  1.1 0.0 copy-start
  1.1 0.0 copy-start.1
  1.1 0.0 copy-start.2
  1.1 0.0 copy-start.3
  1.2 0.0 copy-start.4
  1.2 19.5 %all_to_all.10.tokens_ref = bf16[16,16,768]{2,1,0:T(8,128)(2,1)S(1)} all-to-all(bf16[16,16,768]{2,1,0:T(8,128)(2,1)S(1)} %get-tuple-element.7), channel_id=1, replica_groups=mesh['groups'=2,'gz'=8,'tile'=2] {'gz','tile'}, dimensions={0} | all-to-all | bytes 786432 | tf_op jit(solution)/shard_map/all_to_all | solution.py:526
  20.7 0.0 copy-done.5
  20.7 0.0 copy-done
  20.7 0.0 copy-done.1
  20.7 0.0 copy-done.2
  20.7 0.0 copy-done.3
  20.7 0.0 copy-done.4
  20.7 4.9 %both_blocks.1 = bf16[16,16,768]{2,1,0:T(8,128)(2,1)S(1)} custom-call(bf16[16,16,768]{2,1,0:T(8,128)(2,1)S(1)} %all_to_all.10.tokens_ref, f32[4,96]{1,0:T(4,128)S(1)} %get-tuple-element.8.gains_ref, bf16[2,96,288]{2,1,0:T(8,128)(2,1)S(1)} %copy-done.1, bf16[2,96,96]{2,1,0:T(8,128)(2,1)S(1)} %copy-done.5, bf16[2,96,384]{2,1,0:T(8,128)(2,1)S(1)} %copy-done.2, ...), custom_call_target="tpu_custom_call" | custom-call | tf_op jit(solution)/shard_map/both_blocks/pallas_call | solution.py:492
  25.6 15.5 %all_to_all.11.packed_ref = bf16[16,16,768]{2,1,0:T(8,128)(2,1)S(1)} all-to-all(bf16[16,16,768]{2,1,0:T(8,128)(2,1)S(1)} %both_blocks.1), channel_id=1, replica_groups=mesh['groups'=2,'gz'=8,'tile'=2] {'gz','tile'}, dimensions={0} | all-to-all | bytes 786432 | tf_op jit(solution)/shard_map/all_to_all | solution.py:537
  41.1 0.8 %unpack_windows.1 = bf16[16,12288]{1,0:T(8,128)(2,1)} custom-call(bf16[16,16,768]{2,1,0:T(8,128)(2,1)S(1)} %all_to_all.11.packed_ref), custom_call_target="tpu_custom_call" | custom-call | tf_op jit(solution)/shard_map/unpack_windows/pallas_call | solution.py:479
Async XLA Ops:
  0.0 20.7 %copy-start.5 = (bf16[2,96,96]{2,1,0:T(8,128)(2,1)S(1)}, bf16[2,96,96]{2,1,0:T(8,128)(2,1)}, u32[]{:S(2)}) copy-start(bf16[2,96,96]{2,1,0:T(8,128)(2,1)} %out_weight_ref.1) | copy-start | bytes 110596
  1.1 19.6 %copy-start = (bf16[448,192]{1,0:T(8,128)(2,1)S(1)}, bf16[448,192]{1,0:T(8,128)(2,1)}, u32[]{:S(2)}) copy-start(bf16[448,192]{1,0:T(8,128)(2,1)} %constant.2.clone.order_ref) | copy-start | bytes 516100
  1.1 19.5 %copy-start.1 = (bf16[2,96,288]{2,1,0:T(8,128)(2,1)S(1)}, bf16[2,96,288]{2,1,0:T(8,128)(2,1)}, u32[]{:S(2)}) copy-start(bf16[2,96,288]{2,1,0:T(8,128)(2,1)} %qkv_weight_ref.1) | copy-start | bytes 331780
  1.1 19.5 %copy-start.2 = (bf16[2,96,384]{2,1,0:T(8,128)(2,1)S(1)}, bf16[2,96,384]{2,1,0:T(8,128)(2,1)}, u32[]{:S(2)}) copy-start(bf16[2,96,384]{2,1,0:T(8,128)(2,1)} %up_weight_ref.1) | copy-start | bytes 442372
  1.1 19.5 %copy-start.3 = (bf16[2,384,96]{1,2,0:T(8,128)(2,1)S(1)}, bf16[2,384,96]{1,2,0:T(8,128)(2,1)}, u32[]{:S(2)}) copy-start(bf16[2,384,96]{1,2,0:T(8,128)(2,1)} %param.13) | copy-start | bytes 442372
  1.2 19.5 %copy-start.4 = (f32[3,64,64]{2,1,0:T(8,128)S(1)}, f32[3,64,64]{2,1,0:T(8,128)}, u32[]{:S(2)}) copy-start(f32[3,64,64]{2,1,0:T(8,128)} %param.14) | copy-start | bytes 147460

commit v12 on v11

--- a/solution.py
+++ b/solution.py
@@ -274,7 +274,7 @@
     up = [(turned(up_weight_ref, layer) * gain(2 * layer + 1, GELU_IN)).astype(jnp.bfloat16) for layer in range(2)]
     down = [(down_weight_ref[layer].astype(jnp.float32) * GELU_OUT).astype(jnp.bfloat16) for layer in range(2)]
     out = turned(out_weight_ref, 0).astype(jnp.bfloat16)
-    mix = jnp.concatenate([turned(out_weight_ref, 1).astype(jnp.bfloat16)] * 4, axis=1)
+    mix = jnp.concatenate([turned(out_weight_ref, 1).astype(jnp.bfloat16)] * 8, axis=1)
 
     shape = (heads * planes, planes * channels // 2)
     row = lax.broadcasted_iota(jnp.int32, shape, 0)
@@ -440,7 +440,7 @@
                 axis=0,
             )
             spread.append(wide * value_ref[rows_of(other), :])
-        while len(spread) > 4:
+        while len(spread) > 8:
             spread = [one + two for one, two in zip(spread[::2], spread[1::2])]
         spread = jnp.concatenate(spread, axis=0)
         held[plane]["x"] = planar_ref[rows_of(plane), :] + product(mix, spread)

time: 42.1 us -> 42.3 us (level)
  no operation moved by 1% of the time
where the time goes in v12:
time: 42.3 us; the launch traced here: 42.1 us
  blocking collectives  35 us (83%)
  Pallas kernels  6.96 us (16%)
    all_to_all x1, blocking collectives, window_body(): lax.all_to_all(packed, ('gz', 'tile'), split_axis=0, concat_axis=0, tiled...  19.5 us
    all_to_all x1, blocking collectives, window_body(): lax.all_to_all(mixed, ('gz', 'tile'), split_axis=0, concat_axis=0, tiled=...  15.5 us
    pallas_call x1, Pallas kernels, blocks(): pl.pallas_call(blocks_kernel, out_shape=jax.ShapeDtypeStruct(tokens.shape...  5.06 us
    pallas_call x1, Pallas kernels, pack(): pl.pallas_call(pack_kernel, out_shape=(jax.ShapeDtypeStruct((windows, row...  1.1 us

profile of v12, /device:TPU:0, one launch (start us, length us, event | category | flops | bytes accessed | tf_op | source)
XLA Modules:
  0.0 42.1 jit_solution(6069240374259376967)
XLA Ops:
  0.0 0.0 copy-start.5
  0.0 1.1 %pack_windows.1 = (bf16[16,16,768]{2,1,0:T(8,128)(2,1)S(1)}, f32[4,96]{1,0:T(4,128)S(1)}) custom-call(bf16[16,12288]{1,0:T(8,128)(2,1)} %bitcast.6, f32[4,96]{1,0:T(4,128)} %gains_ref.1), custom_call_target="tpu_custom_call" | custom-call | tf_op jit(solution)/shard_map/pack_windows/pallas_call | solution.py:465
  1.1 0.0 copy-start
  1.1 0.0 copy-start.1
  1.1 0.0 copy-start.2
  1.1 0.0 copy-start.3
  1.2 0.0 copy-start.4
  1.2 19.5 %all_to_all.10.tokens_ref = bf16[16,16,768]{2,1,0:T(8,128)(2,1)S(1)} all-to-all(bf16[16,16,768]{2,1,0:T(8,128)(2,1)S(1)} %get-tuple-element.7), channel_id=1, replica_groups=mesh['groups'=2,'gz'=8,'tile'=2] {'gz','tile'}, dimensions={0} | all-to-all | bytes 786432 | tf_op jit(solution)/shard_map/all_to_all | solution.py:526
  20.7 0.0 copy-done.5
  20.7 0.0 copy-done
  20.7 0.0 copy-done.1
  20.7 0.0 copy-done.2
  20.7 0.0 copy-done.3
  20.7 0.0 copy-done.4
  20.7 5.1 %both_blocks.1 = bf16[16,16,768]{2,1,0:T(8,128)(2,1)S(1)} custom-call(bf16[16,16,768]{2,1,0:T(8,128)(2,1)S(1)} %all_to_all.10.tokens_ref, f32[4,96]{1,0:T(4,128)S(1)} %get-tuple-element.8.gains_ref, bf16[2,96,288]{2,1,0:T(8,128)(2,1)S(1)} %copy-done.1, bf16[2,96,96]{2,1,0:T(8,128)(2,1)S(1)} %copy-done.5, bf16[2,96,384]{2,1,0:T(8,128)(2,1)S(1)} %copy-done.2, ...), custom_call_target="tpu_custom_call" | custom-call | tf_op jit(solution)/shard_map/both_blocks/pallas_call | solution.py:492
  25.8 15.5 %all_to_all.11.packed_ref = bf16[16,16,768]{2,1,0:T(8,128)(2,1)S(1)} all-to-all(bf16[16,16,768]{2,1,0:T(8,128)(2,1)S(1)} %both_blocks.1), channel_id=1, replica_groups=mesh['groups'=2,'gz'=8,'tile'=2] {'gz','tile'}, dimensions={0} | all-to-all | bytes 786432 | tf_op jit(solution)/shard_map/all_to_all | solution.py:537
  41.3 0.8 %unpack_windows.1 = bf16[16,12288]{1,0:T(8,128)(2,1)} custom-call(bf16[16,16,768]{2,1,0:T(8,128)(2,1)S(1)} %all_to_all.11.packed_ref), custom_call_target="tpu_custom_call" | custom-call | tf_op jit(solution)/shard_map/unpack_windows/pallas_call | solution.py:479
Async XLA Ops:
  0.0 20.7 %copy-start.5 = (bf16[2,96,96]{2,1,0:T(8,128)(2,1)S(1)}, bf16[2,96,96]{2,1,0:T(8,128)(2,1)}, u32[]{:S(2)}) copy-start(bf16[2,96,96]{2,1,0:T(8,128)(2,1)} %out_weight_ref.1) | copy-start | bytes 110596
  1.1 19.6 %copy-start = (bf16[448,192]{1,0:T(8,128)(2,1)S(1)}, bf16[448,192]{1,0:T(8,128)(2,1)}, u32[]{:S(2)}) copy-start(bf16[448,192]{1,0:T(8,128)(2,1)} %constant.2.clone.order_ref) | copy-start | bytes 516100
  1.1 19.5 %copy-start.1 = (bf16[2,96,288]{2,1,0:T(8,128)(2,1)S(1)}, bf16[2,96,288]{2,1,0:T(8,128)(2,1)}, u32[]{:S(2)}) copy-start(bf16[2,96,288]{2,1,0:T(8,128)(2,1)} %qkv_weight_ref.1) | copy-start | bytes 331780
  1.1 19.5 %copy-start.2 = (bf16[2,96,384]{2,1,0:T(8,128)(2,1)S(1)}, bf16[2,96,384]{2,1,0:T(8,128)(2,1)}, u32[]{:S(2)}) copy-start(bf16[2,96,384]{2,1,0:T(8,128)(2,1)} %up_weight_ref.1) | copy-start | bytes 442372
  1.1 19.5 %copy-start.3 = (bf16[2,384,96]{1,2,0:T(8,128)(2,1)S(1)}, bf16[2,384,96]{1,2,0:T(8,128)(2,1)}, u32[]{:S(2)}) copy-start(bf16[2,384,96]{1,2,0:T(8,128)(2,1)} %param.13) | copy-start | bytes 442372
  1.2 19.5 %copy-start.4 = (f32[3,64,64]{2,1,0:T(8,128)S(1)}, f32[3,64,64]{2,1,0:T(8,128)}, u32[]{:S(2)}) copy-start(f32[3,64,64]{2,1,0:T(8,128)} %param.14) | copy-start | bytes 147460
